TPU v7x, 256 devices: a whole 4x4x8 slice. The times are simulated.
256 devices in a mesh: blk: 16 (over z_hi, y, core), rows: 16 (over x, z_lo).
Axes of the slice: x: 4, y: 4, z: 8 (z_hi: 2, z_lo: 4; z = z_hi * 4 + z_lo), core: 2. Of those that a mesh axis runs over, the one named last changes fastest.
Arguments:
- section_weights: bfloat16 [16, 256, 9, 256], P('blk'), may hold values from -0.125 to 0.125
- grad_acc: bfloat16 [16, 256, 9, 256], P('blk', 'rows'), may hold values from -6 to 6
- saved_inputs: bfloat16 [3, 16, 64, 256, 256], P(None, 'blk', 'rows'), may hold values from -6 to 6
- cotangent: bfloat16 [16, 64, 256, 256], P('blk', 'rows'), may hold values from -6 to 6
- fresh_grads: bfloat16 [2, 64, 256, 256], P(None, 'rows'), may hold values from -6 to 6
Outputs:
- tick_states: bfloat16 [3, 16, 64, 256, 256], P(None, 'blk', 'rows')
- grad_out: bfloat16 [16, 256, 9, 256], P('blk', 'rows')
All inputs are finite; a program needn't handle non-finite values.
Results may differ from a plain program's by a relative error of at most 0.0057.
Values may be sent and summed in bfloat16 or wider, within the bound.
No kernel may reach another device: no remote copies, remote signals or barrier semaphores. Data moves between devices by JAX's collectives and lax.ppermute only.
A program may use at most 128 MiB of HBM per device.

v0:
```python
import jax
import jax.numpy as jnp
from jax import lax
from jax.sharding import PartitionSpec as P

TICKS = 3


def padded(cells, sides, width):
    for axis, dim in sides:
        count = lax.axis_size(axis)
        ends = count - 1
        head = lax.slice_in_dim(cells, 0, width, axis=dim)
        tail = lax.slice_in_dim(cells, cells.shape[dim] - width, cells.shape[dim], axis=dim)
        cells = jnp.concatenate(
            [
                lax.ppermute(tail, axis, [(i, (i + 1) % count) for i in range(ends)]),
                cells,
                lax.ppermute(head, axis, [((i + 1) % count, i) for i in range(ends)]),
            ],
            axis=dim,
        )
    return cells


def shifted(value, axis, by):
    peers = lax.axis_size(axis)
    return lax.ppermute(value, axis, [(i, (i + by) % peers) for i in range(peers)])


def widen_columns(tile_data):
    return jnp.pad(tile_data, ((0, 0), (0, 0), (1, 1)))


def back_project(kernel, grad_wide, height, columns):
    running = None
    for tap_index in range(9):
        row_shift = tap_index // 3
        col_shift = tap_index % 3
        window = grad_wide[
            2 - row_shift : 2 - row_shift + height, :, 2 - col_shift : 2 - col_shift + columns
        ]
        product = jnp.einsum(
            "oi,row->riw", kernel[:, tap_index, :], window, preferred_element_type=jnp.float32
        )
        running = product if running is None else running + product
    return running


def weight_terms(grad_tile, input_wide, cell_scale):
    height = grad_tile.shape[0]
    columns = grad_tile.shape[2]
    tap_list = []
    for tap_index in range(9):
        row_shift = tap_index // 3
        col_shift = tap_index % 3
        window = input_wide[row_shift : row_shift + height, :, col_shift : col_shift + columns]
        tap_grad = jnp.einsum("row,riw->oi", grad_tile, window, preferred_element_type=jnp.float32)
        tap_list.append(tap_grad * cell_scale)
    return jnp.stack(tap_list, axis=1)


def tick_work(grad_tile, saved_tile, kernel, held_grads, cell_scale):
    height = grad_tile.shape[0]
    columns = grad_tile.shape[2]
    grad_wide = widen_columns(padded(grad_tile, (("rows", 0),), 1))
    inputs = jnp.maximum(saved_tile, 0)
    input_wide = widen_columns(padded(inputs, (("rows", 0),), 1))
    back_sum = back_project(kernel, grad_wide, height, columns)
    new_tile = jnp.where(saved_tile > 0, back_sum, 0.0).astype(jnp.bfloat16)
    summed = lax.psum_scatter(
        weight_terms(grad_tile, input_wide, cell_scale), "rows", scatter_dimension=0, tiled=True
    )
    updated = (held_grads.astype(jnp.float32) + summed).astype(jnp.bfloat16)
    return (new_tile, updated)


def shards(section_weights, grad_acc, saved_inputs, cotangent, fresh_grads):
    cycle_size = lax.axis_size("blk")
    position = lax.axis_index("blk")
    kernel = section_weights[0]
    held_grads = grad_acc[0]
    height = cotangent.shape[1]
    columns = cotangent.shape[3]
    cell_scale = float(lax.axis_size("rows") * height * columns) ** (-0.5)
    current = cotangent[0]
    states = []
    for tick_index in range(TICKS):
        if tick_index > 0:
            restart = position == (cycle_size - tick_index) % cycle_size
            current = jnp.where(restart, fresh_grads[tick_index - 1], current)
        current, held_grads = tick_work(
            current, saved_inputs[tick_index, 0], kernel, held_grads, cell_scale
        )
        states.append(current)
        if tick_index + 1 < TICKS:
            kernel, held_grads = shifted((kernel, held_grads), "blk", -1)
    return (jnp.stack(states)[:, None], held_grads[None])


def solution(mesh):
    return jax.shard_map(
        shards,
        mesh=mesh,
        in_specs=(
            P("blk", None, None, None),
            P("blk", "rows", None, None),
            P(None, "blk", "rows", None, None),
            P("blk", "rows", None, None),
            P(None, "rows", None, None),
        ),
        out_specs=(P(None, "blk", "rows", None, None), P("blk", "rows", None, None)),
        check_vma=False,
    )
```

profile of v0, /device:TPU:2, one launch (start us, length us, event | category | flops | bytes accessed | tf_op | source)
XLA Modules:
  0.0 411.5 jit_solution(1801114441696677046)
XLA Ops:
  7.2 1.5 fusion.221
  10.5 3.8 collective-permute-start.8
  14.3 4.7 %collective-permute-start.9 = (bf16[1,256,256]{1,2,0:T(8,128)(2,1)}, bf16[1,256,256]{1,2,0:T(8,128)(2,1)S(1)}, u32[]{:S(2)}, u32[]{:S(2)}) collective-permute-start(bf16[1,256,256]{1,2,0:T(8,128)(2,1)} %get-tuple-element.12), channel_id=1, source_target_pairs={{1,0},{2,1},{3,2},{4,3},{5,4},{6,5},{7,6},{8,7},{9,8},{10,9},{11,1... | collective-permute-start | bytes 393224 | tf_op jit(solution)/shard_map/ppermute | solution.py:19
  20.0 3.8 collective-permute-start.1
  23.8 2.0 collective-permute-start
  26.9 1.9 collective-permute-start.11
  29.7 2.0 copy.251
  33.7 6.7 %collective-permute-start.12 = (bf16[1,256,256]{1,2,0:T(8,128)(2,1)}, bf16[1,256,256]{1,2,0:T(8,128)(2,1)}, u32[]{:S(2)}, u32[]{:S(2)}) collective-permute-start(bf16[1,256,256]{1,2,0:T(8,128)(2,1)} %get-tuple-element.16), channel_id=1, source_target_pairs={{1,0},{2,1},{3,2},{4,3},{5,4},{6,5},{7,6},{8,7},{9,8},{10,9},{11,1... | collective-permute-start | bytes 393224 | tf_op jit(solution)/shard_map/ppermute | solution.py:19
  40.5 7.5 %collective-permute-start.4 = (bf16[256,9,256]{2,0,1:T(8,128)(2,1)}, bf16[256,9,256]{2,0,1:T(8,128)(2,1)}, u32[]{:S(2)}, u32[]{:S(2)}) collective-permute-start(bf16[256,9,256]{2,0,1:T(8,128)(2,1)} %bitcast.4), channel_id=1, source_target_pairs={{0,240},{16,0},{32,16},{48,32},{64,48},{80,64},{96,80},{112,96},{1... | collective-permute-start | bytes 3538952 | tf_op jit(solution)/shard_map/ppermute | solution.py:28
  47.9 1.3 select_maximum_fusion.4
  50.3 1.9 fusion.104
  52.2 1.1 fusion.54
  57.5 1.1 fusion.106
  58.6 1.1 fusion.64
  59.6 5.0 %copy.134 = f32[256,9,256]{2,1,0:T(8,128)} copy(f32[256,9,256]{0,2,1:T(8,128)} %fusion.64) | data formatting | bytes 4718592 | tf_op jit(solution)/shard_map/stack | solution.py:60
  64.7 1.9 collective-permute-start.14
  66.6 6.8 %collective-permute-start.15 = (bf16[1,256,256]{1,2,0:T(8,128)(2,1)}, bf16[1,256,256]{1,2,0:T(8,128)(2,1)S(1)}, u32[]{:S(2)}, u32[]{:S(2)}) collective-permute-start(bf16[1,256,256]{1,2,0:T(8,128)(2,1)} %get-tuple-element.20), channel_id=1, source_target_pairs={{1,0},{2,1},{3,2},{4,3},{5,4},{6,5},{7,6},{8,7},{9,8},{10,9},{11,1... | collective-permute-start | bytes 393224 | tf_op jit(solution)/shard_map/ppermute | solution.py:19
  73.7 1.2 fusion.180
  74.9 1.2 fusion.107
  76.1 1.2 select_maximum_fusion.2
  77.3 1.2 convolution_add_fusion.8
  78.5 1.2 convolution_add_fusion.7
  79.7 1.3 convolution_add_fusion.6
  81.0 1.3 convolution_add_fusion.5
  82.3 1.2 convolution_add_fusion.4
  83.5 1.3 convolution_add_fusion.3
  84.8 2.2 bitcast_select_fusion.1
  88.0 1.3 fusion.68
  91.1 1.3 fusion.80
  92.7 3.5 copy.154
  96.2 1.9 collective-permute-start.3
  98.2 3.9 collective-permute-start.2
  102.4 1.1 select_maximum_fusion
  103.5 6.5 %collective-permute-done.3 = bf16[1,256,256]{1,2,0:T(8,128)(2,1)S(1)} collective-permute-done((bf16[1,256,256]{1,2,0:T(8,128)(2,1)S(1)}, bf16[1,256,256]{1,2,0:T(8,128)(2,1)S(1)}, u32[]{:S(2)}, u32[]{:S(2)}) %collective-permute-start.3) | collective-permute-done | bytes 131104 | tf_op jit(solution)/shard_map/ppermute | solution.py:19
  110.2 1.2 fusion.114
  111.4 1.2 fusion.118
  112.6 1.2 fusion.169
  113.8 1.2 fusion.171
  115.0 1.2 fusion.173
  116.2 1.2 fusion.175
  117.5 1.3 fusion.177
  118.7 1.2 fusion.201
  119.9 2.5 bitcast_select_fusion
  122.8 1.3 fusion.86
  126.6 3.5 copy.174
  130.1 4.8 %collective-permute-start.7 = (bf16[256,9,256]{2,0,1:T(8,128)(2,1)}, bf16[256,9,256]{2,0,1:T(8,128)(2,1)S(1)}, u32[]{:S(2)}, u32[]{:S(2)}) collective-permute-start(bf16[256,9,256]{2,0,1:T(8,128)(2,1)} %collective-permute-done.4), channel_id=1, source_target_pairs={{0,240},{16,0},{32,16},{48,32},{64,48},{80,64},{96,80},{112,96},{1... | collective-permute-start | bytes 3538952 | tf_op jit(solution)/shard_map/ppermute | solution.py:28
  134.9 1.9 collective-permute-start.6
  136.8 3.9 collective-permute-start.5
  140.8 53.2 %collective-permute-done.6 = bf16[1,256,256]{1,2,0:T(8,128)(2,1)S(1)} collective-permute-done((bf16[1,256,256]{1,2,0:T(8,128)(2,1)S(1)}, bf16[1,256,256]{1,2,0:T(8,128)(2,1)S(1)}, u32[]{:S(2)}, u32[]{:S(2)}) %collective-permute-start.6) | collective-permute-done | bytes 131104 | tf_op jit(solution)/shard_map/ppermute | solution.py:19
  194.0 2.8 collective-permute-done.5
  197.3 1.3 fusion.126
  198.6 1.3 fusion.160
  199.9 1.3 fusion.162
  201.2 1.3 fusion.164
  202.5 1.3 fusion.166
  203.7 1.3 fusion.158
  205.0 1.3 fusion.200
  207.4 4.7 %fusion.25 = bf16[1,4,256,256]{2,3,1,0:T(8,128)(2,1)} fusion(f32[4,256,256]{2,1,0:T(8,128)} %fusion.158, f32[4,256,256]{2,1,0:T(8,128)} %fusion.126, f32[4,256,256]{2,1,0:T(8,128)} %fusion.160, f32[4,256,256]{2,1,0:T(8,128)} %fusion.162, f32[4,256,256]{2,1,0:T(8,128)} %fusion.200, f32[4,256,256]{2,1,0:T(8,128)} %fusion.164, f32[4,256,256]{2,1,0:T(8,128)} %fusion.166, ...), kind=kOutput, calls=%fused_computation.37 | convolution fusion | flops 137101312 | bytes 10092544 | tf_op jit(solution)/shard_map/oi,row->riw/dot_general | solution.py:43
  212.1 88.3 %reduce-scatter.6.cloned.1.call-done = f32[16,9,256]{2,1,0:T(8,128)} async-done(((f32[256,9,256]{2,1,0:T(8,128)}), f32[16,9,256]{2,1,0:T(8,128)}) %reduce-scatter.6.cloned.1.call-update) | async-done | bytes 147472 | tf_op jit(solution)/shard_map/reduce_scatter | solution.py:71
  301.4 5.0 %collective-permute-start.13 = (bf16[16,9,256]{2,0,1:T(8,128)(2,1)S(1)}, bf16[16,9,256]{2,0,1:T(8,128)(2,1)S(1)}, u32[]{:S(2)}, u32[]{:S(2)}) collective-permute-start(bf16[16,9,256]{2,0,1:T(8,128)(2,1)S(1)} %fusion.199), channel_id=1, source_target_pairs={{0,240},{16,0},{32,16},{48,32},{64,48},{80,64},{96,80},{112,96},{1... | collective-permute-start | bytes 221192 | tf_op jit(solution)/shard_map/ppermute | solution.py:28
  306.4 1.4 maximum_bitcast_fusion
  307.8 1.6 copy.176
  309.3 94.0 %reduce-scatter.8.cloned.1.call-done = f32[16,9,256]{2,1,0:T(8,128)} async-done(((f32[256,9,256]{2,1,0:T(8,128)}), f32[16,9,256]{2,1,0:T(8,128)}) %reduce-scatter.8.cloned.1.call-update) | async-done | bytes 147472 | tf_op jit(solution)/shard_map/reduce_scatter | solution.py:71
  403.3 1.7 fusion.202
  (87 shorter events, 21.4 us)
Async XLA Ops:
  7.2 199.1 %reduce-scatter.4.cloned.1.call-start = ((), (), s32[]{:S(2)}) async-start(), calls=%async_computation.3 | async-start | bytes 4456448 | tf_op jit(solution)/shard_map/reduce_scatter | solution.py:71
  8.7 10.4 %copy-start.6 = (bf16[1,4,256,256]{3,2,1,0:T(8,128)(2,1)S(1)}, bf16[1,4,256,256]{3,2,1,0:T(8,128)(2,1)}, u32[]{:S(2)}) copy-start(bf16[1,4,256,256]{3,2,1,0:T(8,128)(2,1)} %param.8) | copy-start | bytes 1572868
  10.5 23.2 %collective-permute-start.8 = (bf16[1,256,256]{1,2,0:T(8,128)(2,1)}, bf16[1,256,256]{1,2,0:T(8,128)(2,1)}, u32[]{:S(2)}, u32[]{:S(2)}) collective-permute-start(bf16[1,256,256]{1,2,0:T(8,128)(2,1)} %get-tuple-element.11), channel_id=1, source_target_pairs={{0,1},{1,2},{2,3},{3,4},{4,5},{5,6},{6,7},{7,8},{8,9},{9,10},{10,1... | collective-permute-start | bytes 393224 | tf_op jit(solution)/shard_map/ppermute | solution.py:17
  14.3 26.2 %collective-permute-start.9 = (bf16[1,256,256]{1,2,0:T(8,128)(2,1)}, bf16[1,256,256]{1,2,0:T(8,128)(2,1)S(1)}, u32[]{:S(2)}, u32[]{:S(2)}) collective-permute-start(bf16[1,256,256]{1,2,0:T(8,128)(2,1)} %get-tuple-element.12), channel_id=1, source_target_pairs={{1,0},{2,1},{3,2},{4,3},{5,4},{6,5},{7,6},{8,7},{9,8},{10,9},{11,1... | collective-permute-start | bytes 393224 | tf_op jit(solution)/shard_map/ppermute | solution.py:19
  20.0 44.7 %collective-permute-start.1 = (bf16[1,256,256]{1,2,0:T(8,128)(2,1)}, bf16[1,256,256]{1,2,0:T(8,128)(2,1)S(1)}, u32[]{:S(2)}, u32[]{:S(2)}) collective-permute-start(bf16[1,256,256]{1,2,0:T(8,128)(2,1)} %get-tuple-element.28), channel_id=1, source_target_pairs={{1,0},{2,1},{3,2},{4,3},{5,4},{6,5},{7,6},{8,7},{9,8},{10,9},{11,1... | collective-permute-start | bytes 393224 | tf_op jit(solution)/shard_map/ppermute | solution.py:19
  23.8 42.8 %collective-permute-start = (bf16[1,256,256]{1,2,0:T(8,128)(2,1)}, bf16[1,256,256]{1,2,0:T(8,128)(2,1)S(1)}, u32[]{:S(2)}, u32[]{:S(2)}) collective-permute-start(bf16[1,256,256]{1,2,0:T(8,128)(2,1)} %get-tuple-element.27), channel_id=1, source_target_pairs={{0,1},{1,2},{2,3},{3,4},{4,5},{5,6},{6,7},{7,8},{8,9},{9,10},{10,1... | collective-permute-start | bytes 393224 | tf_op jit(solution)/shard_map/ppermute | solution.py:17
  26.0 2.7 copy-start.10
  26.1 50.0 %copy-start = (bf16[4,256,256]{1,2,0:T(8,128)(2,1)}, bf16[4,256,256]{1,2,0:T(8,128)(2,1)S(1)}, u32[]{:S(2)}) copy-start(bf16[4,256,256]{1,2,0:T(8,128)(2,1)S(1)} %get-tuple-element.17) | copy-start | bytes 1572868
  26.9 49.2 %collective-permute-start.11 = (bf16[1,256,256]{1,2,0:T(8,128)(2,1)}, bf16[1,256,256]{1,2,0:T(8,128)(2,1)}, u32[]{:S(2)}, u32[]{:S(2)}) collective-permute-start(bf16[1,256,256]{1,2,0:T(8,128)(2,1)} %get-tuple-element.15), channel_id=1, source_target_pairs={{0,1},{1,2},{2,3},{3,4},{4,5},{5,6},{6,7},{7,8},{8,9},{9,10},{10,1... | collective-permute-start | bytes 393224 | tf_op jit(solution)/shard_map/ppermute | solution.py:17
  32.9 16.3 %copy-start.7 = (bf16[1,4,256,256]{3,2,1,0:T(8,128)(2,1)S(1)}, bf16[1,4,256,256]{3,2,1,0:T(8,128)(2,1)}, u32[]{:S(2)}) copy-start(bf16[1,4,256,256]{3,2,1,0:T(8,128)(2,1)} %param.8) | copy-start | bytes 1572868
  33.7 16.6 %copy-start.2 = (bf16[4,256,256]{1,2,0:T(8,128)(2,1)S(1)}, bf16[4,256,256]{1,2,0:T(8,128)(2,1)}, u32[]{:S(2)}) copy-start(bf16[4,256,256]{1,2,0:T(8,128)(2,1)} %get-tuple-element.13) | copy-start | bytes 1572868
  33.7 42.4 %collective-permute-start.12 = (bf16[1,256,256]{1,2,0:T(8,128)(2,1)}, bf16[1,256,256]{1,2,0:T(8,128)(2,1)}, u32[]{:S(2)}, u32[]{:S(2)}) collective-permute-start(bf16[1,256,256]{1,2,0:T(8,128)(2,1)} %get-tuple-element.16), channel_id=1, source_target_pairs={{1,0},{2,1},{3,2},{4,3},{5,4},{6,5},{7,6},{8,7},{9,8},{10,9},{11,1... | collective-permute-start | bytes 393224 | tf_op jit(solution)/shard_map/ppermute | solution.py:19
  40.5 69.7 %collective-permute-start.4 = (bf16[256,9,256]{2,0,1:T(8,128)(2,1)}, bf16[256,9,256]{2,0,1:T(8,128)(2,1)}, u32[]{:S(2)}, u32[]{:S(2)}) collective-permute-start(bf16[256,9,256]{2,0,1:T(8,128)(2,1)} %bitcast.4), channel_id=1, source_target_pairs={{0,240},{16,0},{32,16},{48,32},{64,48},{80,64},{96,80},{112,96},{1... | collective-permute-start | bytes 3538952 | tf_op jit(solution)/shard_map/ppermute | solution.py:28
  64.6 235.7 %reduce-scatter.6.cloned.1.call-start = ((), (), s32[]{:S(2)}) async-start(), calls=%async_computation.4 | async-start | bytes 4456448 | tf_op jit(solution)/shard_map/reduce_scatter | solution.py:71
  64.7 37.7 %collective-permute-start.14 = (bf16[1,256,256]{1,2,0:T(8,128)(2,1)}, bf16[1,256,256]{1,2,0:T(8,128)(2,1)}, u32[]{:S(2)}, u32[]{:S(2)}) collective-permute-start(bf16[1,256,256]{1,2,0:T(8,128)(2,1)} %get-tuple-element.19), channel_id=1, source_target_pairs={{0,1},{1,2},{2,3},{3,4},{4,5},{5,6},{6,7},{7,8},{8,9},{9,10},{10,1... | collective-permute-start | bytes 393224 | tf_op jit(solution)/shard_map/ppermute | solution.py:17
  66.6 35.8 %collective-permute-start.15 = (bf16[1,256,256]{1,2,0:T(8,128)(2,1)}, bf16[1,256,256]{1,2,0:T(8,128)(2,1)S(1)}, u32[]{:S(2)}, u32[]{:S(2)}) collective-permute-start(bf16[1,256,256]{1,2,0:T(8,128)(2,1)} %get-tuple-element.20), channel_id=1, source_target_pairs={{1,0},{2,1},{3,2},{4,3},{5,4},{6,5},{7,6},{8,7},{9,8},{10,9},{11,1... | collective-permute-start | bytes 393224 | tf_op jit(solution)/shard_map/ppermute | solution.py:19
  79.7 1.3 copy-start.8
  83.5 1.3 copy-start.4
  86.9 1.0 copy-start.1
  96.2 13.8 %collective-permute-start.3 = (bf16[1,256,256]{1,2,0:T(8,128)(2,1)S(1)}, bf16[1,256,256]{1,2,0:T(8,128)(2,1)S(1)}, u32[]{:S(2)}, u32[]{:S(2)}) collective-permute-start(bf16[1,256,256]{1,2,0:T(8,128)(2,1)S(1)} %get-tuple-element.26), channel_id=1, source_target_pairs={{1,0},{2,1},{3,2},{4,3},{5,4},{6,5},{7,6},{8,7},{9,8},{10,9},{11,1... | collective-permute-start | bytes 393224 | tf_op jit(solution)/shard_map/ppermute | solution.py:19
  98.2 11.8 %collective-permute-start.2 = (bf16[1,256,256]{1,2,0:T(8,128)(2,1)S(1)}, bf16[1,256,256]{1,2,0:T(8,128)(2,1)S(1)}, u32[]{:S(2)}, u32[]{:S(2)}) collective-permute-start(bf16[1,256,256]{1,2,0:T(8,128)(2,1)S(1)} %get-tuple-element.25), channel_id=1, source_target_pairs={{0,1},{1,2},{2,3},{3,4},{4,5},{5,6},{6,7},{7,8},{8,9},{9,10},{10,1... | collective-permute-start | bytes 393224 | tf_op jit(solution)/shard_map/ppermute | solution.py:17
  102.1 301.2 %reduce-scatter.8.cloned.1.call-start = ((), (), s32[]{:S(2)}) async-start(), calls=%async_computation.5 | async-start | bytes 4456448 | tf_op jit(solution)/shard_map/reduce_scatter | solution.py:71
  117.4 2.5 copy-start.3
  130.1 66.9 %collective-permute-start.7 = (bf16[256,9,256]{2,0,1:T(8,128)(2,1)}, bf16[256,9,256]{2,0,1:T(8,128)(2,1)S(1)}, u32[]{:S(2)}, u32[]{:S(2)}) collective-permute-start(bf16[256,9,256]{2,0,1:T(8,128)(2,1)} %collective-permute-done.4), channel_id=1, source_target_pairs={{0,240},{16,0},{32,16},{48,32},{64,48},{80,64},{96,80},{112,96},{1... | collective-permute-start | bytes 3538952 | tf_op jit(solution)/shard_map/ppermute | solution.py:28
  134.9 59.1 %collective-permute-start.6 = (bf16[1,256,256]{1,2,0:T(8,128)(2,1)S(1)}, bf16[1,256,256]{1,2,0:T(8,128)(2,1)S(1)}, u32[]{:S(2)}, u32[]{:S(2)}) collective-permute-start(bf16[1,256,256]{1,2,0:T(8,128)(2,1)S(1)} %get-tuple-element.24), channel_id=1, source_target_pairs={{1,0},{2,1},{3,2},{4,3},{5,4},{6,5},{7,6},{8,7},{9,8},{10,9},{11,1... | collective-permute-start | bytes 393224 | tf_op jit(solution)/shard_map/ppermute | solution.py:19
  136.8 60.0 %collective-permute-start.5 = (bf16[1,256,256]{1,2,0:T(8,128)(2,1)S(1)}, bf16[1,256,256]{1,2,0:T(8,128)(2,1)S(1)}, u32[]{:S(2)}, u32[]{:S(2)}) collective-permute-start(bf16[1,256,256]{1,2,0:T(8,128)(2,1)S(1)} %get-tuple-element.23), channel_id=1, source_target_pairs={{0,1},{1,2},{2,3},{3,4},{4,5},{5,6},{6,7},{7,8},{8,9},{9,10},{10,1... | collective-permute-start | bytes 393224 | tf_op jit(solution)/shard_map/ppermute | solution.py:17
  197.0 8.0 %copy-start.9 = (bf16[256,9,256]{2,0,1:T(8,128)(2,1)}, bf16[256,9,256]{2,0,1:T(8,128)(2,1)S(1)}, u32[]{:S(2)}) copy-start(bf16[256,9,256]{2,0,1:T(8,128)(2,1)S(1)} %collective-permute-done.7) | copy-start | bytes 3538948
  203.7 2.5 copy-start.11
  207.3 99.1 %copy-start.5 = (bf16[4,256,256]{1,2,0:T(8,128)(2,1)S(1)}, bf16[4,256,256]{1,2,0:T(8,128)(2,1)}, u32[]{:S(2)}) copy-start(bf16[4,256,256]{1,2,0:T(8,128)(2,1)} %get-tuple-element.30) | copy-start | bytes 1572868
  207.3 93.0 %collective-permute-start.10 = (bf16[16,9,256]{2,0,1:T(8,128)(2,1)S(1)}, bf16[16,9,256]{2,0,1:T(8,128)(2,1)S(1)}, u32[]{:S(2)}, u32[]{:S(2)}) collective-permute-start(bf16[16,9,256]{2,0,1:T(8,128)(2,1)S(1)} %copy.135), channel_id=1, source_target_pairs={{0,240},{16,0},{32,16},{48,32},{64,48},{80,64},{96,80},{112,96},{1... | collective-permute-start | bytes 221192 | tf_op jit(solution)/shard_map/ppermute | solution.py:28
  301.4 7.9 %collective-permute-start.13 = (bf16[16,9,256]{2,0,1:T(8,128)(2,1)S(1)}, bf16[16,9,256]{2,0,1:T(8,128)(2,1)S(1)}, u32[]{:S(2)}, u32[]{:S(2)}) collective-permute-start(bf16[16,9,256]{2,0,1:T(8,128)(2,1)S(1)} %fusion.199), channel_id=1, source_target_pairs={{0,240},{16,0},{32,16},{48,32},{64,48},{80,64},{96,80},{112,96},{1... | collective-permute-start | bytes 221192 | tf_op jit(solution)/shard_map/ppermute | solution.py:28
Sparse Core Ops, SparseCore 0:
  64.8 137.6 reduce-scatter.3
  205.0 95.3 reduce-scatter.5
  302.9 100.3 reduce-scatter.7
where the time goes:
time: 416 us; the launch traced here: 411 us
  waiting for transfers between devices  245 us (59%)
  starting transfers between devices  61.1 us (15%)
  matrix products  57.5 us (14%)
  local copies, waits for them, and re-layouts  23.5 us (6%)
  between operations  14.4 us (3%)
  other arithmetic  10.2 us (2%)
    reduce_scatter x3, waiting for transfers between devices, tick_work(): lax.psum_scatter(weight_terms(grad_tile, input_wide, cell_scale), 'rows',...  182 us
    ppermute x6, waiting for transfers between devices, padded(): lax.ppermute(head, axis, [((i + 1) % count, i) for i in range(ends)])  59.7 us
    dot_general x27, matrix products, back_project(): jnp.einsum('oi,row->riw', kernel[:, tap_index, :], window, preferred_elem...  38.1 us
    ppermute x6, starting transfers between devices, padded(): lax.ppermute(head, axis, [((i + 1) % count, i) for i in range(ends)])  25.9 us
    dot_general x27, matrix products, weight_terms(): jnp.einsum('row,riw->oi', grad_tile, window, preferred_element_type=jnp.f...  19.4 us
    ppermute x6, starting transfers between devices, padded(): lax.ppermute(tail, axis, [(i, (i + 1) % count) for i in range(ends)])  17.5 us
    ppermute x4, starting transfers between devices, shifted(): lax.ppermute(value, axis, [(i, (i + by) % peers) for i in range(peers)])  17.4 us
    another operation x3, local copies, waits for them, and re-layouts, weight_terms(): return jnp.stack(tap_list, axis=1)  12 us
  transfers between devices with their start and end apart: 19, of which 5 were waited for; matrix products, arithmetic and copies ran while one was open for 21% of the time, Pallas kernels for 0%

commit v1 on v0

v1 whole, which is shorter than its diff:
```python
import functools

import jax
import jax.numpy as jnp
from jax import lax
from jax.experimental import pallas as pl
from jax.experimental.pallas import tpu as pltpu
from jax.sharding import PartitionSpec as P

TICKS = 3
BF = jnp.bfloat16
F32 = jnp.float32
VMEM_BYTES = 28 * 1024 * 1024


def whole(memory=pltpu.VMEM):
    return pl.BlockSpec(memory_space=memory)


def fill_shifted(shift_ref, rows):
    for index, row in enumerate(rows):
        wide = row.astype(F32)
        columns = wide.shape[1]
        place = lax.broadcasted_iota(jnp.int32, wide.shape, 1)
        ahead = pltpu.roll(wide, columns - 1, 1)
        behind = pltpu.roll(wide, 1, 1)
        shift_ref[0, index] = jnp.where(place == columns - 1, 0.0, ahead).astype(BF)
        shift_ref[1, index] = row
        shift_ref[2, index] = jnp.where(place == 0, 0.0, behind).astype(BF)


def back_kernel(tick, height, last, *refs):
    refs = list(refs)
    flag = None if last else refs.pop(0)
    up, top, mid, bot, down, kernel, saved = refs[:7]
    refs = refs[7:]
    fresh = None if last else refs.pop(0)
    if tick > 0:
        refs.pop(0)
    states = refs.pop(0)
    if not last:
        next_top, next_mid, next_bot = refs[:3]
        refs = refs[3:]
    shift_ref, turned, result, sem = refs
    channels = top.shape[0]
    rows = [up[...], top[...], *[mid[i] for i in range(height - 2)], bot[...], down[...]]
    fill_shifted(shift_ref, rows)
    for b in range(3):
        for j in range(3):
            turned[b, :, j * channels : (j + 1) * channels] = kernel[3 * (2 - j) + b].T
    for r in range(height):
        total = None
        for b in range(3):
            window = shift_ref[b, r : r + 3].reshape(3 * channels, -1)
            part = jnp.dot(turned[b], window, preferred_element_type=F32)
            total = part if total is None else total + part
        value = jnp.where(saved[r] > 0, total, 0.0).astype(BF)
        result[r] = value
        if not last:
            value = jnp.where(flag[0] > 0, fresh[r], value)
            if r == 0:
                next_top[...] = value
            elif r == height - 1:
                next_bot[...] = value
            else:
                next_mid[r - 1] = value
    copy = pltpu.make_async_copy(result, states.at[tick, 0], sem)
    copy.start()
    copy.wait()


def back_project(tick, edges, kernel, saved, states, restart, fresh):
    up, top, mid, bot, down = edges
    last = restart is None
    height, channels, columns = saved.shape
    args = ([] if last else [restart]) + [up, top, mid, bot, down, kernel, saved]
    specs = ([] if last else [whole(pltpu.SMEM)]) + [whole()] * 7
    if not last:
        args.append(fresh)
        specs.append(whole())
    alias = {}
    if tick > 0:
        alias = {len(args): 0}
        args.append(states)
        specs.append(whole(pl.ANY))
    shapes = [jax.ShapeDtypeStruct((TICKS, 1, height, channels, columns), BF)]
    if not last:
        shapes += [
            jax.ShapeDtypeStruct((channels, columns), BF),
            jax.ShapeDtypeStruct((height - 2, channels, columns), BF),
            jax.ShapeDtypeStruct((channels, columns), BF),
        ]
    return pl.pallas_call(
        functools.partial(back_kernel, tick, height, last),
        out_shape=shapes,
        in_specs=specs,
        out_specs=[whole(pl.ANY)] + [whole()] * (len(shapes) - 1),
        scratch_shapes=[
            pltpu.VMEM((3, height + 2, channels, columns), BF),
            pltpu.VMEM((3, channels, 3 * channels), BF),
            pltpu.VMEM((height, channels, columns), BF),
            pltpu.SemaphoreType.DMA,
        ],
        input_output_aliases=alias,
        compiler_params=pltpu.CompilerParams(vmem_limit_bytes=VMEM_BYTES),
        cost_estimate=pl.CostEstimate(
            flops=18 * height * channels * channels * columns, bytes_accessed=4 << 20, transcendentals=0
        ),
        name="back",
    )(*args)


def weight_kernel(height, scale, spot, up, top, mid, bot, down, saved, own, one, two, three, shift_ref):
    channels = top.shape[0]
    rows = [up[...], top[...], *[mid[i] for i in range(height - 2)], bot[...], down[...]]
    fill_shifted(shift_ref, rows)
    inputs = [jnp.maximum(saved[r], 0) for r in range(height)]
    part = channels // 4
    piece = part // 4
    for k, out in enumerate((own, one, two, three)):
        place = lax.rem(spot[0] + k, 4)
        start = pl.multiple_of(place * part, part)
        total = None
        for r in range(height):
            left = shift_ref[:, r : r + 3, pl.ds(start, part), :].reshape(9 * part, -1)
            term = lax.dot_general(left, inputs[r], (((1,), (1,)), ((), ())), preferred_element_type=F32)
            total = term if total is None else total + term
        total = total * scale
        for b in range(3):
            for j in range(3):
                base = (3 * b + j) * part
                for q in range(4):
                    out[q, 3 * (2 - j) + b] = total[base + q * piece : base + (q + 1) * piece].astype(out.dtype)


def weight_terms(edges, saved, spot, scale):
    height, channels, columns = saved.shape
    part = (4, 9, channels // 16, channels)
    return pl.pallas_call(
        functools.partial(weight_kernel, height, scale),
        out_shape=[jax.ShapeDtypeStruct(part, F32)] + [jax.ShapeDtypeStruct(part, BF)] * 3,
        in_specs=[whole(pltpu.SMEM)] + [whole()] * 6,
        out_specs=[whole()] * 4,
        scratch_shapes=[pltpu.VMEM((3, height + 2, channels, columns), BF)],
        compiler_params=pltpu.CompilerParams(vmem_limit_bytes=VMEM_BYTES),
        cost_estimate=pl.CostEstimate(
            flops=18 * height * channels * channels * columns, bytes_accessed=4 << 20, transcendentals=0
        ),
        name="weight",
    )(spot, *edges, saved)


def regroup_kernel(spot, own, one, two, three, mine, first, second, third):
    for k, out in enumerate((mine, first, second, third)):
        place = lax.rem(spot[0] + k, 4)
        value = (own[place] + one[place].astype(F32)) + (two[place].astype(F32) + three[place].astype(F32))
        out[...] = value.astype(out.dtype)


def regroup(spot, parts):
    shape = parts[0].shape[1:]
    return pl.pallas_call(
        regroup_kernel,
        out_shape=[jax.ShapeDtypeStruct(shape, F32)] + [jax.ShapeDtypeStruct(shape, BF)] * 3,
        in_specs=[whole(pltpu.SMEM)] + [whole()] * 4,
        out_specs=[whole()] * 4,
        compiler_params=pltpu.CompilerParams(vmem_limit_bytes=VMEM_BYTES),
        name="regroup",
    )(spot, *parts)


def finish_kernel(held, own, one, two, three, out):
    value = (own[...] + one[...].astype(F32)) + (two[...].astype(F32) + three[...].astype(F32))
    out[...] = (held[...].astype(F32) + value).astype(BF)


def finish(held, parts):
    return pl.pallas_call(
        finish_kernel,
        out_shape=jax.ShapeDtypeStruct(held.shape, BF),
        in_specs=[whole()] * 5,
        out_specs=whole(),
        name="finish",
    )(held, *parts)


def along(value, move):
    return lax.ppermute(value, "rows", [(x * 4 + z, move(x, z)) for x in range(4) for z in range(4)])


def shifted(value, by):
    return lax.ppermute(value, "blk", [(i, (i + by) % 16) for i in range(16)])


def with_edges(top, mid, bot):
    up = lax.ppermute(bot, "rows", [(i, i + 1) for i in range(15)])
    down = lax.ppermute(top, "rows", [(i + 1, i) for i in range(15)])
    return up, top, mid, bot, down


def reduce_rows(parts, spot_z):
    moved = [parts[0]] + [
        along(parts[k], lambda x, z, k=k: ((x + k) % 4) * 4 + z) for k in (2, 1, 3)
    ]
    pieces = regroup(spot_z, moved)
    return [pieces[0]] + [
        along(pieces[k], lambda x, z, k=k: x * 4 + (z + k) % 4) for k in (2, 1, 3)
    ]


def shards(section_weights, grad_acc, saved_inputs, cotangent, fresh_grads):
    position = lax.axis_index("blk")
    row = lax.axis_index("rows")
    spot_x = (row // 4).reshape(1)
    spot_z = (row % 4).reshape(1)
    kernel = jnp.transpose(section_weights[0], (1, 0, 2))
    held = jnp.transpose(grad_acc[0], (1, 0, 2))
    height = cotangent.shape[1]
    columns = cotangent.shape[3]
    scale = float(16 * height * columns) ** (-0.5)
    image = cotangent[0]
    edges = with_edges(image[0], image[1 : height - 1], image[height - 1])
    kernels = [kernel, shifted(kernel, -1), shifted(kernel, -2)]
    states = None
    for tick in range(TICKS):
        saved = saved_inputs[tick, 0]
        now = edges
        if tick + 1 < TICKS:
            restart = (position == 16 - tick - 1).astype(jnp.int32).reshape(1)
            states, *parts = back_project(tick, now, kernels[tick], saved, states, restart, fresh_grads[tick])
            edges = with_edges(*parts)
        else:
            (states,) = back_project(tick, now, kernels[tick], saved, states, None, None)
        sums = reduce_rows(weight_terms(now, saved, spot_x, scale), spot_z)
        held = finish(held, sums)
        if tick + 1 < TICKS:
            held = shifted(held, -1)
    return states, jnp.transpose(held, (1, 0, 2))[None]


def solution(mesh):
    return jax.shard_map(
        shards,
        mesh=mesh,
        in_specs=(
            P("blk", None, None, None),
            P("blk", "rows", None, None),
            P(None, "blk", "rows", None, None),
            P("blk", "rows", None, None),
            P(None, "rows", None, None),
        ),
        out_specs=(P(None, "blk", "rows", None, None), P("blk", "rows", None, None)),
        check_vma=False,
    )
```

time: 416 us -> 201 us (0.48)
  waiting for transfers between devices: 245 us -> 88.2 us
  matrix products: 57.5 us -> 0 us
  Pallas kernels: 0 us -> 25.6 us
  between operations: 14.4 us -> 1.08 us
  other arithmetic: 10.2 us -> 0 us
  local copies, waits for them, and re-layouts: 23.5 us -> 19.1 us
    reduce_scatter x3 -> x0, waiting for transfers between devices: 182 us -> none  [tick_work(): lax.psum_scatter(weight_terms(grad_tile, input_wide, cell_scale), 'rows',...]
    dot_general x54 -> x0, matrix products: 57.5 us -> none  [the longest x27 38.1 us: back_project(): jnp.einsum('oi,row->riw', kernel[:, tap_index, :], window, preferred_elem...]
    ppermute x16 -> x28, waiting for transfers between devices: 62.6 us -> 88.2 us  [the longest x3 70.5 us: with_edges(): up = lax.ppermute(bot, 'rows', [(i, i + 1) for i in range(15)])]
    pallas_call x0 -> x12, Pallas kernels: none -> 25.6 us  [the longest x3 10 us: back_project(): pl.pallas_call(functools.partial(back_kernel, tick, height, last), out_sh...]
    another operation x3 -> x0, local copies, waits for them, and re-layouts: 12 us -> none  [weight_terms(): return jnp.stack(tap_list, axis=1)]
    unnamed x31 -> x92, local copies, waits for them, and re-layouts: 6.16 us -> 15.7 us
    slice x8 -> x1, local copies, waits for them, and re-layouts: 5.27 us -> 0.02 us  [shards(): edges = with_edges(image[0], image[1:height - 1], image[height - 1])]
    ppermute x16 -> x28, starting transfers between devices: 60.8 us -> 62.9 us  [the longest x18 26.6 us: along(): lax.ppermute(value, 'rows', [(x * 4 + z, move(x, z)) for x in range(4) fo...]
  transfers between devices with their start and end apart: 19 -> 28, of which waited for: 5 -> 10; matrix products, arithmetic and copies ran while one was open for 21% -> 2% of each run, Pallas kernels for 0% -> 12%
where the time goes in v1:
time: 201 us; the launch traced here: 197 us
  waiting for transfers between devices  88.2 us (44%)
  starting transfers between devices  62.9 us (31%)
  Pallas kernels  25.6 us (13%)
  local copies, waits for them, and re-layouts  19.1 us (10%)
    ppermute x3, waiting for transfers between devices, with_edges(): up = lax.ppermute(bot, 'rows', [(i, i + 1) for i in range(15)])  70.5 us
    ppermute x18, starting transfers between devices, along(): lax.ppermute(value, 'rows', [(x * 4 + z, move(x, z)) for x in range(4) fo...  26.6 us
    ppermute x3, starting transfers between devices, with_edges(): down = lax.ppermute(top, 'rows', [(i + 1, i) for i in range(15)])  18.4 us
    unnamed x92, local copies, waits for them, and re-layouts  15.7 us
    ppermute x18, waiting for transfers between devices, along(): lax.ppermute(value, 'rows', [(x * 4 + z, move(x, z)) for x in range(4) fo...  14.5 us
    pallas_call x3, Pallas kernels, back_project(): pl.pallas_call(functools.partial(back_kernel, tick, height, last), out_sh...  10 us
    ppermute x4, starting transfers between devices, shifted(): return lax.ppermute(value, 'blk', [(i, (i + by) % 16) for i in range(16)])  9.9 us
    pallas_call x3, Pallas kernels, weight_terms(): pl.pallas_call(functools.partial(weight_kernel, height, scale), out_shape...  8.74 us
  transfers between devices with their start and end apart: 28, of which 10 were waited for; matrix products, arithmetic and copies ran while one was open for 2% of the time, Pallas kernels for 12%

profile of v1, /device:TPU:2, one launch (start us, length us, event | category | flops | bytes accessed | tf_op | source)
XLA Modules:
  0.0 196.9 jit_solution(18384834311847852449)
XLA Ops:
  0.6 9.2 %collective-permute-start.4 = (bf16[9,256,256]{2,1,0:T(8,128)(2,1)}, bf16[9,256,256]{2,1,0:T(8,128)(2,1)S(1)}, u32[]{:S(2)}, u32[]{:S(2)}) collective-permute-start(bf16[9,256,256]{2,1,0:T(8,128)(2,1)} %bitcast.29), channel_id=1, source_target_pairs={{0,240},{16,0},{32,16},{48,32},{64,48},{80,64},{96,80},{112,96},{1... | collective-permute-start | bytes 3538952 | tf_op jit(solution)/shard_map/ppermute | solution.py:192
  9.8 0.7 collective-permute-start.7
  10.5 1.0 slice_bitcast_fusion.6
  11.5 2.9 %collective-permute-start = (bf16[256,256]{1,0:T(8,128)(2,1)S(1)}, bf16[256,256]{1,0:T(8,128)(2,1)S(1)}, u32[]{:S(2)}, u32[]{:S(2)}) collective-permute-start(bf16[256,256]{1,0:T(8,128)(2,1)S(1)} %get-tuple-element.72.refs_4_.bot), channel_id=1, source_target_pairs={{0,1},{1,2},{2,3},{3,4},{4,5},{5,6},{6,7},{7,8},{8,9},{9,10},{10,1... | collective-permute-start | bytes 393224 | tf_op jit(solution)/shard_map/ppermute | solution.py:196
  14.5 5.6 %collective-permute-start.1 = (bf16[256,256]{1,0:T(8,128)(2,1)S(1)}, bf16[256,256]{1,0:T(8,128)(2,1)S(1)}, u32[]{:S(2)}, u32[]{:S(2)}) collective-permute-start(bf16[256,256]{1,0:T(8,128)(2,1)S(1)} %get-tuple-element.71.refs_2_.top), channel_id=1, source_target_pairs={{1,0},{2,1},{3,2},{4,3},{5,4},{6,5},{7,6},{8,7},{9,8},{10,9},{11,1... | collective-permute-start | bytes 393224 | tf_op jit(solution)/shard_map/ppermute | solution.py:197
  20.1 1.5 slice_bitcast_fusion
  21.7 70.4 %collective-permute-done.refs_1_.up = bf16[256,256]{1,0:T(8,128)(2,1)S(1)} collective-permute-done((bf16[256,256]{1,0:T(8,128)(2,1)S(1)}, bf16[256,256]{1,0:T(8,128)(2,1)S(1)}, u32[]{:S(2)}, u32[]{:S(2)}) %collective-permute-start) | collective-permute-done | bytes 131104 | tf_op jit(solution)/shard_map/ppermute | solution.py:196
  92.1 1.9 collective-permute-done.1.refs_5_.down
  94.1 2.6 %weight.3 = (f32[4,9,16,256]{3,2,1,0:T(8,128)S(1)}, bf16[4,9,16,256]{3,2,1,0:T(8,128)(2,1)}, bf16[4,9,16,256]{3,2,1,0:T(8,128)(2,1)}, bf16[4,9,16,256]{3,2,1,0:T(8,128)(2,1)}) custom-call(s32[1]{0:T(128)} %bitcast.16.spot, bf16[256,256]{1,0:T(8,128)(2,1)S(1)} %collective-permute-done.refs_1_.up, bf16[256,256]{1,0:T(8,128)(2,1)S(1)} %get-tuple-element.71.refs_2_.top, ...), custom_call_target="tpu_custom_call" | custom-call | flops 1207959552 | bytes 4194304 | tf_op jit(solution)/shard_map/weight/pallas_call | solution.py:139
  96.7 0.6 collective-permute-start.10
  97.3 2.4 %collective-permute-start.8 = (bf16[4,9,16,256]{3,2,1,0:T(8,128)(2,1)}, bf16[4,9,16,256]{3,2,1,0:T(8,128)(2,1)}, u32[]{:S(2)}, u32[]{:S(2)}) collective-permute-start(bf16[4,9,16,256]{3,2,1,0:T(8,128)(2,1)} %get-tuple-element.43), channel_id=1, source_target_pairs={{0,8},{1,9},{2,10},{3,11},{4,12},{5,13},{6,14},{7,15},{8,0},{9,1},... | collective-permute-start | bytes 884744 | tf_op jit(solution)/shard_map/ppermute | solution.py:188
  99.7 0.4 collective-permute-start.9
  100.1 0.9 slice_bitcast_fusion.1
  101.0 1.0 copy-done.1
  102.0 1.0 copy-done.2
  103.1 0.9 copy-done.11
  104.0 0.9 copy-done.25
  104.9 0.9 copy-done.27
  105.8 1.3 copy-done.28
  107.1 0.9 copy-done.30
  108.0 0.9 copy-done.32
  108.9 3.0 %back.3 = (bf16[3,1,4,256,256]{4,3,2,1,0:T(8,128)(2,1)}, bf16[256,256]{1,0:T(8,128)(2,1)S(1)}, bf16[2,256,256]{2,1,0:T(8,128)(2,1)S(1)}, bf16[256,256]{1,0:T(8,128)(2,1)}) custom-call(s32[1]{0:T(128)} %bitcast.1.refs_0_, bf16[256,256]{1,0:T(8,128)(2,1)S(1)} %copy-done.30, bf16[256,256]{1,0:T(8,128)(2,1)S(1)} %copy-done.25, ...), custom_call_target="tpu_custom_call" | custom-call | flops 1207959552 | bytes 4194304 | tf_op jit(solution)/shard_map/back/pallas_call | solution.py:93
  111.9 0.7 copy-done.8
  112.6 3.0 %collective-permute-start.2 = (bf16[256,256]{1,0:T(8,128)(2,1)}, bf16[256,256]{1,0:T(8,128)(2,1)}, u32[]{:S(2)}, u32[]{:S(2)}) collective-permute-start(bf16[256,256]{1,0:T(8,128)(2,1)} %get-tuple-element.34.refs_4_.bot), channel_id=1, source_target_pairs={{0,1},{1,2},{2,3},{3,4},{4,5},{5,6},{6,7},{7,8},{8,9},{9,10},{10,1... | collective-permute-start | bytes 393224 | tf_op jit(solution)/shard_map/ppermute | solution.py:196
  115.6 5.5 %collective-permute-start.3 = (bf16[256,256]{1,0:T(8,128)(2,1)S(1)}, bf16[256,256]{1,0:T(8,128)(2,1)}, u32[]{:S(2)}, u32[]{:S(2)}) collective-permute-start(bf16[256,256]{1,0:T(8,128)(2,1)S(1)} %get-tuple-element.35.refs_2_.top), channel_id=1, source_target_pairs={{1,0},{2,1},{3,2},{4,3},{5,4},{6,5},{7,6},{8,7},{9,8},{10,9},{11,1... | collective-permute-start | bytes 393224 | tf_op jit(solution)/shard_map/ppermute | solution.py:197
  121.2 1.3 regroup.3
  122.7 0.9 collective-permute-start.12
  123.6 0.6 collective-permute-done.3.refs_5_.down
  124.2 4.6 %collective-permute-start.13 = (bf16[9,16,256]{2,1,0:T(8,128)(2,1)S(1)}, bf16[9,16,256]{2,1,0:T(8,128)(2,1)S(1)}, u32[]{:S(2)}, u32[]{:S(2)}) collective-permute-start(bf16[9,16,256]{2,1,0:T(8,128)(2,1)S(1)} %get-tuple-element.49), channel_id=1, source_target_pairs={{0,3},{1,0},{2,1},{3,2},{4,7},{5,4},{6,5},{7,6},{8,11},{9,8},{10,9... | collective-permute-start | bytes 221192 | tf_op jit(solution)/shard_map/ppermute | solution.py:188
  128.8 0.9 copy-done.23
  129.7 3.4 %back.4 = (bf16[3,1,4,256,256]{4,3,2,1,0:T(8,128)(2,1)}, bf16[256,256]{1,0:T(8,128)(2,1)S(1)}, bf16[2,256,256]{2,1,0:T(8,128)(2,1)S(1)}, bf16[256,256]{1,0:T(8,128)(2,1)S(1)}) custom-call(s32[1]{0:T(128)} %bitcast.refs_0_, bf16[256,256]{1,0:T(8,128)(2,1)} %collective-permute-done.2.refs_1_.up, ...), custom_call_target="tpu_custom_call", output_to_operand_aliasing={{0}: (9, {})} | custom-call | flops 1207959552 | bytes 4194304 | tf_op jit(solution)/shard_map/back/pallas_call | solution.py:93
  133.1 2.1 %collective-permute-start.5 = (bf16[256,256]{1,0:T(8,128)(2,1)S(1)}, bf16[256,256]{1,0:T(8,128)(2,1)S(1)}, u32[]{:S(2)}, u32[]{:S(2)}) collective-permute-start(bf16[256,256]{1,0:T(8,128)(2,1)S(1)} %get-tuple-element.38.refs_3_.bot), channel_id=1, source_target_pairs={{0,1},{1,2},{2,3},{3,4},{4,5},{5,6},{6,7},{7,8},{8,9},{9,10},{10,1... | collective-permute-start | bytes 393224 | tf_op jit(solution)/shard_map/ppermute | solution.py:196
  135.2 3.5 %weight.4 = (f32[4,9,16,256]{3,2,1,0:T(8,128)S(1)}, bf16[4,9,16,256]{3,2,1,0:T(8,128)(2,1)}, bf16[4,9,16,256]{3,2,1,0:T(8,128)(2,1)S(1)}, bf16[4,9,16,256]{3,2,1,0:T(8,128)(2,1)}) custom-call(s32[1]{0:T(128)} %bitcast.16.spot, bf16[256,256]{1,0:T(8,128)(2,1)} %collective-permute-done.2.refs_1_.up, bf16[256,256]{1,0:T(8,128)(2,1)S(1)} %copy-done.23, ...), custom_call_target="tpu_custom_call" | custom-call | flops 1207959552 | bytes 4194304 | tf_op jit(solution)/shard_map/weight/pallas_call | solution.py:139
  138.8 1.1 collective-permute-start.15
  139.9 2.0 %collective-permute-start.16 = (bf16[4,9,16,256]{3,2,1,0:T(8,128)(2,1)}, bf16[4,9,16,256]{3,2,1,0:T(8,128)(2,1)S(1)}, u32[]{:S(2)}, u32[]{:S(2)}) collective-permute-start(bf16[4,9,16,256]{3,2,1,0:T(8,128)(2,1)} %get-tuple-element.52), channel_id=1, source_target_pairs={{0,4},{1,5},{2,6},{3,7},{4,8},{5,9},{6,10},{7,11},{8,12},{9,13},{1... | collective-permute-start | bytes 884744 | tf_op jit(solution)/shard_map/ppermute | solution.py:188
  141.9 0.6 copy-done.39
  142.5 2.6 %collective-permute-start.17 = (bf16[4,9,16,256]{3,2,1,0:T(8,128)(2,1)}, bf16[4,9,16,256]{3,2,1,0:T(8,128)(2,1)S(1)}, u32[]{:S(2)}, u32[]{:S(2)}) collective-permute-start(bf16[4,9,16,256]{3,2,1,0:T(8,128)(2,1)} %get-tuple-element.53), channel_id=1, source_target_pairs={{0,12},{1,13},{2,14},{3,15},{4,0},{5,1},{6,2},{7,3},{8,4},{9,5},{1... | collective-permute-start | bytes 884744 | tf_op jit(solution)/shard_map/ppermute | solution.py:188
  145.1 7.2 %collective-permute-start.6 = (bf16[256,256]{1,0:T(8,128)(2,1)S(1)}, bf16[256,256]{1,0:T(8,128)(2,1)S(1)}, u32[]{:S(2)}, u32[]{:S(2)}) collective-permute-start(bf16[256,256]{1,0:T(8,128)(2,1)S(1)} %get-tuple-element.39.refs_1_.top), channel_id=1, source_target_pairs={{1,0},{2,1},{3,2},{4,3},{5,4},{6,5},{7,6},{8,7},{9,8},{10,9},{11,1... | collective-permute-start | bytes 393224 | tf_op jit(solution)/shard_map/ppermute | solution.py:197
  152.3 1.7 finish.3
  154.1 0.8 collective-permute-done.6.refs_4_.down
  154.8 1.0 copy-done.6
  155.8 0.9 copy-done.16
  156.7 2.6 %weight.5 = (f32[4,9,16,256]{3,2,1,0:T(8,128)S(1)}, bf16[4,9,16,256]{3,2,1,0:T(8,128)(2,1)}, bf16[4,9,16,256]{3,2,1,0:T(8,128)(2,1)}, bf16[4,9,16,256]{3,2,1,0:T(8,128)(2,1)}) custom-call(s32[1]{0:T(128)} %bitcast.16.spot, bf16[256,256]{1,0:T(8,128)(2,1)S(1)} %collective-permute-done.5.refs_0_.up, bf16[256,256]{1,0:T(8,128)(2,1)S(1)} %get-tuple-element.39.refs_1_.top, ...), custom_call_target="tpu_custom_call" | custom-call | flops 1207959552 | bytes 4194304 | tf_op jit(solution)/shard_map/weight/pallas_call | solution.py:139
  159.3 1.1 collective-permute-start.22
  160.6 0.7 copy-done.3
  161.3 1.8 collective-permute-start.24
  163.2 1.0 copy-done.4
  164.3 0.7 copy-done.14
  165.0 0.3 collective-permute-start.18
  165.3 5.1 %collective-permute-done.18.one = bf16[9,16,256]{2,1,0:T(8,128)(2,1)S(1)} collective-permute-done((bf16[9,16,256]{2,1,0:T(8,128)(2,1)S(1)}, bf16[9,16,256]{2,1,0:T(8,128)(2,1)S(1)}, u32[]{:S(2)}, u32[]{:S(2)}) %collective-permute-start.18) | collective-permute-done | bytes 73760 | tf_op jit(solution)/shard_map/ppermute | solution.py:188
  170.4 2.1 %collective-permute-start.19 = (bf16[9,16,256]{2,1,0:T(8,128)(2,1)S(1)}, bf16[9,16,256]{2,1,0:T(8,128)(2,1)S(1)}, u32[]{:S(2)}, u32[]{:S(2)}) collective-permute-start(bf16[9,16,256]{2,1,0:T(8,128)(2,1)S(1)} %get-tuple-element.56), channel_id=1, source_target_pairs={{0,1},{1,2},{2,3},{3,0},{4,5},{5,6},{6,7},{7,4},{8,9},{9,10},{10,1... | collective-permute-start | bytes 221192 | tf_op jit(solution)/shard_map/ppermute | solution.py:188
  172.5 4.7 %collective-permute-done.19.two = bf16[9,16,256]{2,1,0:T(8,128)(2,1)S(1)} collective-permute-done((bf16[9,16,256]{2,1,0:T(8,128)(2,1)S(1)}, bf16[9,16,256]{2,1,0:T(8,128)(2,1)S(1)}, u32[]{:S(2)}, u32[]{:S(2)}) %collective-permute-start.19) | collective-permute-done | bytes 73760 | tf_op jit(solution)/shard_map/ppermute | solution.py:188
  177.2 2.0 %collective-permute-start.20 = (bf16[9,16,256]{2,1,0:T(8,128)(2,1)S(1)}, bf16[9,16,256]{2,1,0:T(8,128)(2,1)S(1)}, u32[]{:S(2)}, u32[]{:S(2)}) collective-permute-start(bf16[9,16,256]{2,1,0:T(8,128)(2,1)S(1)} %get-tuple-element.57), channel_id=1, source_target_pairs={{0,3},{1,0},{2,1},{3,2},{4,7},{5,4},{6,5},{7,6},{8,11},{9,8},{10,9... | collective-permute-start | bytes 221192 | tf_op jit(solution)/shard_map/ppermute | solution.py:188
  179.2 2.4 %collective-permute-done.20.three = bf16[9,16,256]{2,1,0:T(8,128)(2,1)S(1)} collective-permute-done((bf16[9,16,256]{2,1,0:T(8,128)(2,1)S(1)}, bf16[9,16,256]{2,1,0:T(8,128)(2,1)S(1)}, u32[]{:S(2)}, u32[]{:S(2)}) %collective-permute-start.20) | collective-permute-done | bytes 73760 | tf_op jit(solution)/shard_map/ppermute | solution.py:188
  181.6 0.6 copy-done.45
  182.2 1.7 finish.4
  184.1 0.6 collective-permute-start.25
  184.7 3.8 %collective-permute-start.26 = (bf16[9,16,256]{2,1,0:T(8,128)(2,1)S(1)}, bf16[9,16,256]{2,1,0:T(8,128)(2,1)S(1)}, u32[]{:S(2)}, u32[]{:S(2)}) collective-permute-start(bf16[9,16,256]{2,1,0:T(8,128)(2,1)S(1)} %get-tuple-element.64), channel_id=1, source_target_pairs={{0,1},{1,2},{2,3},{3,0},{4,5},{5,6},{6,7},{7,4},{8,9},{9,10},{10,1... | collective-permute-start | bytes 221192 | tf_op jit(solution)/shard_map/ppermute | solution.py:188
  188.6 3.6 %back.5 = bf16[3,1,4,256,256]{4,3,2,1,0:T(8,128)(2,1)} custom-call(bf16[256,256]{1,0:T(8,128)(2,1)S(1)} %copy-done.19, bf16[256,256]{1,0:T(8,128)(2,1)S(1)} %get-tuple-element.39.refs_1_.top, bf16[2,256,256]{2,1,0:T(8,128)(2,1)S(1)} %copy-done.7, bf16[256,256]{1,0:T(8,128)(2,1)S(1)} %copy-done.17, ...), custom_call_target="tpu_custom_call", output_to_operand_aliasing={{}: (7, {})} | custom-call | flops 1207959552 | bytes 4194304 | tf_op jit(solution)/shard_map/back/pallas_call | solution.py:93
  192.2 1.5 collective-permute-done.25.one
  193.8 0.4 collective-permute-done.26.two
  194.1 0.4 collective-permute-done.27.three
  194.8 0.4 copy-done.42
  195.2 1.7 finish.5
  (100 shorter events, 1.1 us)
Async XLA Ops:
  0.6 128.1 %collective-permute-start.4 = (bf16[9,256,256]{2,1,0:T(8,128)(2,1)}, bf16[9,256,256]{2,1,0:T(8,128)(2,1)S(1)}, u32[]{:S(2)}, u32[]{:S(2)}) collective-permute-start(bf16[9,256,256]{2,1,0:T(8,128)(2,1)} %bitcast.29), channel_id=1, source_target_pairs={{0,240},{16,0},{32,16},{48,32},{64,48},{80,64},{96,80},{112,96},{1... | collective-permute-start | bytes 3538952 | tf_op jit(solution)/shard_map/ppermute | solution.py:192
  9.8 178.8 %collective-permute-start.7 = (bf16[9,256,256]{2,1,0:T(8,128)(2,1)}, bf16[9,256,256]{2,1,0:T(8,128)(2,1)}, u32[]{:S(2)}, u32[]{:S(2)}) collective-permute-start(bf16[9,256,256]{2,1,0:T(8,128)(2,1)} %bitcast.30), channel_id=1, source_target_pairs={{0,224},{16,240},{32,0},{48,16},{64,32},{80,48},{96,64},{112,80},{... | collective-permute-start | bytes 3538952 | tf_op jit(solution)/shard_map/ppermute | solution.py:192
  11.5 82.5 %copy-start.24 = (bf16[256,256]{1,0:T(8,128)(2,1)}, bf16[256,256]{1,0:T(8,128)(2,1)S(1)}, u32[]{:S(2)}) copy-start(bf16[256,256]{1,0:T(8,128)(2,1)S(1)} %get-tuple-element.71.refs_2_.top) | copy-start | bytes 393220
  11.5 82.5 %copy-start.26 = (bf16[256,256]{1,0:T(8,128)(2,1)}, bf16[256,256]{1,0:T(8,128)(2,1)S(1)}, u32[]{:S(2)}) copy-start(bf16[256,256]{1,0:T(8,128)(2,1)S(1)} %get-tuple-element.72.refs_4_.bot) | copy-start | bytes 393220
  11.5 80.6 %collective-permute-start = (bf16[256,256]{1,0:T(8,128)(2,1)S(1)}, bf16[256,256]{1,0:T(8,128)(2,1)S(1)}, u32[]{:S(2)}, u32[]{:S(2)}) collective-permute-start(bf16[256,256]{1,0:T(8,128)(2,1)S(1)} %get-tuple-element.72.refs_4_.bot), channel_id=1, source_target_pairs={{0,1},{1,2},{2,3},{3,4},{4,5},{5,6},{6,7},{7,8},{8,9},{9,10},{10,1... | collective-permute-start | bytes 393224 | tf_op jit(solution)/shard_map/ppermute | solution.py:196
  14.5 79.6 %collective-permute-start.1 = (bf16[256,256]{1,0:T(8,128)(2,1)S(1)}, bf16[256,256]{1,0:T(8,128)(2,1)S(1)}, u32[]{:S(2)}, u32[]{:S(2)}) collective-permute-start(bf16[256,256]{1,0:T(8,128)(2,1)S(1)} %get-tuple-element.71.refs_2_.top), channel_id=1, source_target_pairs={{1,0},{2,1},{3,2},{4,3},{5,4},{6,5},{7,6},{8,7},{9,8},{10,9},{11,1... | collective-permute-start | bytes 393224 | tf_op jit(solution)/shard_map/ppermute | solution.py:197
  20.1 1.5 copy-start.34
  21.7 75.0 %copy-start = (bf16[4,256,256]{2,1,0:T(8,128)(2,1)}, bf16[4,256,256]{2,1,0:T(8,128)(2,1)S(1)}, u32[]{:S(2)}) copy-start(bf16[4,256,256]{2,1,0:T(8,128)(2,1)S(1)} %get-tuple-element.67.refs_7_.saved) | copy-start | bytes 1572868
  21.7 75.0 %copy-start.10 = (bf16[2,256,256]{2,1,0:T(8,128)(2,1)}, bf16[2,256,256]{2,1,0:T(8,128)(2,1)S(1)}, u32[]{:S(2)}) copy-start(bf16[2,256,256]{2,1,0:T(8,128)(2,1)S(1)} %slice_bitcast_fusion.5.refs_3_.mid) | copy-start | bytes 786436
  92.1 4.6 %copy-start.29 = (bf16[256,256]{1,0:T(8,128)(2,1)}, bf16[256,256]{1,0:T(8,128)(2,1)S(1)}, u32[]{:S(2)}) copy-start(bf16[256,256]{1,0:T(8,128)(2,1)S(1)} %collective-permute-done.refs_1_.up) | copy-start | bytes 393220
  94.0 2.6 %copy-start.31 = (bf16[256,256]{1,0:T(8,128)(2,1)}, bf16[256,256]{1,0:T(8,128)(2,1)S(1)}, u32[]{:S(2)}) copy-start(bf16[256,256]{1,0:T(8,128)(2,1)S(1)} %collective-permute-done.1.refs_5_.down) | copy-start | bytes 393220
  94.0 6.0 %copy-start.33 = (bf16[2,4,256,256]{3,2,1,0:T(8,128)(2,1)S(1)}, bf16[2,4,256,256]{3,2,1,0:T(8,128)(2,1)}, u32[]{:S(2)}) copy-start(bf16[2,4,256,256]{3,2,1,0:T(8,128)(2,1)} %param.9) | copy-start | bytes 3145732
  96.7 15.9 %collective-permute-start.10 = (bf16[4,9,16,256]{3,2,1,0:T(8,128)(2,1)}, bf16[4,9,16,256]{3,2,1,0:T(8,128)(2,1)}, u32[]{:S(2)}, u32[]{:S(2)}) collective-permute-start(bf16[4,9,16,256]{3,2,1,0:T(8,128)(2,1)} %get-tuple-element.45), channel_id=1, source_target_pairs={{0,12},{1,13},{2,14},{3,15},{4,0},{5,1},{6,2},{7,3},{8,4},{9,5},{1... | collective-permute-start | bytes 884744 | tf_op jit(solution)/shard_map/ppermute | solution.py:188
  97.3 18.3 %collective-permute-start.8 = (bf16[4,9,16,256]{3,2,1,0:T(8,128)(2,1)}, bf16[4,9,16,256]{3,2,1,0:T(8,128)(2,1)}, u32[]{:S(2)}, u32[]{:S(2)}) collective-permute-start(bf16[4,9,16,256]{3,2,1,0:T(8,128)(2,1)} %get-tuple-element.43), channel_id=1, source_target_pairs={{0,8},{1,9},{2,10},{3,11},{4,12},{5,13},{6,14},{7,15},{8,0},{9,1},... | collective-permute-start | bytes 884744 | tf_op jit(solution)/shard_map/ppermute | solution.py:188
  99.7 21.5 %collective-permute-start.9 = (bf16[4,9,16,256]{3,2,1,0:T(8,128)(2,1)}, bf16[4,9,16,256]{3,2,1,0:T(8,128)(2,1)}, u32[]{:S(2)}, u32[]{:S(2)}) collective-permute-start(bf16[4,9,16,256]{3,2,1,0:T(8,128)(2,1)} %get-tuple-element.44), channel_id=1, source_target_pairs={{0,4},{1,5},{2,6},{3,7},{4,8},{5,9},{6,10},{7,11},{8,12},{9,13},{1... | collective-permute-start | bytes 884744 | tf_op jit(solution)/shard_map/ppermute | solution.py:188
  101.0 1.0 copy-start.1
  102.0 1.0 copy-start.2
  103.1 0.9 copy-start.11
  104.0 0.9 copy-start.25
  104.9 0.9 copy-start.27
  105.8 1.3 copy-start.28
  108.0 0.9 copy-start.32
  112.6 16.1 %copy-start.22 = (bf16[256,256]{1,0:T(8,128)(2,1)}, bf16[256,256]{1,0:T(8,128)(2,1)S(1)}, u32[]{:S(2)}) copy-start(bf16[256,256]{1,0:T(8,128)(2,1)S(1)} %get-tuple-element.35.refs_2_.top) | copy-start | bytes 393220
  112.6 10.1 %collective-permute-start.2 = (bf16[256,256]{1,0:T(8,128)(2,1)}, bf16[256,256]{1,0:T(8,128)(2,1)}, u32[]{:S(2)}, u32[]{:S(2)}) collective-permute-start(bf16[256,256]{1,0:T(8,128)(2,1)} %get-tuple-element.34.refs_4_.bot), channel_id=1, source_target_pairs={{0,1},{1,2},{2,3},{3,4},{4,5},{5,6},{6,7},{7,8},{8,9},{9,10},{10,1... | collective-permute-start | bytes 393224 | tf_op jit(solution)/shard_map/ppermute | solution.py:196
  115.6 8.6 %collective-permute-start.3 = (bf16[256,256]{1,0:T(8,128)(2,1)S(1)}, bf16[256,256]{1,0:T(8,128)(2,1)}, u32[]{:S(2)}, u32[]{:S(2)}) collective-permute-start(bf16[256,256]{1,0:T(8,128)(2,1)S(1)} %get-tuple-element.35.refs_2_.top), channel_id=1, source_target_pairs={{1,0},{2,1},{3,2},{4,3},{5,4},{6,5},{7,6},{8,7},{9,8},{10,9},{11,1... | collective-permute-start | bytes 393224 | tf_op jit(solution)/shard_map/ppermute | solution.py:197
  121.2 7.6 %copy-start.9 = (bf16[2,256,256]{2,1,0:T(8,128)(2,1)S(1)}, bf16[2,256,256]{2,1,0:T(8,128)(2,1)}, u32[]{:S(2)}) copy-start(bf16[2,256,256]{2,1,0:T(8,128)(2,1)} %copy-done.8) | copy-start | bytes 786436
  122.5 10.5 %copy-start.12 = (f32[9,16,256]{2,1,0:T(8,128)}, f32[9,16,256]{2,1,0:T(8,128)S(1)}, u32[]{:S(2)}) copy-start(f32[9,16,256]{2,1,0:T(8,128)S(1)} %get-tuple-element.46.own) | copy-start | bytes 442372
  122.6 16.2 %collective-permute-start.11 = (bf16[9,16,256]{2,1,0:T(8,128)(2,1)S(1)}, bf16[9,16,256]{2,1,0:T(8,128)(2,1)S(1)}, u32[]{:S(2)}, u32[]{:S(2)}) collective-permute-start(bf16[9,16,256]{2,1,0:T(8,128)(2,1)S(1)} %get-tuple-element.47), channel_id=1, source_target_pairs={{0,2},{1,3},{2,0},{3,1},{4,6},{5,7},{6,4},{7,5},{8,10},{9,11},{10,... | collective-permute-start | bytes 221192 | tf_op jit(solution)/shard_map/ppermute | solution.py:188
  122.7 17.2 %collective-permute-start.12 = (bf16[9,16,256]{2,1,0:T(8,128)(2,1)S(1)}, bf16[9,16,256]{2,1,0:T(8,128)(2,1)S(1)}, u32[]{:S(2)}, u32[]{:S(2)}) collective-permute-start(bf16[9,16,256]{2,1,0:T(8,128)(2,1)S(1)} %get-tuple-element.48), channel_id=1, source_target_pairs={{0,1},{1,2},{2,3},{3,0},{4,5},{5,6},{6,7},{7,4},{8,9},{9,10},{10,1... | collective-permute-start | bytes 221192 | tf_op jit(solution)/shard_map/ppermute | solution.py:188
  124.2 17.7 %collective-permute-start.13 = (bf16[9,16,256]{2,1,0:T(8,128)(2,1)S(1)}, bf16[9,16,256]{2,1,0:T(8,128)(2,1)S(1)}, u32[]{:S(2)}, u32[]{:S(2)}) collective-permute-start(bf16[9,16,256]{2,1,0:T(8,128)(2,1)S(1)} %get-tuple-element.49), channel_id=1, source_target_pairs={{0,3},{1,0},{2,1},{3,2},{4,7},{5,4},{6,5},{7,6},{8,11},{9,8},{10,9... | collective-permute-start | bytes 221192 | tf_op jit(solution)/shard_map/ppermute | solution.py:188
  128.8 0.9 copy-start.23
  133.1 5.7 %copy-start.5 = (bf16[2,256,256]{2,1,0:T(8,128)(2,1)}, bf16[2,256,256]{2,1,0:T(8,128)(2,1)S(1)}, u32[]{:S(2)}) copy-start(bf16[2,256,256]{2,1,0:T(8,128)(2,1)S(1)} %get-tuple-element.40.refs_2_.mid) | copy-start | bytes 786436
  133.1 5.7 %copy-start.15 = (bf16[256,256]{1,0:T(8,128)(2,1)}, bf16[256,256]{1,0:T(8,128)(2,1)S(1)}, u32[]{:S(2)}) copy-start(bf16[256,256]{1,0:T(8,128)(2,1)S(1)} %get-tuple-element.38.refs_3_.bot) | copy-start | bytes 393220
  133.1 12.0 %collective-permute-start.5 = (bf16[256,256]{1,0:T(8,128)(2,1)S(1)}, bf16[256,256]{1,0:T(8,128)(2,1)S(1)}, u32[]{:S(2)}, u32[]{:S(2)}) collective-permute-start(bf16[256,256]{1,0:T(8,128)(2,1)S(1)} %get-tuple-element.38.refs_3_.bot), channel_id=1, source_target_pairs={{0,1},{1,2},{2,3},{3,4},{4,5},{5,6},{6,7},{7,8},{8,9},{9,10},{10,1... | collective-permute-start | bytes 393224 | tf_op jit(solution)/shard_map/ppermute | solution.py:196
  138.8 13.6 %copy-start.35 = (bf16[9,16,256]{2,1,0:T(8,128)(2,1)}, bf16[9,16,256]{2,1,0:T(8,128)(2,1)S(1)}, u32[]{:S(2)}) copy-start(bf16[9,16,256]{2,1,0:T(8,128)(2,1)S(1)} %collective-permute-done.11.one) | copy-start | bytes 221188
  138.8 20.6 %collective-permute-start.15 = (bf16[4,9,16,256]{3,2,1,0:T(8,128)(2,1)S(1)}, bf16[4,9,16,256]{3,2,1,0:T(8,128)(2,1)S(1)}, u32[]{:S(2)}, u32[]{:S(2)}) collective-permute-start(bf16[4,9,16,256]{3,2,1,0:T(8,128)(2,1)S(1)} %get-tuple-element.51), channel_id=1, source_target_pairs={{0,8},{1,9},{2,10},{3,11},{4,12},{5,13},{6,14},{7,15},{8,0},{9,1},... | collective-permute-start | bytes 884744 | tf_op jit(solution)/shard_map/ppermute | solution.py:188
  139.9 2.0 %copy-start.36 = (bf16[9,16,256]{2,1,0:T(8,128)(2,1)}, bf16[9,16,256]{2,1,0:T(8,128)(2,1)S(1)}, u32[]{:S(2)}) copy-start(bf16[9,16,256]{2,1,0:T(8,128)(2,1)S(1)} %collective-permute-done.12.two) | copy-start | bytes 221188
  139.9 20.6 %collective-permute-start.16 = (bf16[4,9,16,256]{3,2,1,0:T(8,128)(2,1)}, bf16[4,9,16,256]{3,2,1,0:T(8,128)(2,1)S(1)}, u32[]{:S(2)}, u32[]{:S(2)}) collective-permute-start(bf16[4,9,16,256]{3,2,1,0:T(8,128)(2,1)} %get-tuple-element.52), channel_id=1, source_target_pairs={{0,4},{1,5},{2,6},{3,7},{4,8},{5,9},{6,10},{7,11},{8,12},{9,13},{1... | collective-permute-start | bytes 884744 | tf_op jit(solution)/shard_map/ppermute | solution.py:188
  142.5 18.1 %collective-permute-start.17 = (bf16[4,9,16,256]{3,2,1,0:T(8,128)(2,1)}, bf16[4,9,16,256]{3,2,1,0:T(8,128)(2,1)S(1)}, u32[]{:S(2)}, u32[]{:S(2)}) collective-permute-start(bf16[4,9,16,256]{3,2,1,0:T(8,128)(2,1)} %get-tuple-element.53), channel_id=1, source_target_pairs={{0,12},{1,13},{2,14},{3,15},{4,0},{5,1},{6,2},{7,3},{8,4},{9,5},{1... | collective-permute-start | bytes 884744 | tf_op jit(solution)/shard_map/ppermute | solution.py:188
  145.1 14.2 %copy-start.18 = (bf16[256,256]{1,0:T(8,128)(2,1)}, bf16[256,256]{1,0:T(8,128)(2,1)S(1)}, u32[]{:S(2)}) copy-start(bf16[256,256]{1,0:T(8,128)(2,1)S(1)} %collective-permute-done.5.refs_0_.up) | copy-start | bytes 393220
  145.1 9.7 %collective-permute-start.6 = (bf16[256,256]{1,0:T(8,128)(2,1)S(1)}, bf16[256,256]{1,0:T(8,128)(2,1)S(1)}, u32[]{:S(2)}, u32[]{:S(2)}) collective-permute-start(bf16[256,256]{1,0:T(8,128)(2,1)S(1)} %get-tuple-element.39.refs_1_.top), channel_id=1, source_target_pairs={{1,0},{2,1},{3,2},{4,3},{5,4},{6,5},{7,6},{8,7},{9,8},{10,9},{11,1... | collective-permute-start | bytes 393224 | tf_op jit(solution)/shard_map/ppermute | solution.py:197
  154.8 4.5 %copy-start.20 = (bf16[256,256]{1,0:T(8,128)(2,1)}, bf16[256,256]{1,0:T(8,128)(2,1)S(1)}, u32[]{:S(2)}) copy-start(bf16[256,256]{1,0:T(8,128)(2,1)S(1)} %collective-permute-done.6.refs_4_.down) | copy-start | bytes 393220
  154.8 10.2 %collective-permute-start.14 = (bf16[9,16,256]{2,1,0:T(8,128)(2,1)}, bf16[9,16,256]{2,1,0:T(8,128)(2,1)S(1)}, u32[]{:S(2)}, u32[]{:S(2)}) collective-permute-start(bf16[9,16,256]{2,1,0:T(8,128)(2,1)} %finish.3), channel_id=1, source_target_pairs={{0,240},{16,0},{32,16},{48,32},{64,48},{80,64},{96,80},{112,96},{1... | collective-permute-start | bytes 221192 | tf_op jit(solution)/shard_map/ppermute | solution.py:192
  154.8 1.0 copy-start.6
  159.3 24.6 %collective-permute-start.22 = (bf16[4,9,16,256]{3,2,1,0:T(8,128)(2,1)}, bf16[4,9,16,256]{3,2,1,0:T(8,128)(2,1)S(1)}, u32[]{:S(2)}, u32[]{:S(2)}) collective-permute-start(bf16[4,9,16,256]{3,2,1,0:T(8,128)(2,1)} %get-tuple-element.59), channel_id=1, source_target_pairs={{0,8},{1,9},{2,10},{3,11},{4,12},{5,13},{6,14},{7,15},{8,0},{9,1},... | collective-permute-start | bytes 884744 | tf_op jit(solution)/shard_map/ppermute | solution.py:188
  160.4 23.5 %collective-permute-start.23 = (bf16[4,9,16,256]{3,2,1,0:T(8,128)(2,1)}, bf16[4,9,16,256]{3,2,1,0:T(8,128)(2,1)S(1)}, u32[]{:S(2)}, u32[]{:S(2)}) collective-permute-start(bf16[4,9,16,256]{3,2,1,0:T(8,128)(2,1)} %get-tuple-element.60), channel_id=1, source_target_pairs={{0,4},{1,5},{2,6},{3,7},{4,8},{5,9},{6,10},{7,11},{8,12},{9,13},{1... | collective-permute-start | bytes 884744 | tf_op jit(solution)/shard_map/ppermute | solution.py:188
  161.3 22.6 %collective-permute-start.24 = (bf16[4,9,16,256]{3,2,1,0:T(8,128)(2,1)}, bf16[4,9,16,256]{3,2,1,0:T(8,128)(2,1)S(1)}, u32[]{:S(2)}, u32[]{:S(2)}) collective-permute-start(bf16[4,9,16,256]{3,2,1,0:T(8,128)(2,1)} %get-tuple-element.61), channel_id=1, source_target_pairs={{0,12},{1,13},{2,14},{3,15},{4,0},{5,1},{6,2},{7,3},{8,4},{9,5},{1... | collective-permute-start | bytes 884744 | tf_op jit(solution)/shard_map/ppermute | solution.py:188
  163.2 1.0 copy-start.4
  165.0 23.6 %copy-start.7 = (bf16[2,256,256]{2,1,0:T(8,128)(2,1)S(1)}, bf16[2,256,256]{2,1,0:T(8,128)(2,1)}, u32[]{:S(2)}) copy-start(bf16[2,256,256]{2,1,0:T(8,128)(2,1)} %copy-done.5) | copy-start | bytes 786436
  165.0 23.6 %copy-start.17 = (bf16[256,256]{1,0:T(8,128)(2,1)S(1)}, bf16[256,256]{1,0:T(8,128)(2,1)}, u32[]{:S(2)}) copy-start(bf16[256,256]{1,0:T(8,128)(2,1)} %copy-done.15) | copy-start | bytes 393220
  165.0 23.6 %copy-start.19 = (bf16[256,256]{1,0:T(8,128)(2,1)S(1)}, bf16[256,256]{1,0:T(8,128)(2,1)}, u32[]{:S(2)}) copy-start(bf16[256,256]{1,0:T(8,128)(2,1)} %copy-done.18) | copy-start | bytes 393220
  165.0 23.6 %copy-start.21 = (bf16[256,256]{1,0:T(8,128)(2,1)S(1)}, bf16[256,256]{1,0:T(8,128)(2,1)}, u32[]{:S(2)}) copy-start(bf16[256,256]{1,0:T(8,128)(2,1)} %copy-done.20) | copy-start | bytes 393220
  165.0 16.6 %copy-start.37 = (bf16[9,16,256]{2,1,0:T(8,128)(2,1)}, bf16[9,16,256]{2,1,0:T(8,128)(2,1)S(1)}, u32[]{:S(2)}) copy-start(bf16[9,16,256]{2,1,0:T(8,128)(2,1)S(1)} %collective-permute-done.14.held) | copy-start | bytes 221188
  165.0 5.4 %collective-permute-start.18 = (bf16[9,16,256]{2,1,0:T(8,128)(2,1)S(1)}, bf16[9,16,256]{2,1,0:T(8,128)(2,1)S(1)}, u32[]{:S(2)}, u32[]{:S(2)}) collective-permute-start(bf16[9,16,256]{2,1,0:T(8,128)(2,1)S(1)} %get-tuple-element.55), channel_id=1, source_target_pairs={{0,2},{1,3},{2,0},{3,1},{4,6},{5,7},{6,4},{7,5},{8,10},{9,11},{10,... | collective-permute-start | bytes 221192 | tf_op jit(solution)/shard_map/ppermute | solution.py:188
  170.4 11.2 %copy-start.43 = (bf16[9,16,256]{2,1,0:T(8,128)(2,1)}, bf16[9,16,256]{2,1,0:T(8,128)(2,1)S(1)}, u32[]{:S(2)}) copy-start(bf16[9,16,256]{2,1,0:T(8,128)(2,1)S(1)} %collective-permute-done.18.one) | copy-start | bytes 221188
  170.4 6.9 %collective-permute-start.19 = (bf16[9,16,256]{2,1,0:T(8,128)(2,1)S(1)}, bf16[9,16,256]{2,1,0:T(8,128)(2,1)S(1)}, u32[]{:S(2)}, u32[]{:S(2)}) collective-permute-start(bf16[9,16,256]{2,1,0:T(8,128)(2,1)S(1)} %get-tuple-element.56), channel_id=1, source_target_pairs={{0,1},{1,2},{2,3},{3,0},{4,5},{5,6},{6,7},{7,4},{8,9},{9,10},{10,1... | collective-permute-start | bytes 221192 | tf_op jit(solution)/shard_map/ppermute | solution.py:188
  177.2 4.4 %copy-start.44 = (bf16[9,16,256]{2,1,0:T(8,128)(2,1)}, bf16[9,16,256]{2,1,0:T(8,128)(2,1)S(1)}, u32[]{:S(2)}) copy-start(bf16[9,16,256]{2,1,0:T(8,128)(2,1)S(1)} %collective-permute-done.19.two) | copy-start | bytes 221188
  177.2 4.4 %collective-permute-start.20 = (bf16[9,16,256]{2,1,0:T(8,128)(2,1)S(1)}, bf16[9,16,256]{2,1,0:T(8,128)(2,1)S(1)}, u32[]{:S(2)}, u32[]{:S(2)}) collective-permute-start(bf16[9,16,256]{2,1,0:T(8,128)(2,1)S(1)} %get-tuple-element.57), channel_id=1, source_target_pairs={{0,3},{1,0},{2,1},{3,2},{4,7},{5,4},{6,5},{7,6},{8,11},{9,8},{10,9... | collective-permute-start | bytes 221192 | tf_op jit(solution)/shard_map/ppermute | solution.py:188
  183.9 8.3 %collective-permute-start.21 = (bf16[9,16,256]{2,1,0:T(8,128)(2,1)}, bf16[9,16,256]{2,1,0:T(8,128)(2,1)S(1)}, u32[]{:S(2)}, u32[]{:S(2)}) collective-permute-start(bf16[9,16,256]{2,1,0:T(8,128)(2,1)} %finish.4), channel_id=1, source_target_pairs={{0,240},{16,0},{32,16},{48,32},{64,48},{80,64},{96,80},{112,96},{1... | collective-permute-start | bytes 221192 | tf_op jit(solution)/shard_map/ppermute | solution.py:192
  184.1 8.1 %copy-start.13 = (f32[9,16,256]{2,1,0:T(8,128)}, f32[9,16,256]{2,1,0:T(8,128)S(1)}, u32[]{:S(2)}) copy-start(f32[9,16,256]{2,1,0:T(8,128)S(1)} %get-tuple-element.62.own) | copy-start | bytes 442372
  184.1 9.6 %collective-permute-start.25 = (bf16[9,16,256]{2,1,0:T(8,128)(2,1)S(1)}, bf16[9,16,256]{2,1,0:T(8,128)(2,1)S(1)}, u32[]{:S(2)}, u32[]{:S(2)}) collective-permute-start(bf16[9,16,256]{2,1,0:T(8,128)(2,1)S(1)} %get-tuple-element.63), channel_id=1, source_target_pairs={{0,2},{1,3},{2,0},{3,1},{4,6},{5,7},{6,4},{7,5},{8,10},{9,11},{10,... | collective-permute-start | bytes 221192 | tf_op jit(solution)/shard_map/ppermute | solution.py:188
  184.7 9.4 %collective-permute-start.26 = (bf16[9,16,256]{2,1,0:T(8,128)(2,1)S(1)}, bf16[9,16,256]{2,1,0:T(8,128)(2,1)S(1)}, u32[]{:S(2)}, u32[]{:S(2)}) collective-permute-start(bf16[9,16,256]{2,1,0:T(8,128)(2,1)S(1)} %get-tuple-element.64), channel_id=1, source_target_pairs={{0,1},{1,2},{2,3},{3,0},{4,5},{5,6},{6,7},{7,4},{8,9},{9,10},{10,1... | collective-permute-start | bytes 221192 | tf_op jit(solution)/shard_map/ppermute | solution.py:188
  188.5 6.0 %collective-permute-start.27 = (bf16[9,16,256]{2,1,0:T(8,128)(2,1)S(1)}, bf16[9,16,256]{2,1,0:T(8,128)(2,1)S(1)}, u32[]{:S(2)}, u32[]{:S(2)}) collective-permute-start(bf16[9,16,256]{2,1,0:T(8,128)(2,1)S(1)} %get-tuple-element.65), channel_id=1, source_target_pairs={{0,3},{1,0},{2,1},{3,2},{4,7},{5,4},{6,5},{7,6},{8,11},{9,8},{10,9... | collective-permute-start | bytes 221192 | tf_op jit(solution)/shard_map/ppermute | solution.py:188
  192.2 2.3 %copy-start.38 = (bf16[9,16,256]{2,1,0:T(8,128)(2,1)}, bf16[9,16,256]{2,1,0:T(8,128)(2,1)S(1)}, u32[]{:S(2)}) copy-start(bf16[9,16,256]{2,1,0:T(8,128)(2,1)S(1)} %collective-permute-done.21.held) | copy-start | bytes 221188
  (10 other events, 7.2 us)

commit v2 on v1

v2 whole, which is shorter than its diff:
```python
import functools

import jax
import jax.numpy as jnp
from jax import lax
from jax.experimental import pallas as pl
from jax.experimental.pallas import tpu as pltpu
from jax.sharding import PartitionSpec as P

TICKS = 3
BF = jnp.bfloat16
F32 = jnp.float32
VMEM_BYTES = 12 * 1024 * 1024
SMALL_VMEM_BYTES = 4 * 1024 * 1024


def whole(memory=pltpu.VMEM):
    return pl.BlockSpec(memory_space=memory)


def fill_shifted(shift_ref, rows):
    for index, row in enumerate(rows):
        wide = row.astype(F32)
        columns = wide.shape[1]
        place = lax.broadcasted_iota(jnp.int32, wide.shape, 1)
        ahead = pltpu.roll(wide, columns - 1, 1)
        behind = pltpu.roll(wide, 1, 1)
        shift_ref[0, index] = jnp.where(place == columns - 1, 0.0, ahead).astype(BF)
        shift_ref[1, index] = row
        shift_ref[2, index] = jnp.where(place == 0, 0.0, behind).astype(BF)


def back_kernel(tick, height, *refs):
    refs = list(refs)
    last = tick == TICKS - 1
    flag = None if last else refs.pop(0)
    spot = refs.pop(0) if tick > 0 else None
    up, top, mid, bot, down, kernel, saved = refs[:7]
    refs = refs[7:]
    if tick > 0:
        pieces = refs[:4]
        refs = refs[4:]
    fresh = None if last else refs.pop(0)
    if tick > 0:
        refs.pop(0)
    states = refs.pop(0)
    if not last:
        next_top, next_mid, next_bot = refs[:3]
        refs = refs[3:]
    if tick > 0:
        joined = refs.pop(0)
        part = pieces[0].shape[1]
        for k in range(4):
            start = pl.multiple_of(lax.rem(spot[0] + k, 4) * part, part)
            joined[:, pl.ds(start, part), :] = kernel[:, pl.ds(start, part), :] + pieces[k][...]
        kernel = joined
    shift_ref, turned, result, sem = refs
    channels = top.shape[0]
    rows = [up[...], top[...], *[mid[i] for i in range(height - 2)], bot[...], down[...]]
    fill_shifted(shift_ref, rows)
    for b in range(3):
        for j in range(3):
            turned[b, :, j * channels : (j + 1) * channels] = kernel[3 * (2 - j) + b].T
    for r in range(height):
        total = None
        for b in range(3):
            window = shift_ref[b, r : r + 3].reshape(3 * channels, -1)
            part = jnp.dot(turned[b], window, preferred_element_type=F32)
            total = part if total is None else total + part
        value = jnp.where(saved[r] > 0, total, 0.0).astype(BF)
        result[r] = value
        if not last:
            value = jnp.where(flag[0] > 0, fresh[r], value)
            if r == 0:
                next_top[...] = value
            elif r == height - 1:
                next_bot[...] = value
            else:
                next_mid[r - 1] = value
    copy = pltpu.make_async_copy(result, states.at[tick, 0], sem)
    copy.start()
    copy.wait()


def back_project(tick, edges, kernel, pieces, saved, states, restart, fresh, spot):
    last = tick == TICKS - 1
    height, channels, columns = saved.shape
    args, specs = [], []

    def give(value, memory=pltpu.VMEM):
        args.append(value)
        specs.append(whole(memory))

    if not last:
        give(restart, pltpu.SMEM)
    if tick > 0:
        give(spot, pltpu.SMEM)
    for value in (*edges, kernel, saved):
        give(value)
    if tick > 0:
        for value in pieces:
            give(value)
    if not last:
        give(fresh)
    alias = {}
    if tick > 0:
        alias = {len(args): 0}
        give(states, pl.ANY)
    shapes = [jax.ShapeDtypeStruct((TICKS, 1, height, channels, columns), BF)]
    scratch = [
        pltpu.VMEM((3, height + 2, channels, columns), BF),
        pltpu.VMEM((3, channels, 3 * channels), BF),
        pltpu.VMEM((height, channels, columns), BF),
        pltpu.SemaphoreType.DMA,
    ]
    if not last:
        shapes += [
            jax.ShapeDtypeStruct((channels, columns), BF),
            jax.ShapeDtypeStruct((height - 2, channels, columns), BF),
            jax.ShapeDtypeStruct((channels, columns), BF),
        ]
        if tick > 0:
            shapes.append(jax.ShapeDtypeStruct(kernel.shape, BF))
    else:
        scratch = [pltpu.VMEM(kernel.shape, BF)] + scratch
    return pl.pallas_call(
        functools.partial(back_kernel, tick, height),
        out_shape=shapes,
        in_specs=specs,
        out_specs=[whole(pl.ANY)] + [whole()] * (len(shapes) - 1),
        scratch_shapes=scratch,
        input_output_aliases=alias,
        compiler_params=pltpu.CompilerParams(vmem_limit_bytes=VMEM_BYTES),
        cost_estimate=pl.CostEstimate(
            flops=18 * height * channels * channels * columns, bytes_accessed=4 << 20, transcendentals=0
        ),
        name="back",
    )(*args)


def weight_kernel(tick, height, scale, *refs):
    refs = list(refs)
    spot = refs.pop(0) if tick > 0 else None
    even = refs.pop(0) if tick == 1 else None
    up, top, mid, bot, down, saved = refs[:6]
    refs = refs[6:]
    other = refs.pop(0) if tick > 0 else None
    shift_ref = refs.pop()
    channels = top.shape[0]
    rows = [up[...], top[...], *[mid[i] for i in range(height - 2)], bot[...], down[...]]
    fill_shifted(shift_ref, rows)
    inputs = [jnp.maximum(saved[r], 0) for r in range(height)]
    part = channels // 4
    piece = part // 4
    for k in range(4):
        place = lax.rem(spot[0] + k, 4) if tick > 0 else k
        start = pl.multiple_of(place * part, part) if tick > 0 else k * part
        total = None
        for r in range(height):
            left = shift_ref[:, r : r + 3, pl.ds(start, part), :].reshape(9 * part, -1)
            term = lax.dot_general(left, inputs[r], (((1,), (1,)), ((), ())), preferred_element_type=F32)
            total = term if total is None else total + term
        total = total * scale
        for b in range(3):
            for j in range(3):
                base = (3 * b + j) * part
                tap = 3 * (2 - j) + b
                for q in range(4):
                    value = total[base + q * piece : base + (q + 1) * piece]
                    if tick == 0:
                        refs[0][k, q, tap] = value.astype(BF)
                        continue
                    out = refs[k]
                    if tick == 1:
                        refs[4][place, q, tap] = value.astype(BF)
                        value = jnp.where(even[0] > 0, value, 0.0)
                    out[q, tap] = (value + other[place, q, tap].astype(F32)).astype(out.dtype)


def weight_terms(tick, edges, saved, scale, spot=None, even=None, other=None):
    height, channels, columns = saved.shape
    part = (4, 9, channels // 16, channels)
    full = jax.ShapeDtypeStruct((4, *part), BF)
    shapes = [jax.ShapeDtypeStruct(part, F32)] + [jax.ShapeDtypeStruct(part, BF)] * 3
    scalars = [[], [spot, even], [spot]][tick]
    rest = [*edges, saved] + ([other] if tick > 0 else [])
    return pl.pallas_call(
        functools.partial(weight_kernel, tick, height, scale),
        out_shape=[[full], shapes + [full], shapes][tick],
        in_specs=[whole(pltpu.SMEM)] * len(scalars) + [whole()] * len(rest),
        out_specs=[whole()] * (1, 5, 4)[tick],
        scratch_shapes=[pltpu.VMEM((3, height + 2, channels, columns), BF)],
        compiler_params=pltpu.CompilerParams(vmem_limit_bytes=VMEM_BYTES),
        cost_estimate=pl.CostEstimate(
            flops=18 * height * channels * channels * columns, bytes_accessed=4 << 20, transcendentals=0
        ),
        name="weight",
    )(*scalars, *rest)


def regroup_kernel(spot, own, one, two, three, mine, first, second, third):
    for k, out in enumerate((mine, first, second, third)):
        place = lax.rem(spot[0] + k, 4)
        value = (own[place] + one[place].astype(F32)) + (two[place].astype(F32) + three[place].astype(F32))
        out[...] = value.astype(out.dtype)


def regroup(spot, parts):
    shape = parts[0].shape[1:]
    return pl.pallas_call(
        regroup_kernel,
        out_shape=[jax.ShapeDtypeStruct(shape, F32)] + [jax.ShapeDtypeStruct(shape, BF)] * 3,
        in_specs=[whole(pltpu.SMEM)] + [whole()] * 4,
        out_specs=[whole()] * 4,
        compiler_params=pltpu.CompilerParams(vmem_limit_bytes=SMALL_VMEM_BYTES),
        name="regroup",
    )(spot, *parts)


def total_of(own, one, two, three):
    return (own[...] + one[...].astype(F32)) + (two[...].astype(F32) + three[...].astype(F32))


def collect_kernel(own, one, two, three, out):
    out[...] = total_of(own, one, two, three).astype(BF)


def finish_kernel(held, early, own, one, two, three, out):
    out[...] = (held[...].astype(F32) + early[...].astype(F32) + total_of(own, one, two, three)).astype(BF)


def finish(parts, *before):
    return pl.pallas_call(
        finish_kernel if before else collect_kernel,
        out_shape=jax.ShapeDtypeStruct(parts[0].shape, BF),
        in_specs=[whole()] * (4 + len(before)),
        out_specs=whole(),
        compiler_params=pltpu.CompilerParams(vmem_limit_bytes=SMALL_VMEM_BYTES),
        name="finish",
    )(*before, *parts)


def along(value, move):
    return lax.ppermute(value, "rows", [(x * 4 + z, move(x, z)) for x in range(4) for z in range(4)])


def along_odd(value, move):
    pairs = [(b * 16 + x * 4 + z, b * 16 + move(x, z)) for b in range(1, 16, 2) for x in range(4) for z in range(4)]
    return lax.ppermute(value, ("blk", "rows"), pairs)


def around(value, pairs):
    return lax.ppermute(value, "blk", pairs)


def with_edges(top, mid, bot):
    up = lax.ppermute(bot, "rows", [(i, i + 1) for i in range(15)])
    down = lax.ppermute(top, "rows", [(i + 1, i) for i in range(15)])
    return up, top, mid, bot, down


def gathered(own):
    return [own] + [along_odd(own, lambda x, z, k=k: ((x - k) % 4) * 4 + z) for k in (1, 2, 3)]


def reduce_rows(parts, spot_z):
    moved = [parts[0]] + [along(parts[k], lambda x, z, k=k: ((x + k) % 4) * 4 + z) for k in (1, 2, 3)]
    pieces = regroup(spot_z, moved)
    return [pieces[0]] + [along(pieces[k], lambda x, z, k=k: x * 4 + (z + k) % 4) for k in (1, 2, 3)]


def shards(section_weights, grad_acc, saved_inputs, cotangent, fresh_grads):
    position = lax.axis_index("blk")
    row = lax.axis_index("rows")
    spot_x = (row // 4).reshape(1)
    spot_z = (row % 4).reshape(1)
    even = (position % 2 == 0).astype(jnp.int32).reshape(1)
    kernel = jnp.transpose(section_weights[0], (1, 0, 2))
    held = jnp.transpose(grad_acc[0], (1, 0, 2))
    height = cotangent.shape[1]
    channels = cotangent.shape[2]
    columns = cotangent.shape[3]
    scale = float(16 * height * columns) ** (-0.5)
    evens = range(0, 16, 2)
    down_core = [(b + 1, b) for b in evens]
    image = cotangent[0]
    edges = with_edges(image[0], image[1 : height - 1], image[height - 1])
    quarter = lax.dynamic_slice_in_dim(kernel, spot_x[0] * (channels // 4), channels // 4, 1)
    pieces_one = gathered(around(quarter, [(b, (b - 1) % 16) for b in evens]))
    kernel_one = around(kernel, down_core)

    def back(tick, edges, kernel, pieces, states):
        restart = (position == 16 - tick - 1).astype(jnp.int32).reshape(1)
        fresh = fresh_grads[tick] if tick + 1 < TICKS else None
        return back_project(tick, edges, kernel, pieces, saved_inputs[tick, 0], states, restart, fresh, spot_x)

    states, *parts = back(0, edges, kernel, None, None)
    edges_one = with_edges(*parts)
    (sums,) = weight_terms(0, edges, saved_inputs[0, 0], scale)
    other = around(sums, [(b, b ^ 1) for b in range(16)])
    states, *parts, used = back(1, edges_one, kernel_one, pieces_one, states)
    edges_two = with_edges(*parts)
    *parts, sums = weight_terms(1, edges_one, saved_inputs[1, 0], scale, spot_x, even, other)
    other = around(sums, down_core)
    early = finish(reduce_rows(parts, spot_z))
    held = around(held, [(b, (b - 2) % 16) for b in range(16)])
    early = around(early, [(b, (b - 1) % 16) for b in evens] + [(b + 1, (b - 2) % 16) for b in evens])
    parts = weight_terms(2, edges_two, saved_inputs[2, 0], scale, spot_x, even, other)
    pieces_two = gathered(around(quarter, [(b + 1, (b - 1) % 16) for b in evens]))
    kernel_two = around(used, down_core)
    (states,) = back(2, edges_two, kernel_two, pieces_two, states)
    held = finish(reduce_rows(parts, spot_z), held, early)
    return states, jnp.transpose(held, (1, 0, 2))[None]


def solution(mesh):
    return jax.shard_map(
        shards,
        mesh=mesh,
        in_specs=(
            P("blk", None, None, None),
            P("blk", "rows", None, None),
            P(None, "blk", "rows", None, None),
            P("blk", "rows", None, None),
            P(None, "rows", None, None),
        ),
        out_specs=(P(None, "blk", "rows", None, None), P("blk", "rows", None, None)),
        check_vma=False,
    )
```

time: 201 us -> 173 us (0.86); the launches traced: 197 us -> 171 us
  waiting for transfers between devices: 88.2 us -> 34.9 us
  starting transfers between devices: 62.9 us -> 87.7 us
  local copies, waits for them, and re-layouts: 19.1 us -> 21.2 us
    ppermute x3, waiting for transfers between devices: 70.5 us -> 8.25 us  [with_edges(): up = lax.ppermute(bot, 'rows', [(i, i + 1) for i in range(15)])]
    ppermute x4 -> x14, starting transfers between devices: 9.9 us -> 52.5 us  [the longest x8 46.3 us: around(): return lax.ppermute(value, 'blk', pairs)]
    ppermute x18 -> x12, starting transfers between devices: 26.6 us -> 14.2 us  [along(): lax.ppermute(value, 'rows', [(x * 4 + z, move(x, z)) for x in range(4) fo...]
    ppermute x3, waiting for transfers between devices: 3.24 us -> 11.1 us  [with_edges(): down = lax.ppermute(top, 'rows', [(i + 1, i) for i in range(15)])]
    ppermute x3, starting transfers between devices: 18.4 us -> 12.8 us  [with_edges(): down = lax.ppermute(top, 'rows', [(i + 1, i) for i in range(15)])]
    ppermute x4 -> x14, waiting for transfers between devices: 0.01 us -> 5.46 us  [the longest x8 5.44 us: around(): return lax.ppermute(value, 'blk', pairs)]
    ppermute x18 -> x12, waiting for transfers between devices: 14.5 us -> 10.1 us  [along(): lax.ppermute(value, 'rows', [(x * 4 + z, move(x, z)) for x in range(4) fo...]
    unnamed x92 -> x76, local copies, waits for them, and re-layouts: 15.7 us -> 16.2 us
  transfers between devices with their start and end apart: 28 -> 32, of which waited for: 10 -> 11; matrix products, arithmetic and copies ran while one was open for 2% -> 2% of each run, Pallas kernels for 12% -> 14%
where the time goes in v2:
time: 173 us; the launch traced here: 171 us
  starting transfers between devices  87.7 us (51%)
  waiting for transfers between devices  34.9 us (20%)
  Pallas kernels  26.4 us (15%)
  local copies, waits for them, and re-layouts  21.2 us (12%)
    ppermute x8, starting transfers between devices, around(): return lax.ppermute(value, 'blk', pairs)  46.3 us
    unnamed x76, local copies, waits for them, and re-layouts  16.2 us
    ppermute x12, starting transfers between devices, along(): lax.ppermute(value, 'rows', [(x * 4 + z, move(x, z)) for x in range(4) fo...  14.2 us
    ppermute x3, starting transfers between devices, with_edges(): down = lax.ppermute(top, 'rows', [(i + 1, i) for i in range(15)])  12.8 us
    pallas_call x3, Pallas kernels, back_project(): pl.pallas_call(functools.partial(back_kernel, tick, height), out_shape=sh...  12.8 us
    ppermute x3, waiting for transfers between devices, with_edges(): down = lax.ppermute(top, 'rows', [(i + 1, i) for i in range(15)])  11.1 us
    pallas_call x3, Pallas kernels, weight_terms(): pl.pallas_call(functools.partial(weight_kernel, tick, height, scale), out...  10.6 us
    ppermute x12, waiting for transfers between devices, along(): lax.ppermute(value, 'rows', [(x * 4 + z, move(x, z)) for x in range(4) fo...  10.1 us
  transfers between devices with their start and end apart: 32, of which 11 were waited for; matrix products, arithmetic and copies ran while one was open for 2% of the time, Pallas kernels for 14%

profile of v2, /device:TPU:2, one launch (start us, length us, event | category | flops | bytes accessed | tf_op | source)
XLA Modules:
  0.0 171.3 jit_solution(9531507466065542549)
XLA Ops:
  0.6 1.0 slice_bitcast_fusion.6
  1.6 3.8 %collective-permute-start = (bf16[256,256]{1,0:T(8,128)(2,1)S(1)}, bf16[256,256]{1,0:T(8,128)(2,1)S(1)}, u32[]{:S(2)}, u32[]{:S(2)}) collective-permute-start(bf16[256,256]{1,0:T(8,128)(2,1)S(1)} %get-tuple-element.60.refs_4_.refs_3_), channel_id=1, source_target_pairs={{0,1},{1,2},{2,3},{3,4},{4,5},{5,6},{6,7},{7,8},{8,9},{9,10},{10,1... | collective-permute-start | bytes 393224 | tf_op jit(solution)/shard_map/ppermute | solution.py:257
  5.5 4.8 %collective-permute-start.1 = (bf16[256,256]{1,0:T(8,128)(2,1)S(1)}, bf16[256,256]{1,0:T(8,128)(2,1)S(1)}, u32[]{:S(2)}, u32[]{:S(2)}) collective-permute-start(bf16[256,256]{1,0:T(8,128)(2,1)S(1)} %get-tuple-element.59.refs_2_.refs_1_), channel_id=1, source_target_pairs={{1,0},{2,1},{3,2},{4,3},{5,4},{6,5},{7,6},{8,7},{9,8},{10,9},{11,1... | collective-permute-start | bytes 393224 | tf_op jit(solution)/shard_map/ppermute | solution.py:258
  10.3 1.5 slice_bitcast_fusion
  11.9 2.6 %collective-permute-done.1.refs_5_.refs_4_ = bf16[256,256]{1,0:T(8,128)(2,1)S(1)} collective-permute-done((bf16[256,256]{1,0:T(8,128)(2,1)S(1)}, bf16[256,256]{1,0:T(8,128)(2,1)S(1)}, u32[]{:S(2)}, u32[]{:S(2)}) %collective-permute-start.1) | collective-permute-done | bytes 131104 | tf_op jit(solution)/shard_map/ppermute | solution.py:258
  14.5 2.5 %weight.3 = bf16[4,4,9,16,256]{4,3,2,1,0:T(8,128)(2,1)} custom-call(bf16[256,256]{1,0:T(8,128)(2,1)S(1)} %collective-permute-done.refs_1_.refs_0_, bf16[256,256]{1,0:T(8,128)(2,1)S(1)} %get-tuple-element.59.refs_2_.refs_1_, bf16[2,256,256]{2,1,0:T(8,128)(2,1)S(1)} %slice_bitcast_fusion.5.refs_3_.refs_2_, ...), custom_call_target="tpu_custom_call" | custom-call | flops 1207959552 | bytes 4194304 | tf_op jit(solution)/shard_map/weight/pallas_call | solution.py:187
  17.0 1.3 collective-permute-start.4
  18.3 0.9 slice_bitcast_fusion.1
  19.1 1.0 copy-done
  20.2 0.9 copy-done.22
  21.1 0.9 copy-done.24
  22.0 0.9 copy-done.32
  22.9 0.9 copy-done.34
  23.8 4.4 %back.3 = (bf16[3,1,4,256,256]{4,3,2,1,0:T(8,128)(2,1)}, bf16[256,256]{1,0:T(8,128)(2,1)}, bf16[2,256,256]{2,1,0:T(8,128)(2,1)S(1)}, bf16[256,256]{1,0:T(8,128)(2,1)}) custom-call(s32[1]{0:T(128)} %bitcast.2.refs_0_, bf16[256,256]{1,0:T(8,128)(2,1)S(1)} %copy-done.32, bf16[256,256]{1,0:T(8,128)(2,1)S(1)} %copy-done.22, ...), custom_call_target="tpu_custom_call" | custom-call | flops 1207959552 | bytes 4194304 | tf_op jit(solution)/shard_map/back/pallas_call | solution.py:126
  28.9 2.4 %collective-permute-start.2 = (bf16[256,256]{1,0:T(8,128)(2,1)}, bf16[256,256]{1,0:T(8,128)(2,1)S(1)}, u32[]{:S(2)}, u32[]{:S(2)}) collective-permute-start(bf16[256,256]{1,0:T(8,128)(2,1)} %get-tuple-element.28.refs_5_), channel_id=1, source_target_pairs={{0,1},{1,2},{2,3},{3,4},{4,5},{5,6},{6,7},{7,8},{8,9},{9,10},{10,1... | collective-permute-start | bytes 393224 | tf_op jit(solution)/shard_map/ppermute | solution.py:257
  31.3 6.1 %collective-permute-start.3 = (bf16[256,256]{1,0:T(8,128)(2,1)}, bf16[256,256]{1,0:T(8,128)(2,1)S(1)}, u32[]{:S(2)}, u32[]{:S(2)}) collective-permute-start(bf16[256,256]{1,0:T(8,128)(2,1)} %get-tuple-element.29.refs_3_), channel_id=1, source_target_pairs={{1,0},{2,1},{3,2},{4,3},{5,4},{6,5},{7,6},{8,7},{9,8},{10,9},{11,1... | collective-permute-start | bytes 393224 | tf_op jit(solution)/shard_map/ppermute | solution.py:258
  37.4 2.5 %collective-permute-done.2.refs_2_ = bf16[256,256]{1,0:T(8,128)(2,1)S(1)} collective-permute-done((bf16[256,256]{1,0:T(8,128)(2,1)}, bf16[256,256]{1,0:T(8,128)(2,1)S(1)}, u32[]{:S(2)}, u32[]{:S(2)}) %collective-permute-start.2) | collective-permute-done | bytes 131104 | tf_op jit(solution)/shard_map/ppermute | solution.py:257
  40.0 2.6 %collective-permute-done.3.refs_6_ = bf16[256,256]{1,0:T(8,128)(2,1)S(1)} collective-permute-done((bf16[256,256]{1,0:T(8,128)(2,1)}, bf16[256,256]{1,0:T(8,128)(2,1)S(1)}, u32[]{:S(2)}, u32[]{:S(2)}) %collective-permute-start.3) | collective-permute-done | bytes 131104 | tf_op jit(solution)/shard_map/ppermute | solution.py:258
  43.2 0.9 copy-done.8
  44.2 0.9 copy-done.19
  45.1 4.4 %weight.4 = (f32[4,9,16,256]{3,2,1,0:T(8,128)S(1)}, bf16[4,9,16,256]{3,2,1,0:T(8,128)(2,1)S(1)}, bf16[4,9,16,256]{3,2,1,0:T(8,128)(2,1)S(1)}, bf16[4,9,16,256]{3,2,1,0:T(8,128)(2,1)}, bf16[4,4,9,16,256]{4,3,2,1,0:T(8,128)(2,1)}) custom-call(s32[1]{0:T(128)} %bitcast.refs_1_.refs_0_, s32[1]{0:T(128)} %bitcast.20.refs_1_, ...), custom_call_target="tpu_custom_call" | custom-call | flops 1207959552 | bytes 4194304 | tf_op jit(solution)/shard_map/weight/pallas_call | solution.py:187
  49.5 0.7 copy-done.25
  50.2 0.7 copy-done.27
  50.9 1.3 collective-permute-start.25
  52.2 1.7 dynamic-slice_bitcast_fusion
  53.9 13.8 %collective-permute-start.5 = (bf16[9,64,256]{2,1,0:T(8,128)(2,1)}, bf16[9,64,256]{2,1,0:T(8,128)(2,1)}, u32[]{:S(2)}, u32[]{:S(2)}) collective-permute-start(bf16[9,64,256]{2,1,0:T(8,128)(2,1)} %dynamic-slice_bitcast_fusion), channel_id=1, source_target_pairs={{0,240},{32,16},{64,48},{96,80},{128,112},{160,144},{192,176},{224... | collective-permute-start | bytes 884744 | tf_op jit(solution)/shard_map/ppermute | solution.py:253
  67.7 5.4 %collective-permute-done.5.refs_9_ = bf16[9,64,256]{2,1,0:T(8,128)(2,1)} collective-permute-done((bf16[9,64,256]{2,1,0:T(8,128)(2,1)}, bf16[9,64,256]{2,1,0:T(8,128)(2,1)}, u32[]{:S(2)}, u32[]{:S(2)}) %collective-permute-start.5) | collective-permute-done | bytes 294944 | tf_op jit(solution)/shard_map/ppermute | solution.py:253
  73.1 1.4 collective-permute-start.6
  74.5 1.4 collective-permute-start.7
  75.9 1.4 collective-permute-start.8
  77.3 0.9 copy-done.9
  78.2 0.9 copy-done.17
  79.1 0.9 copy-done.20
  80.0 4.9 %back.4 = (bf16[3,1,4,256,256]{4,3,2,1,0:T(8,128)(2,1)}, bf16[256,256]{1,0:T(8,128)(2,1)S(1)}, bf16[2,256,256]{2,1,0:T(8,128)(2,1)S(1)}, bf16[256,256]{1,0:T(8,128)(2,1)S(1)}, bf16[9,256,256]{2,1,0:T(8,128)(2,1)}) custom-call(s32[1]{0:T(128)} %bitcast.1.refs_0_, s32[1]{0:T(128)} %bitcast.refs_1_.refs_0_, ...), custom_call_target="tpu_custom_call", output_to_operand_aliasing={{0}: (14, {})} | custom-call | flops 1207959552 | bytes 4194304 | tf_op jit(solution)/shard_map/back/pallas_call | solution.py:126
  85.0 1.3 collective-permute-start.11
  86.3 1.9 %collective-permute-start.9 = (bf16[256,256]{1,0:T(8,128)(2,1)S(1)}, bf16[256,256]{1,0:T(8,128)(2,1)S(1)}, u32[]{:S(2)}, u32[]{:S(2)}) collective-permute-start(bf16[256,256]{1,0:T(8,128)(2,1)S(1)} %get-tuple-element.32.refs_4_), channel_id=1, source_target_pairs={{0,1},{1,2},{2,3},{3,4},{4,5},{5,6},{6,7},{7,8},{8,9},{9,10},{10,1... | collective-permute-start | bytes 393224 | tf_op jit(solution)/shard_map/ppermute | solution.py:257
  88.2 1.3 collective-permute-start.18
  89.5 0.7 collective-permute-start.19
  90.3 5.7 %collective-permute-done.9.refs_1_ = bf16[256,256]{1,0:T(8,128)(2,1)S(1)} collective-permute-done((bf16[256,256]{1,0:T(8,128)(2,1)S(1)}, bf16[256,256]{1,0:T(8,128)(2,1)S(1)}, u32[]{:S(2)}, u32[]{:S(2)}) %collective-permute-start.9) | collective-permute-done | bytes 131104 | tf_op jit(solution)/shard_map/ppermute | solution.py:257
  96.0 1.9 %collective-permute-start.10 = (bf16[256,256]{1,0:T(8,128)(2,1)S(1)}, bf16[256,256]{1,0:T(8,128)(2,1)S(1)}, u32[]{:S(2)}, u32[]{:S(2)}) collective-permute-start(bf16[256,256]{1,0:T(8,128)(2,1)S(1)} %get-tuple-element.33.refs_2_), channel_id=1, source_target_pairs={{1,0},{2,1},{3,2},{4,3},{5,4},{6,5},{7,6},{8,7},{9,8},{10,9},{11,1... | collective-permute-start | bytes 393224 | tf_op jit(solution)/shard_map/ppermute | solution.py:258
  97.9 5.9 %collective-permute-done.10.refs_5_ = bf16[256,256]{1,0:T(8,128)(2,1)S(1)} collective-permute-done((bf16[256,256]{1,0:T(8,128)(2,1)S(1)}, bf16[256,256]{1,0:T(8,128)(2,1)S(1)}, u32[]{:S(2)}, u32[]{:S(2)}) %collective-permute-start.10) | collective-permute-done | bytes 131104 | tf_op jit(solution)/shard_map/ppermute | solution.py:258
  103.8 1.4 collective-permute-start.12
  105.2 3.8 %weight.5 = (f32[4,9,16,256]{3,2,1,0:T(8,128)S(1)}, bf16[4,9,16,256]{3,2,1,0:T(8,128)(2,1)}, bf16[4,9,16,256]{3,2,1,0:T(8,128)(2,1)}, bf16[4,9,16,256]{3,2,1,0:T(8,128)(2,1)S(1)}) custom-call(s32[1]{0:T(128)} %bitcast.refs_1_.refs_0_, bf16[256,256]{1,0:T(8,128)(2,1)S(1)} %collective-permute-done.9.refs_1_, bf16[256,256]{1,0:T(8,128)(2,1)S(1)} %get-tuple-element.33.refs_2_, ...), custom_call_target="tpu_custom_call" | custom-call | flops 1207959552 | bytes 4194304 | tf_op jit(solution)/shard_map/weight/pallas_call | solution.py:187
  109.1 0.7 copy-done.29
  109.8 0.7 copy-done.1
  110.5 2.0 %collective-permute-start.26 = (bf16[4,9,16,256]{3,2,1,0:T(8,128)(2,1)}, bf16[4,9,16,256]{3,2,1,0:T(8,128)(2,1)S(1)}, u32[]{:S(2)}, u32[]{:S(2)}) collective-permute-start(bf16[4,9,16,256]{3,2,1,0:T(8,128)(2,1)} %get-tuple-element.47), channel_id=1, source_target_pairs={{0,4},{1,5},{2,6},{3,7},{4,8},{5,9},{6,10},{7,11},{8,12},{9,13},{1... | collective-permute-start | bytes 884744 | tf_op jit(solution)/shard_map/ppermute | solution.py:244
  112.5 0.7 copy-done.3
  113.2 1.3 collective-permute-start.27
  114.5 1.0 copy-done.2
  115.5 1.0 copy-done.4
  116.5 1.2 regroup.2
  117.8 2.1 %collective-permute-start.22 = (bf16[9,16,256]{2,1,0:T(8,128)(2,1)S(1)}, bf16[9,16,256]{2,1,0:T(8,128)(2,1)S(1)}, u32[]{:S(2)}, u32[]{:S(2)}) collective-permute-start(bf16[9,16,256]{2,1,0:T(8,128)(2,1)S(1)} %get-tuple-element.43), channel_id=1, source_target_pairs={{0,2},{1,3},{2,0},{3,1},{4,6},{5,7},{6,4},{7,5},{8,10},{9,11},{10,... | collective-permute-start | bytes 221192 | tf_op jit(solution)/shard_map/ppermute | solution.py:244
  119.9 4.0 %collective-permute-done.21.one = bf16[9,16,256]{2,1,0:T(8,128)(2,1)S(1)} collective-permute-done((bf16[9,16,256]{2,1,0:T(8,128)(2,1)S(1)}, bf16[9,16,256]{2,1,0:T(8,128)(2,1)S(1)}, u32[]{:S(2)}, u32[]{:S(2)}) %collective-permute-start.21) | collective-permute-done | bytes 73760 | tf_op jit(solution)/shard_map/ppermute | solution.py:244
  123.9 2.7 %collective-permute-start.28 = (bf16[4,9,16,256]{3,2,1,0:T(8,128)(2,1)S(1)}, bf16[4,9,16,256]{3,2,1,0:T(8,128)(2,1)S(1)}, u32[]{:S(2)}, u32[]{:S(2)}) collective-permute-start(bf16[4,9,16,256]{3,2,1,0:T(8,128)(2,1)S(1)} %copy-done.30), channel_id=1, source_target_pairs={{0,12},{1,13},{2,14},{3,15},{4,0},{5,1},{6,2},{7,3},{8,4},{9,5},{1... | collective-permute-start | bytes 884744 | tf_op jit(solution)/shard_map/ppermute | solution.py:244
  126.6 1.6 collective-permute-done.23.three
  130.9 1.7 collective-permute-start.16
  132.6 1.1 regroup.3
  133.7 25.6 %collective-permute-start.24 = (bf16[9,16,256]{2,1,0:T(8,128)(2,1)S(1)}, bf16[9,16,256]{2,1,0:T(8,128)(2,1)S(1)}, u32[]{:S(2)}, u32[]{:S(2)}) collective-permute-start(bf16[9,16,256]{2,1,0:T(8,128)(2,1)S(1)} %finish.2), channel_id=1, source_target_pairs={{0,240},{32,16},{64,48},{96,80},{128,112},{160,144},{192,176},{224... | collective-permute-start | bytes 221192 | tf_op jit(solution)/shard_map/ppermute | solution.py:253
  159.2 2.9 %collective-permute-start.30 = (bf16[9,16,256]{2,1,0:T(8,128)(2,1)S(1)}, bf16[9,16,256]{2,1,0:T(8,128)(2,1)S(1)}, u32[]{:S(2)}, u32[]{:S(2)}) collective-permute-start(bf16[9,16,256]{2,1,0:T(8,128)(2,1)S(1)} %get-tuple-element.52), channel_id=1, source_target_pairs={{0,2},{1,3},{2,0},{3,1},{4,6},{5,7},{6,4},{7,5},{8,10},{9,11},{10,... | collective-permute-start | bytes 221192 | tf_op jit(solution)/shard_map/ppermute | solution.py:244
  162.1 1.0 collective-permute-start.31
  163.2 3.5 %back.5 = bf16[3,1,4,256,256]{4,3,2,1,0:T(8,128)(2,1)} custom-call(s32[1]{0:T(128)} %bitcast.refs_1_.refs_0_, bf16[256,256]{1,0:T(8,128)(2,1)S(1)} %copy-done.13, bf16[256,256]{1,0:T(8,128)(2,1)S(1)} %get-tuple-element.33.refs_2_, bf16[2,256,256]{2,1,0:T(8,128)(2,1)S(1)} %copy-done.6, ...), custom_call_target="tpu_custom_call", output_to_operand_aliasing={{}: (12, {})} | custom-call | flops 1207959552 | bytes 4194304 | tf_op jit(solution)/shard_map/back/pallas_call | solution.py:126
  166.7 0.7 collective-permute-done.29.one
  167.4 3.2 %collective-permute-done.30.two = bf16[9,16,256]{2,1,0:T(8,128)(2,1)S(1)} collective-permute-done((bf16[9,16,256]{2,1,0:T(8,128)(2,1)S(1)}, bf16[9,16,256]{2,1,0:T(8,128)(2,1)S(1)}, u32[]{:S(2)}, u32[]{:S(2)}) %collective-permute-start.30) | collective-permute-done | bytes 73760 | tf_op jit(solution)/shard_map/ppermute | solution.py:244
  170.6 0.7 finish.3
  (91 shorter events, 4.2 us)
Async XLA Ops:
  1.6 12.9 %copy-start.21 = (bf16[256,256]{1,0:T(8,128)(2,1)}, bf16[256,256]{1,0:T(8,128)(2,1)S(1)}, u32[]{:S(2)}) copy-start(bf16[256,256]{1,0:T(8,128)(2,1)S(1)} %get-tuple-element.59.refs_2_.refs_1_) | copy-start | bytes 393220
  1.6 12.8 %copy-start.23 = (bf16[256,256]{1,0:T(8,128)(2,1)}, bf16[256,256]{1,0:T(8,128)(2,1)S(1)}, u32[]{:S(2)}) copy-start(bf16[256,256]{1,0:T(8,128)(2,1)S(1)} %get-tuple-element.60.refs_4_.refs_3_) | copy-start | bytes 393220
  1.6 10.2 %collective-permute-start = (bf16[256,256]{1,0:T(8,128)(2,1)S(1)}, bf16[256,256]{1,0:T(8,128)(2,1)S(1)}, u32[]{:S(2)}, u32[]{:S(2)}) collective-permute-start(bf16[256,256]{1,0:T(8,128)(2,1)S(1)} %get-tuple-element.60.refs_4_.refs_3_), channel_id=1, source_target_pairs={{0,1},{1,2},{2,3},{3,4},{4,5},{5,6},{6,7},{7,8},{8,9},{9,10},{10,1... | collective-permute-start | bytes 393224 | tf_op jit(solution)/shard_map/ppermute | solution.py:257
  5.5 6.3 %copy-start.36 = (bf16[1,4,256,256]{3,2,1,0:T(8,128)(2,1)S(1)}, bf16[1,4,256,256]{3,2,1,0:T(8,128)(2,1)}, u32[]{:S(2)}) copy-start(bf16[1,4,256,256]{3,2,1,0:T(8,128)(2,1)} %param.8) | copy-start | bytes 1572868
  5.5 9.0 %collective-permute-start.1 = (bf16[256,256]{1,0:T(8,128)(2,1)S(1)}, bf16[256,256]{1,0:T(8,128)(2,1)S(1)}, u32[]{:S(2)}, u32[]{:S(2)}) collective-permute-start(bf16[256,256]{1,0:T(8,128)(2,1)S(1)} %get-tuple-element.59.refs_2_.refs_1_), channel_id=1, source_target_pairs={{1,0},{2,1},{3,2},{4,3},{5,4},{6,5},{7,6},{8,7},{9,8},{10,9},{11,1... | collective-permute-start | bytes 393224 | tf_op jit(solution)/shard_map/ppermute | solution.py:258
  11.9 5.1 %copy-start.31 = (bf16[256,256]{1,0:T(8,128)(2,1)}, bf16[256,256]{1,0:T(8,128)(2,1)S(1)}, u32[]{:S(2)}) copy-start(bf16[256,256]{1,0:T(8,128)(2,1)S(1)} %collective-permute-done.refs_1_.refs_0_) | copy-start | bytes 393220
  14.5 2.5 %copy-start.33 = (bf16[256,256]{1,0:T(8,128)(2,1)}, bf16[256,256]{1,0:T(8,128)(2,1)S(1)}, u32[]{:S(2)}) copy-start(bf16[256,256]{1,0:T(8,128)(2,1)S(1)} %collective-permute-done.1.refs_5_.refs_4_) | copy-start | bytes 393220
  14.5 3.8 %copy-start.35 = (bf16[2,4,256,256]{3,2,1,0:T(8,128)(2,1)S(1)}, bf16[2,4,256,256]{3,2,1,0:T(8,128)(2,1)}, u32[]{:S(2)}) copy-start(bf16[2,4,256,256]{3,2,1,0:T(8,128)(2,1)} %param.9) | copy-start | bytes 3145732
  16.9 26.3 %collective-permute-start.17 = (bf16[4,4,9,16,256]{4,3,2,1,0:T(8,128)(2,1)}, bf16[4,4,9,16,256]{4,3,2,1,0:T(8,128)(2,1)}, u32[]{:S(2)}, u32[]{:S(2)}) collective-permute-start(bf16[4,4,9,16,256]{4,3,2,1,0:T(8,128)(2,1)} %weight.3), channel_id=1, source_target_pairs={{0,16},{16,0},{32,48},{48,32},{64,80},{80,64},{96,112},{112,96},{1... | collective-permute-start | bytes 3538952 | tf_op jit(solution)/shard_map/ppermute | solution.py:253
  17.0 60.3 %collective-permute-start.4 = (bf16[9,256,256]{2,1,0:T(8,128)(2,1)}, bf16[9,256,256]{2,1,0:T(8,128)(2,1)S(1)}, u32[]{:S(2)}, u32[]{:S(2)}) collective-permute-start(bf16[9,256,256]{2,1,0:T(8,128)(2,1)} %bitcast.7.refs_6_), channel_id=1, source_target_pairs={{16,0},{48,32},{80,64},{112,96},{144,128},{176,160},{208,192},{240... | collective-permute-start | bytes 3538952 | tf_op jit(solution)/shard_map/ppermute | solution.py:253
  19.1 1.0 copy-start
  20.2 0.9 copy-start.22
  21.1 0.9 copy-start.24
  22.0 0.9 copy-start.32
  22.9 0.9 copy-start.34
  28.9 11.1 %collective-permute-start.2 = (bf16[256,256]{1,0:T(8,128)(2,1)}, bf16[256,256]{1,0:T(8,128)(2,1)S(1)}, u32[]{:S(2)}, u32[]{:S(2)}) collective-permute-start(bf16[256,256]{1,0:T(8,128)(2,1)} %get-tuple-element.28.refs_5_), channel_id=1, source_target_pairs={{0,1},{1,2},{2,3},{3,4},{4,5},{5,6},{6,7},{7,8},{8,9},{9,10},{10,1... | collective-permute-start | bytes 393224 | tf_op jit(solution)/shard_map/ppermute | solution.py:257
  31.3 11.2 %collective-permute-start.3 = (bf16[256,256]{1,0:T(8,128)(2,1)}, bf16[256,256]{1,0:T(8,128)(2,1)S(1)}, u32[]{:S(2)}, u32[]{:S(2)}) collective-permute-start(bf16[256,256]{1,0:T(8,128)(2,1)} %get-tuple-element.29.refs_3_), channel_id=1, source_target_pairs={{1,0},{2,1},{3,2},{4,3},{5,4},{6,5},{7,6},{8,7},{9,8},{10,9},{11,1... | collective-permute-start | bytes 393224 | tf_op jit(solution)/shard_map/ppermute | solution.py:258
  40.0 9.5 %copy-start.16 = (bf16[256,256]{1,0:T(8,128)(2,1)}, bf16[256,256]{1,0:T(8,128)(2,1)S(1)}, u32[]{:S(2)}) copy-start(bf16[256,256]{1,0:T(8,128)(2,1)S(1)} %collective-permute-done.2.refs_2_) | copy-start | bytes 393220
  43.2 1.0 copy-start.8
  44.2 0.9 copy-start.19
  50.9 52.9 %collective-permute-start.25 = (bf16[4,4,9,16,256]{4,3,2,1,0:T(8,128)(2,1)}, bf16[4,4,9,16,256]{4,3,2,1,0:T(8,128)(2,1)}, u32[]{:S(2)}, u32[]{:S(2)}) collective-permute-start(bf16[4,4,9,16,256]{4,3,2,1,0:T(8,128)(2,1)} %get-tuple-element.45), channel_id=1, source_target_pairs={{16,0},{48,32},{80,64},{112,96},{144,128},{176,160},{208,192},{240... | collective-permute-start | bytes 3538952 | tf_op jit(solution)/shard_map/ppermute | solution.py:253
  53.9 19.2 %collective-permute-start.5 = (bf16[9,64,256]{2,1,0:T(8,128)(2,1)}, bf16[9,64,256]{2,1,0:T(8,128)(2,1)}, u32[]{:S(2)}, u32[]{:S(2)}) collective-permute-start(bf16[9,64,256]{2,1,0:T(8,128)(2,1)} %dynamic-slice_bitcast_fusion), channel_id=1, source_target_pairs={{0,240},{32,16},{64,48},{96,80},{128,112},{160,144},{192,176},{224... | collective-permute-start | bytes 884744 | tf_op jit(solution)/shard_map/ppermute | solution.py:253
  73.1 4.1 %collective-permute-start.6 = (bf16[9,64,256]{2,1,0:T(8,128)(2,1)}, bf16[9,64,256]{2,1,0:T(8,128)(2,1)}, u32[]{:S(2)}, u32[]{:S(2)}) collective-permute-start(bf16[9,64,256]{2,1,0:T(8,128)(2,1)} %collective-permute-done.5.refs_9_), channel_id=1, source_target_pairs={{16,28},{17,29},{18,30},{19,31},{20,16},{21,17},{22,18},{23,19},{2... | collective-permute-start | bytes 884744 | tf_op jit(solution)/shard_map/ppermute | solution.py:249
  74.5 2.8 %collective-permute-start.7 = (bf16[9,64,256]{2,1,0:T(8,128)(2,1)}, bf16[9,64,256]{2,1,0:T(8,128)(2,1)}, u32[]{:S(2)}, u32[]{:S(2)}) collective-permute-start(bf16[9,64,256]{2,1,0:T(8,128)(2,1)} %collective-permute-done.5.refs_9_), channel_id=1, source_target_pairs={{16,24},{17,25},{18,26},{19,27},{20,28},{21,29},{22,30},{23,31},{2... | collective-permute-start | bytes 884744 | tf_op jit(solution)/shard_map/ppermute | solution.py:249
  75.9 1.4 collective-permute-start.8
  77.3 1.0 copy-start.9
  78.2 0.9 copy-start.17
  79.1 0.9 copy-start.20
  80.0 8.2 %copy-start.28 = (bf16[4,9,16,256]{3,2,1,0:T(8,128)(2,1)S(1)}, bf16[4,9,16,256]{3,2,1,0:T(8,128)(2,1)}, u32[]{:S(2)}) copy-start(bf16[4,9,16,256]{3,2,1,0:T(8,128)(2,1)} %copy-done.27) | copy-start | bytes 884740
  80.0 9.5 %copy-start.26 = (bf16[4,9,16,256]{3,2,1,0:T(8,128)(2,1)S(1)}, bf16[4,9,16,256]{3,2,1,0:T(8,128)(2,1)}, u32[]{:S(2)}) copy-start(bf16[4,9,16,256]{3,2,1,0:T(8,128)(2,1)} %copy-done.25) | copy-start | bytes 884740
  85.0 24.0 %copy-start.5 = (bf16[2,256,256]{2,1,0:T(8,128)(2,1)}, bf16[2,256,256]{2,1,0:T(8,128)(2,1)S(1)}, u32[]{:S(2)}) copy-start(bf16[2,256,256]{2,1,0:T(8,128)(2,1)S(1)} %get-tuple-element.34.refs_3_) | copy-start | bytes 786436
  85.0 24.0 %copy-start.10 = (bf16[256,256]{1,0:T(8,128)(2,1)}, bf16[256,256]{1,0:T(8,128)(2,1)S(1)}, u32[]{:S(2)}) copy-start(bf16[256,256]{1,0:T(8,128)(2,1)S(1)} %get-tuple-element.32.refs_4_) | copy-start | bytes 393220
  85.0 77.1 %collective-permute-start.11 = (bf16[9,256,256]{2,1,0:T(8,128)(2,1)}, bf16[9,256,256]{2,1,0:T(8,128)(2,1)S(1)}, u32[]{:S(2)}, u32[]{:S(2)}) collective-permute-start(bf16[9,256,256]{2,1,0:T(8,128)(2,1)} %get-tuple-element.35), channel_id=1, source_target_pairs={{16,0},{48,32},{80,64},{112,96},{144,128},{176,160},{208,192},{240... | collective-permute-start | bytes 3538952 | tf_op jit(solution)/shard_map/ppermute | solution.py:253
  86.3 9.7 %collective-permute-start.9 = (bf16[256,256]{1,0:T(8,128)(2,1)S(1)}, bf16[256,256]{1,0:T(8,128)(2,1)S(1)}, u32[]{:S(2)}, u32[]{:S(2)}) collective-permute-start(bf16[256,256]{1,0:T(8,128)(2,1)S(1)} %get-tuple-element.32.refs_4_), channel_id=1, source_target_pairs={{0,1},{1,2},{2,3},{3,4},{4,5},{5,6},{6,7},{7,8},{8,9},{9,10},{10,1... | collective-permute-start | bytes 393224 | tf_op jit(solution)/shard_map/ppermute | solution.py:257
  88.2 21.5 %collective-permute-start.18 = (bf16[4,9,16,256]{3,2,1,0:T(8,128)(2,1)S(1)}, bf16[4,9,16,256]{3,2,1,0:T(8,128)(2,1)S(1)}, u32[]{:S(2)}, u32[]{:S(2)}) collective-permute-start(bf16[4,9,16,256]{3,2,1,0:T(8,128)(2,1)S(1)} %copy-done.28), channel_id=1, source_target_pairs={{0,4},{1,5},{2,6},{3,7},{4,8},{5,9},{6,10},{7,11},{8,12},{9,13},{1... | collective-permute-start | bytes 884744 | tf_op jit(solution)/shard_map/ppermute | solution.py:244
  89.5 23.0 %collective-permute-start.19 = (bf16[4,9,16,256]{3,2,1,0:T(8,128)(2,1)S(1)}, bf16[4,9,16,256]{3,2,1,0:T(8,128)(2,1)S(1)}, u32[]{:S(2)}, u32[]{:S(2)}) collective-permute-start(bf16[4,9,16,256]{3,2,1,0:T(8,128)(2,1)S(1)} %copy-done.26), channel_id=1, source_target_pairs={{0,8},{1,9},{2,10},{3,11},{4,12},{5,13},{6,14},{7,15},{8,0},{9,1},... | collective-permute-start | bytes 884744 | tf_op jit(solution)/shard_map/ppermute | solution.py:244
  96.0 13.1 %copy-start.12 = (bf16[256,256]{1,0:T(8,128)(2,1)}, bf16[256,256]{1,0:T(8,128)(2,1)S(1)}, u32[]{:S(2)}) copy-start(bf16[256,256]{1,0:T(8,128)(2,1)S(1)} %collective-permute-done.9.refs_1_) | copy-start | bytes 393220
  96.0 7.8 %collective-permute-start.10 = (bf16[256,256]{1,0:T(8,128)(2,1)S(1)}, bf16[256,256]{1,0:T(8,128)(2,1)S(1)}, u32[]{:S(2)}, u32[]{:S(2)}) collective-permute-start(bf16[256,256]{1,0:T(8,128)(2,1)S(1)} %get-tuple-element.33.refs_2_), channel_id=1, source_target_pairs={{1,0},{2,1},{3,2},{4,3},{5,4},{6,5},{7,6},{8,7},{9,8},{10,9},{11,1... | collective-permute-start | bytes 393224 | tf_op jit(solution)/shard_map/ppermute | solution.py:258
  103.8 5.2 %copy-start.14 = (bf16[256,256]{1,0:T(8,128)(2,1)}, bf16[256,256]{1,0:T(8,128)(2,1)S(1)}, u32[]{:S(2)}) copy-start(bf16[256,256]{1,0:T(8,128)(2,1)S(1)} %collective-permute-done.10.refs_5_) | copy-start | bytes 393220
  103.8 10.8 %collective-permute-start.20 = (bf16[4,9,16,256]{3,2,1,0:T(8,128)(2,1)}, bf16[4,9,16,256]{3,2,1,0:T(8,128)(2,1)}, u32[]{:S(2)}, u32[]{:S(2)}) collective-permute-start(bf16[4,9,16,256]{3,2,1,0:T(8,128)(2,1)} %get-tuple-element.40), channel_id=1, source_target_pairs={{0,12},{1,13},{2,14},{3,15},{4,0},{5,1},{6,2},{7,3},{8,4},{9,5},{1... | collective-permute-start | bytes 884744 | tf_op jit(solution)/shard_map/ppermute | solution.py:244
  103.8 14.0 %collective-permute-start.12 = (bf16[9,64,256]{2,1,0:T(8,128)(2,1)}, bf16[9,64,256]{2,1,0:T(8,128)(2,1)}, u32[]{:S(2)}, u32[]{:S(2)}) collective-permute-start(bf16[9,64,256]{2,1,0:T(8,128)(2,1)} %dynamic-slice_bitcast_fusion), channel_id=1, source_target_pairs={{16,240},{48,16},{80,48},{112,80},{144,112},{176,144},{208,176},{2... | collective-permute-start | bytes 884744 | tf_op jit(solution)/shard_map/ppermute | solution.py:253
  105.2 25.7 %copy-start.37 = (bf16[1,16,9,256]{3,1,2,0:T(8,128)(2,1)S(1)}, bf16[1,16,9,256]{3,1,2,0:T(8,128)(2,1)}, u32[]{:S(2)}) copy-start(bf16[1,16,9,256]{3,1,2,0:T(8,128)(2,1)} %param.6) | copy-start | bytes 221188
  109.8 0.7 copy-start.1
  110.5 18.5 %collective-permute-start.26 = (bf16[4,9,16,256]{3,2,1,0:T(8,128)(2,1)}, bf16[4,9,16,256]{3,2,1,0:T(8,128)(2,1)S(1)}, u32[]{:S(2)}, u32[]{:S(2)}) collective-permute-start(bf16[4,9,16,256]{3,2,1,0:T(8,128)(2,1)} %get-tuple-element.47), channel_id=1, source_target_pairs={{0,4},{1,5},{2,6},{3,7},{4,8},{5,9},{6,10},{7,11},{8,12},{9,13},{1... | collective-permute-start | bytes 884744 | tf_op jit(solution)/shard_map/ppermute | solution.py:244
  113.2 16.4 %collective-permute-start.27 = (bf16[4,9,16,256]{3,2,1,0:T(8,128)(2,1)}, bf16[4,9,16,256]{3,2,1,0:T(8,128)(2,1)}, u32[]{:S(2)}, u32[]{:S(2)}) collective-permute-start(bf16[4,9,16,256]{3,2,1,0:T(8,128)(2,1)} %get-tuple-element.48), channel_id=1, source_target_pairs={{0,8},{1,9},{2,10},{3,11},{4,12},{5,13},{6,14},{7,15},{8,0},{9,1},... | collective-permute-start | bytes 884744 | tf_op jit(solution)/shard_map/ppermute | solution.py:244
  114.5 1.0 copy-start.2
  115.5 1.0 copy-start.4
  116.5 7.4 %copy-start.30 = (bf16[4,9,16,256]{3,2,1,0:T(8,128)(2,1)S(1)}, bf16[4,9,16,256]{3,2,1,0:T(8,128)(2,1)}, u32[]{:S(2)}) copy-start(bf16[4,9,16,256]{3,2,1,0:T(8,128)(2,1)} %copy-done.29) | copy-start | bytes 884740
  117.6 45.5 %copy-start.6 = (bf16[2,256,256]{2,1,0:T(8,128)(2,1)S(1)}, bf16[2,256,256]{2,1,0:T(8,128)(2,1)}, u32[]{:S(2)}) copy-start(bf16[2,256,256]{2,1,0:T(8,128)(2,1)} %copy-done.5) | copy-start | bytes 786436
  117.6 45.5 %copy-start.11 = (bf16[256,256]{1,0:T(8,128)(2,1)S(1)}, bf16[256,256]{1,0:T(8,128)(2,1)}, u32[]{:S(2)}) copy-start(bf16[256,256]{1,0:T(8,128)(2,1)} %copy-done.10) | copy-start | bytes 393220
  117.6 45.5 %copy-start.13 = (bf16[256,256]{1,0:T(8,128)(2,1)S(1)}, bf16[256,256]{1,0:T(8,128)(2,1)}, u32[]{:S(2)}) copy-start(bf16[256,256]{1,0:T(8,128)(2,1)} %copy-done.12) | copy-start | bytes 393220
  117.7 45.5 %copy-start.15 = (bf16[256,256]{1,0:T(8,128)(2,1)S(1)}, bf16[256,256]{1,0:T(8,128)(2,1)}, u32[]{:S(2)}) copy-start(bf16[256,256]{1,0:T(8,128)(2,1)} %copy-done.14) | copy-start | bytes 393220
  117.7 6.2 %collective-permute-start.21 = (bf16[9,16,256]{2,1,0:T(8,128)(2,1)S(1)}, bf16[9,16,256]{2,1,0:T(8,128)(2,1)S(1)}, u32[]{:S(2)}, u32[]{:S(2)}) collective-permute-start(bf16[9,16,256]{2,1,0:T(8,128)(2,1)S(1)} %get-tuple-element.42), channel_id=1, source_target_pairs={{0,1},{1,2},{2,3},{3,0},{4,5},{5,6},{6,7},{7,4},{8,9},{9,10},{10,1... | collective-permute-start | bytes 221192 | tf_op jit(solution)/shard_map/ppermute | solution.py:244
  117.8 6.1 %collective-permute-start.22 = (bf16[9,16,256]{2,1,0:T(8,128)(2,1)S(1)}, bf16[9,16,256]{2,1,0:T(8,128)(2,1)S(1)}, u32[]{:S(2)}, u32[]{:S(2)}) collective-permute-start(bf16[9,16,256]{2,1,0:T(8,128)(2,1)S(1)} %get-tuple-element.43), channel_id=1, source_target_pairs={{0,2},{1,3},{2,0},{3,1},{4,6},{5,7},{6,4},{7,5},{8,10},{9,11},{10,... | collective-permute-start | bytes 221192 | tf_op jit(solution)/shard_map/ppermute | solution.py:244
  123.9 4.4 %collective-permute-start.23 = (bf16[9,16,256]{2,1,0:T(8,128)(2,1)S(1)}, bf16[9,16,256]{2,1,0:T(8,128)(2,1)S(1)}, u32[]{:S(2)}, u32[]{:S(2)}) collective-permute-start(bf16[9,16,256]{2,1,0:T(8,128)(2,1)S(1)} %get-tuple-element.44), channel_id=1, source_target_pairs={{0,3},{1,0},{2,1},{3,2},{4,7},{5,4},{6,5},{7,6},{8,11},{9,8},{10,9... | collective-permute-start | bytes 221192 | tf_op jit(solution)/shard_map/ppermute | solution.py:244
  123.9 6.9 %collective-permute-start.28 = (bf16[4,9,16,256]{3,2,1,0:T(8,128)(2,1)S(1)}, bf16[4,9,16,256]{3,2,1,0:T(8,128)(2,1)S(1)}, u32[]{:S(2)}, u32[]{:S(2)}) collective-permute-start(bf16[4,9,16,256]{3,2,1,0:T(8,128)(2,1)S(1)} %copy-done.30), channel_id=1, source_target_pairs={{0,12},{1,13},{2,14},{3,15},{4,0},{5,1},{6,2},{7,3},{8,4},{9,5},{1... | collective-permute-start | bytes 884744 | tf_op jit(solution)/shard_map/ppermute | solution.py:244
  128.3 5.4 %collective-permute-start.13 = (bf16[9,64,256]{2,1,0:T(8,128)(2,1)}, bf16[9,64,256]{2,1,0:T(8,128)(2,1)S(1)}, u32[]{:S(2)}, u32[]{:S(2)}) collective-permute-start(bf16[9,64,256]{2,1,0:T(8,128)(2,1)} %collective-permute-done.12.refs_8_), channel_id=1, source_target_pairs={{16,28},{17,29},{18,30},{19,31},{20,16},{21,17},{22,18},{23,19},{2... | collective-permute-start | bytes 884744 | tf_op jit(solution)/shard_map/ppermute | solution.py:249
  128.9 30.3 %collective-permute-start.14 = (bf16[9,64,256]{2,1,0:T(8,128)(2,1)}, bf16[9,64,256]{2,1,0:T(8,128)(2,1)S(1)}, u32[]{:S(2)}, u32[]{:S(2)}) collective-permute-start(bf16[9,64,256]{2,1,0:T(8,128)(2,1)} %collective-permute-done.12.refs_8_), channel_id=1, source_target_pairs={{16,24},{17,25},{18,26},{19,27},{20,28},{21,29},{22,30},{23,31},{2... | collective-permute-start | bytes 884744 | tf_op jit(solution)/shard_map/ppermute | solution.py:249
  129.6 29.6 %collective-permute-start.15 = (bf16[9,64,256]{2,1,0:T(8,128)(2,1)}, bf16[9,64,256]{2,1,0:T(8,128)(2,1)S(1)}, u32[]{:S(2)}, u32[]{:S(2)}) collective-permute-start(bf16[9,64,256]{2,1,0:T(8,128)(2,1)} %collective-permute-done.12.refs_8_), channel_id=1, source_target_pairs={{16,20},{17,21},{18,22},{19,23},{20,24},{21,25},{22,26},{23,27},{2... | collective-permute-start | bytes 884744 | tf_op jit(solution)/shard_map/ppermute | solution.py:249
  130.9 35.8 %collective-permute-start.16 = (bf16[9,16,256]{2,1,0:T(8,128)(2,1)S(1)}, bf16[9,16,256]{2,1,0:T(8,128)(2,1)S(1)}, u32[]{:S(2)}, u32[]{:S(2)}) collective-permute-start(bf16[9,16,256]{2,1,0:T(8,128)(2,1)S(1)} %bitcast.35), channel_id=1, source_target_pairs={{0,224},{16,240},{32,0},{48,16},{64,32},{80,48},{96,64},{112,80},{... | collective-permute-start | bytes 221192 | tf_op jit(solution)/shard_map/ppermute | solution.py:253
  133.7 33.0 %collective-permute-start.24 = (bf16[9,16,256]{2,1,0:T(8,128)(2,1)S(1)}, bf16[9,16,256]{2,1,0:T(8,128)(2,1)S(1)}, u32[]{:S(2)}, u32[]{:S(2)}) collective-permute-start(bf16[9,16,256]{2,1,0:T(8,128)(2,1)S(1)} %finish.2), channel_id=1, source_target_pairs={{0,240},{32,16},{64,48},{96,80},{128,112},{160,144},{192,176},{224... | collective-permute-start | bytes 221192 | tf_op jit(solution)/shard_map/ppermute | solution.py:253
  159.2 8.2 %collective-permute-start.29 = (bf16[9,16,256]{2,1,0:T(8,128)(2,1)S(1)}, bf16[9,16,256]{2,1,0:T(8,128)(2,1)S(1)}, u32[]{:S(2)}, u32[]{:S(2)}) collective-permute-start(bf16[9,16,256]{2,1,0:T(8,128)(2,1)S(1)} %get-tuple-element.51), channel_id=1, source_target_pairs={{0,1},{1,2},{2,3},{3,0},{4,5},{5,6},{6,7},{7,4},{8,9},{9,10},{10,1... | collective-permute-start | bytes 221192 | tf_op jit(solution)/shard_map/ppermute | solution.py:244
  159.2 11.4 %collective-permute-start.30 = (bf16[9,16,256]{2,1,0:T(8,128)(2,1)S(1)}, bf16[9,16,256]{2,1,0:T(8,128)(2,1)S(1)}, u32[]{:S(2)}, u32[]{:S(2)}) collective-permute-start(bf16[9,16,256]{2,1,0:T(8,128)(2,1)S(1)} %get-tuple-element.52), channel_id=1, source_target_pairs={{0,2},{1,3},{2,0},{3,1},{4,6},{5,7},{6,4},{7,5},{8,10},{9,11},{10,... | collective-permute-start | bytes 221192 | tf_op jit(solution)/shard_map/ppermute | solution.py:244
  162.1 8.5 %collective-permute-start.31 = (bf16[9,16,256]{2,1,0:T(8,128)(2,1)S(1)}, bf16[9,16,256]{2,1,0:T(8,128)(2,1)S(1)}, u32[]{:S(2)}, u32[]{:S(2)}) collective-permute-start(bf16[9,16,256]{2,1,0:T(8,128)(2,1)S(1)} %get-tuple-element.53), channel_id=1, source_target_pairs={{0,3},{1,0},{2,1},{3,2},{4,7},{5,4},{6,5},{7,6},{8,11},{9,8},{10,9... | collective-permute-start | bytes 221192 | tf_op jit(solution)/shard_map/ppermute | solution.py:244
  (6 other events, 4.2 us)

commit v3 on v1

v3 whole, which is shorter than its diff:
```python
import functools

import jax
import jax.numpy as jnp
from jax import lax
from jax.experimental import pallas as pl
from jax.experimental.pallas import tpu as pltpu
from jax.sharding import PartitionSpec as P

TICKS = 3
BF = jnp.bfloat16
F32 = jnp.float32
VMEM_BYTES = 12 * 1024 * 1024
SMALL_VMEM_BYTES = 6 * 1024 * 1024


def whole(memory=pltpu.VMEM):
    return pl.BlockSpec(memory_space=memory)


def fill_shifted(shift_ref, rows):
    for index, row in enumerate(rows):
        wide = row.astype(F32)
        columns = wide.shape[1]
        place = lax.broadcasted_iota(jnp.int32, wide.shape, 1)
        ahead = pltpu.roll(wide, columns - 1, 1)
        behind = pltpu.roll(wide, 1, 1)
        shift_ref[0, index] = jnp.where(place == columns - 1, 0.0, ahead).astype(BF)
        shift_ref[1, index] = row
        shift_ref[2, index] = jnp.where(place == 0, 0.0, behind).astype(BF)


def near(shape, kind=BF):
    return jax.ShapeDtypeStruct(shape, kind)


def kept(value):
    return pltpu.with_memory_space_constraint(value, pltpu.HBM)


def fetch(pairs, sems):
    copies = [pltpu.make_async_copy(source, target, sems.at[i]) for i, (source, target) in enumerate(pairs)]
    for copy in copies:
        copy.start()
    return copies


def gradient_rows(edges, image):
    if image is None:
        up, top, mid, bot, down = edges
        return [up[...], top[...], *[mid[i] for i in range(mid.shape[0])], bot[...], down[...]]
    return [edges[0][...], *[image[i] for i in range(image.shape[0])], edges[1][...]]


def back_kernel(tick, *refs):
    refs = list(refs)
    first, last = tick == 0, tick == TICKS - 1
    restart = lax.axis_index("blk") == lax.axis_size("blk") - tick - 1
    edges = [refs.pop(0) for _ in range(2 if first else 5)]
    image_far = refs.pop(0) if first else None
    kernel = refs.pop(0)
    pieces = [refs.pop(0) for _ in range(2)] if tick == 1 else []
    saved_far = refs.pop(0)
    fresh_far = None if last else refs.pop(0)
    if not first:
        refs.pop(0)
    states = refs.pop(0)
    outs = [] if last else [refs.pop(0) for _ in range(3)]
    joined = kernel if last else refs.pop(0)
    shift_ref, turned, result, saved = [refs.pop(0) for _ in range(4)]
    fresh = None if last else refs.pop(0)
    image = refs.pop(0) if first else None
    sems, sem = refs
    height, channels, _ = saved.shape
    pairs = [(saved_far.at[tick, 0], saved)]
    if first:
        pairs = [(image_far.at[0], image), (kernel, joined)] + pairs
    if not last:
        pairs.append((fresh_far.at[tick], fresh))
    copies = fetch(pairs, sems)
    if first:
        copies.pop(0).wait()
    fill_shifted(shift_ref, gradient_rows(edges, image))
    if first:
        copies.pop(0).wait()
    for k, piece in enumerate(pieces):
        part = piece.shape[1]
        start = pl.multiple_of(lax.rem(lax.axis_index("rows") // 4 + k, 2) * part, part)
        joined[:, pl.ds(start, part), :] = kernel[:, pl.ds(start, part), :] + piece[...]
    for b in range(3):
        for j in range(3):
            turned[b, :, j * channels : (j + 1) * channels] = joined[3 * (2 - j) + b].T
    for copy in copies:
        copy.wait()
    copies = []
    for r in range(height):
        total = None
        for b in range(3):
            window = shift_ref[b, r : r + 3].reshape(3 * channels, -1)
            part = jnp.dot(turned[b], window, preferred_element_type=F32)
            total = part if total is None else total + part
        value = jnp.where(saved[r] > 0, total, 0.0).astype(BF)
        result[r] = value
        copy = pltpu.make_async_copy(result.at[r], states.at[tick, 0, r], sem.at[r])
        copy.start()
        copies.append(copy)
        if not last:
            value = jnp.where(restart, fresh[r], value)
            if r == 0:
                outs[0][...] = value
            elif r == height - 1:
                outs[2][...] = value
            else:
                outs[1][r - 1] = value
    for copy in copies:
        copy.wait()


def back_project(tick, edges, image, kernel, pieces, saved, states, fresh):
    first, last = tick == 0, tick == TICKS - 1
    _, _, height, channels, columns = saved.shape
    args, specs = [], []

    def give(value, memory=pltpu.VMEM):
        args.append(kept(value) if memory is pl.ANY else value)
        specs.append(whole(memory))

    for value in edges:
        give(value)
    if first:
        give(image, pl.ANY)
        give(kernel, pl.ANY)
    else:
        for value in (kernel, *pieces):
            give(value)
    give(saved, pl.ANY)
    if not last:
        give(fresh, pl.ANY)
    alias = {}
    if not first:
        alias = {len(args): 0}
        give(states, pl.ANY)
    shapes = [jax.ShapeDtypeStruct((TICKS, 1, height, channels, columns), BF)]
    block = (height, channels, columns)
    scratch = [
        pltpu.VMEM((3, height + 2, channels, columns), BF),
        pltpu.VMEM((3, channels, 3 * channels), BF),
        pltpu.VMEM(block, BF),
        pltpu.VMEM(block, BF),
    ]
    if not last:
        shapes += [near((channels, columns)), near((height - 2, channels, columns)), near((channels, columns))]
        scratch.append(pltpu.VMEM(block, BF))
    if first:
        scratch.append(pltpu.VMEM(block, BF))
    if tick == 1:
        shapes.append(near(kernel.shape))
    if first:
        scratch = [pltpu.VMEM(kernel.shape, BF)] + scratch
    scratch += [pltpu.SemaphoreType.DMA((4,)), pltpu.SemaphoreType.DMA((height,))]
    return pl.pallas_call(
        functools.partial(back_kernel, tick),
        out_shape=shapes,
        in_specs=specs,
        out_specs=[whole(pl.ANY)] + [whole()] * (len(shapes) - 1),
        scratch_shapes=scratch,
        input_output_aliases=alias,
        compiler_params=pltpu.CompilerParams(vmem_limit_bytes=VMEM_BYTES),
        cost_estimate=pl.CostEstimate(flops=1, bytes_accessed=1, transcendentals=0),
        name="back",
    )(*args)


def weight_kernel(tick, scale, *refs):
    refs = list(refs)
    first = tick == 0
    edges = [refs.pop(0) for _ in range(2 if first else 5)]
    image_far = refs.pop(0) if first else None
    saved_far = refs.pop(0)
    out = refs.pop(0)
    sems = refs.pop()
    image = refs.pop() if first else None
    saved = refs.pop()
    shift_ref = refs.pop()
    height, channels, _ = saved.shape
    pairs = [(saved_far.at[tick, 0], saved)]
    if first:
        pairs.insert(0, (image_far.at[0], image))
    copies = fetch(pairs, sems)
    if first:
        copies.pop(0).wait()
    fill_shifted(shift_ref, gradient_rows(edges, image))
    copies.pop(0).wait()
    inputs = [jnp.maximum(saved[r], 0) for r in range(height)]
    part = channels // 4
    piece = part // 4
    for k in range(4):
        total = None
        for r in range(height):
            left = shift_ref[:, r : r + 3, k * part : (k + 1) * part, :].reshape(9 * part, -1)
            term = lax.dot_general(left, inputs[r], (((1,), (1,)), ((), ())), preferred_element_type=F32)
            total = term if total is None else total + term
        total = total * scale
        for b in range(3):
            for j in range(3):
                base = (3 * b + j) * part
                tap = 3 * (2 - j) + b
                for q in range(4):
                    value = total[base + q * piece : base + (q + 1) * piece]
                    out[k, q, tap] = value.astype(BF)


def weight_terms(tick, edges, image, saved, scale):
    _, _, height, channels, columns = saved.shape
    rest = [(edge, pltpu.VMEM) for edge in edges]
    if tick == 0:
        rest.append((kept(image), pl.ANY))
    rest.append((kept(saved), pl.ANY))
    block = pltpu.VMEM((height, channels, columns), BF)
    return pl.pallas_call(
        functools.partial(weight_kernel, tick, scale),
        out_shape=near((4, 4, 9, channels // 16, channels)),
        in_specs=[whole(memory) for _, memory in rest],
        out_specs=whole(),
        scratch_shapes=[pltpu.VMEM((3, height + 2, channels, columns), BF)]
        + [block] * (2 if tick == 0 else 1)
        + [pltpu.SemaphoreType.DMA((2,))],
        compiler_params=pltpu.CompilerParams(vmem_limit_bytes=VMEM_BYTES),
        cost_estimate=pl.CostEstimate(flops=1, bytes_accessed=1, transcendentals=0),
        name="weight",
    )(*[value for value, _ in rest])


def half_kernel(kernel, out, sem):
    part = out.shape[1]
    start = pl.multiple_of(lax.rem(lax.axis_index("rows") // 4, 2) * part, part)
    copy = pltpu.make_async_copy(kernel.at[:, pl.ds(start, part), :], out, sem)
    copy.start()
    copy.wait()


def half_of(kernel):
    taps, rows, columns = kernel.shape
    return pl.pallas_call(
        half_kernel,
        out_shape=near((taps, rows // 2, columns)),
        in_specs=[whole(pl.ANY)],
        out_specs=whole(),
        scratch_shapes=[pltpu.SemaphoreType.DMA],
        compiler_params=pltpu.CompilerParams(vmem_limit_bytes=SMALL_VMEM_BYTES),
        name="half",
    )(kept(kernel))


def pair_kernel(zero, two, other, *outs):
    odd = lax.axis_index("blk") % 2 == 1
    for k in range(4):
        place = lax.rem(lax.axis_index("rows") // 4 + k, 4)
        for q in range(4):
            more = other[place, q].astype(F32)
            early = zero[place, q].astype(F32) + jnp.where(odd, more, 0.0)
            late = two[place, q].astype(F32) + jnp.where(odd, 0.0, more)
            outs[k][q] = early.astype(outs[k].dtype)
            outs[4 + k][q] = late.astype(outs[4 + k].dtype)


def regroup_kernel(own, one, two, three, keep, send):
    place = lax.rem(lax.axis_index("rows"), 4)
    beside = place + 1 - 2 * lax.rem(place, 2)
    spots = (place, lax.rem(place + 2, 4), beside, lax.rem(beside + 2, 4))
    for k, spot in enumerate(spots):
        value = (own[spot] + one[spot].astype(F32)) + (two[spot].astype(F32) + three[spot].astype(F32))
        if k < 2:
            keep[k] = value
        else:
            send[k - 2] = value.astype(BF)


def halve_kernel(keep, came, kept_on, send):
    kept_on[...] = keep[0] + came[0].astype(F32)
    send[...] = (keep[1] + came[1].astype(F32)).astype(BF)


def finish_kernel(held, keep, came, out):
    out[...] = (held[...].astype(F32) + (keep[...] + came[...].astype(F32))).astype(BF)


def small(kernel, shapes, *args):
    return pl.pallas_call(
        kernel,
        out_shape=shapes,
        in_specs=[whole()] * len(args),
        out_specs=[whole()] * len(shapes),
        compiler_params=pltpu.CompilerParams(vmem_limit_bytes=SMALL_VMEM_BYTES),
        cost_estimate=pl.CostEstimate(flops=1, bytes_accessed=1, transcendentals=0),
        name=kernel.__name__,
    )(*args)


def after(values, *others):
    return lax.optimization_barrier((values, others))[0]


def along(value, move):
    return lax.ppermute(value, "rows", [(x * 4 + z, move(x, z)) for x in range(4) for z in range(4)])


def along_odd(value, move):
    pairs = [(b * 16 + x * 4 + z, b * 16 + move(x, z)) for b in range(1, 16, 2) for x in range(4) for z in range(4)]
    return lax.ppermute(value, ("blk", "rows"), pairs)


def around(value, pairs):
    return lax.ppermute(value, "blk", pairs)


def with_edges(top, mid, bot):
    up = lax.ppermute(bot, "rows", [(i, i + 1) for i in range(15)])
    down = lax.ppermute(top, "rows", [(i + 1, i) for i in range(15)])
    return up, top, mid, bot, down


def over_x(parts):
    return [parts[0]] + [along(parts[k], lambda x, z, k=k: ((x + k) % 4) * 4 + z) for k in (1, 2, 3)]


def part_over_z(parts, held):
    shape = (2, *held.shape)
    keep, send = small(regroup_kernel, [near(shape, F32), near(shape)], *parts)
    return keep, along(send, lambda x, z: x * 4 + (z ^ 1))


def rest_over_z(keep, came):
    shape = keep.shape[1:]
    keep, send = small(halve_kernel, [near(shape, F32), near(shape)], keep, came)
    return keep, along(send, lambda x, z: x * 4 + (z ^ 2))


def summed_over_z(parts, held):
    return rest_over_z(*part_over_z(parts, held))


def shards(section_weights, grad_acc, saved_inputs, cotangent, fresh_grads):
    kernel = jnp.transpose(section_weights[0], (1, 0, 2))
    held = jnp.transpose(grad_acc[0], (1, 0, 2))
    height = cotangent.shape[1]
    columns = cotangent.shape[3]
    scale = float(16 * height * columns) ** (-0.5)
    image = cotangent[0]
    back_by = lambda by: [(b, (b - by) % 16) for b in range(16)]
    evens = range(0, 16, 2)

    def back(tick, edges, kernel, pieces, states):
        return back_project(tick, edges, cotangent, kernel, pieces, saved_inputs, states, fresh_grads)

    def weight(tick, edges):
        return weight_terms(tick, edges, cotangent, saved_inputs, scale)

    half = around(half_of(kernel), [(b, (b - 1) % 16) for b in evens])
    up, _, _, _, down = with_edges(image[0], None, image[height - 1])
    half, kernel_here = after((half, kernel), up, down)
    kernel_one = around(kernel_here, [(b + 1, b) for b in evens])
    states, *parts = back(0, (up, down), kernel, (), None)
    edges_one = with_edges(*parts)
    halves = [half, along_odd(half, lambda x, z: (x ^ 1) * 4 + z)]
    sums_zero = weight(0, after((up, down), parts[0]))
    edges_one = after(edges_one, sums_zero)
    states, *parts, used = back(1, edges_one, kernel_one, halves, states)
    edges_two = with_edges(*parts)
    sums_one = weight(1, after(edges_one, parts[0]))
    edges_two, used, sums_one = lax.optimization_barrier((edges_two, used, sums_one))
    other = around(sums_one, [(b, b ^ 1) for b in range(16)])
    kernel_two = around(used, back_by(1))
    sums_two = weight(2, edges_two)
    part = (4, *held.shape)
    spread = ([near(part, F32)] + [near(part)] * 3) * 2
    both = small(pair_kernel, spread, sums_zero, sums_two, other)
    first, last = over_x(both[:4]), over_x(both[4:])
    early = small(finish_kernel, [near(held.shape)], held, *summed_over_z(first, held))
    early = around(early[0], back_by(2))
    keep, came = part_over_z(last, held)
    (states,) = back(2, edges_two, kernel_two, (), states)
    came = after(came, states)
    (held,) = small(finish_kernel, [near(held.shape)], early, *rest_over_z(keep, came))
    return states, jnp.transpose(held, (1, 0, 2))[None]


def solution(mesh):
    return jax.shard_map(
        shards,
        mesh=mesh,
        in_specs=(
            P("blk", None, None, None),
            P("blk", "rows", None, None),
            P(None, "blk", "rows", None, None),
            P("blk", "rows", None, None),
            P(None, "rows", None, None),
        ),
        out_specs=(P(None, "blk", "rows", None, None), P("blk", "rows", None, None)),
        check_vma=False,
    )
```

time: 201 us -> 120 us (0.60); the launches traced: 197 us -> 118 us
  waiting for transfers between devices: 88.2 us -> 42.4 us
  local copies, waits for them, and re-layouts: 19.1 us -> 0.04 us
  starting transfers between devices: 62.9 us -> 52.3 us
  Pallas kernels: 25.6 us -> 22.8 us
    ppermute x3, waiting for transfers between devices: 70.5 us -> 1.47 us  [with_edges(): up = lax.ppermute(bot, 'rows', [(i, i + 1) for i in range(15)])]
    unnamed x92 -> x6, local copies, waits for them, and re-layouts: 15.7 us -> 0.02 us
    ppermute x18 -> x10, waiting for transfers between devices: 14.5 us -> 26.6 us  [along(): lax.ppermute(value, 'rows', [(x * 4 + z, move(x, z)) for x in range(4) fo...]
    ppermute x18 -> x10, starting transfers between devices: 26.6 us -> 14.7 us  [along(): lax.ppermute(value, 'rows', [(x * 4 + z, move(x, z)) for x in range(4) fo...]
    ppermute x3, waiting for transfers between devices: 3.24 us -> 14.3 us  [with_edges(): down = lax.ppermute(top, 'rows', [(i + 1, i) for i in range(15)])]
    ppermute x4 -> x6, starting transfers between devices: 9.9 us -> 14.6 us  [the longest x5 13.9 us: around(): return lax.ppermute(value, 'blk', pairs)]
    squeeze x3 -> x1, local copies, waits for them, and re-layouts: 3.38 us -> 0.02 us  [shards(): up, _, _, _, down = with_edges(image[0], None, image[height - 1])]
    pallas_call x12 -> x14, Pallas kernels: 25.6 us -> 22.8 us  [the longest x3 11.1 us: back_project(): pl.pallas_call(functools.partial(back_kernel, tick), out_shape=shapes, in...]
  transfers between devices with their start and end apart: 28 -> 22, of which waited for: 10 -> 8; matrix products, arithmetic and copies ran while one was open for 2% -> 0% of each run, Pallas kernels for 12% -> 15%
where the time goes in v3:
time: 120 us; the launch traced here: 118 us
  starting transfers between devices  52.3 us (44%)
  waiting for transfers between devices  42.4 us (35%)
  Pallas kernels  22.8 us (19%)
    ppermute x10, waiting for transfers between devices, along(): lax.ppermute(value, 'rows', [(x * 4 + z, move(x, z)) for x in range(4) fo...  26.6 us
    ppermute x3, starting transfers between devices, with_edges(): down = lax.ppermute(top, 'rows', [(i + 1, i) for i in range(15)])  16.1 us
    ppermute x10, starting transfers between devices, along(): lax.ppermute(value, 'rows', [(x * 4 + z, move(x, z)) for x in range(4) fo...  14.7 us
    ppermute x3, waiting for transfers between devices, with_edges(): down = lax.ppermute(top, 'rows', [(i + 1, i) for i in range(15)])  14.3 us
    ppermute x5, starting transfers between devices, around(): return lax.ppermute(value, 'blk', pairs)  13.9 us
    pallas_call x3, Pallas kernels, back_project(): pl.pallas_call(functools.partial(back_kernel, tick), out_shape=shapes, in...  11.1 us
    pallas_call x3, Pallas kernels, weight_terms(): pl.pallas_call(functools.partial(weight_kernel, tick, scale), out_shape=n...  8.84 us
    ppermute x3, starting transfers between devices, with_edges(): up = lax.ppermute(bot, 'rows', [(i, i + 1) for i in range(15)])  6.87 us
  transfers between devices with their start and end apart: 22, of which 8 were waited for; matrix products, arithmetic and copies ran while one was open for 0% of the time, Pallas kernels for 15%

profile of v3, /device:TPU:2, one launch (start us, length us, event | category | flops | bytes accessed | tf_op | source)
XLA Modules:
  0.0 118.4 jit_solution(14614725738855726957)
XLA Ops:
  0.6 0.0 copy-start.1
  0.6 0.0 copy-start.2
  0.7 1.2 %half.1 = bf16[9,128,256]{2,1,0:T(8,128)(2,1)S(1)} custom-call(bf16[9,256,256]{2,1,0:T(8,128)(2,1)} %bitcast.14), custom_call_target="tpu_custom_call" | custom-call | tf_op jit(solution)/shard_map/half/pallas_call | solution.py:244
  1.9 11.0 %collective-permute-start.4 = (bf16[9,128,256]{2,1,0:T(8,128)(2,1)S(1)}, bf16[9,128,256]{2,1,0:T(8,128)(2,1)S(1)}, u32[]{:S(2)}, u32[]{:S(2)}) collective-permute-start(bf16[9,128,256]{2,1,0:T(8,128)(2,1)S(1)} %half.1), channel_id=1, source_target_pairs={{0,240},{32,16},{64,48},{96,80},{128,112},{160,144},{192,176},{224... | collective-permute-start | bytes 1769480 | tf_op jit(solution)/shard_map/ppermute | solution.py:314
  12.9 0.0 copy-done.2
  12.9 3.8 %collective-permute-start.1 = (bf16[256,256]{1,0:T(8,128)(2,1)S(1)}, bf16[256,256]{1,0:T(8,128)(2,1)S(1)}, u32[]{:S(2)}, u32[]{:S(2)}) collective-permute-start(bf16[256,256]{1,0:T(8,128)(2,1)S(1)} %get-tuple-element.96), channel_id=1, source_target_pairs={{1,0},{2,1},{3,2},{4,3},{5,4},{6,5},{7,6},{8,7},{9,8},{10,9},{11,1... | collective-permute-start | bytes 393224 | tf_op jit(solution)/shard_map/ppermute | solution.py:319
  16.8 2.0 %collective-permute-start = (bf16[256,256]{1,0:T(8,128)(2,1)S(1)}, bf16[256,256]{1,0:T(8,128)(2,1)S(1)}, u32[]{:S(2)}, u32[]{:S(2)}) collective-permute-start(bf16[256,256]{1,0:T(8,128)(2,1)S(1)} %get-tuple-element.97), channel_id=1, source_target_pairs={{0,1},{1,2},{2,3},{3,4},{4,5},{5,6},{6,7},{7,8},{8,9},{9,10},{10,1... | collective-permute-start | bytes 393224 | tf_op jit(solution)/shard_map/ppermute | solution.py:318
  18.8 12.1 %collective-permute-done.1.refs_1_ = bf16[256,256]{1,0:T(8,128)(2,1)S(1)} collective-permute-done((bf16[256,256]{1,0:T(8,128)(2,1)S(1)}, bf16[256,256]{1,0:T(8,128)(2,1)S(1)}, u32[]{:S(2)}, u32[]{:S(2)}) %collective-permute-start.1) | collective-permute-done | bytes 131104 | tf_op jit(solution)/shard_map/ppermute | solution.py:319
  30.8 1.5 %collective-permute-done.refs_0_ = bf16[256,256]{1,0:T(8,128)(2,1)S(1)} collective-permute-done((bf16[256,256]{1,0:T(8,128)(2,1)S(1)}, bf16[256,256]{1,0:T(8,128)(2,1)S(1)}, u32[]{:S(2)}, u32[]{:S(2)}) %collective-permute-start) | collective-permute-done | bytes 131104 | tf_op jit(solution)/shard_map/ppermute | solution.py:318
  32.3 0.0 collective-permute-done.4.refs_6_
  32.3 0.0 copy-done.1
  32.3 1.3 %collective-permute-start.5 = (bf16[9,256,256]{2,1,0:T(8,128)(2,1)S(1)}, bf16[9,256,256]{2,1,0:T(8,128)(2,1)S(1)}, u32[]{:S(2)}, u32[]{:S(2)}) collective-permute-start(bf16[9,256,256]{2,1,0:T(8,128)(2,1)S(1)} %bitcast.16), channel_id=1, source_target_pairs={{16,0},{48,32},{80,64},{112,96},{144,128},{176,160},{208,192},{240... | collective-permute-start | bytes 3538952 | tf_op jit(solution)/shard_map/ppermute | solution.py:314
  33.6 0.7 collective-permute-start.6
  34.3 4.1 %back.3 = (bf16[3,1,4,256,256]{4,3,2,1,0:T(8,128)(2,1)}, bf16[256,256]{1,0:T(8,128)(2,1)S(1)}, bf16[2,256,256]{2,1,0:T(8,128)(2,1)S(1)}, bf16[256,256]{1,0:T(8,128)(2,1)S(1)}) custom-call(bf16[256,256]{1,0:T(8,128)(2,1)S(1)} %collective-permute-done.refs_0_, bf16[256,256]{1,0:T(8,128)(2,1)S(1)} %collective-permute-done.1.refs_1_, ...), custom_call_target="tpu_custom_call" | custom-call | flops 1 | bytes 1 | tf_op jit(solution)/shard_map/back/pallas_call | solution.py:161
  38.4 1.9 %collective-permute-start.2 = (bf16[256,256]{1,0:T(8,128)(2,1)S(1)}, bf16[256,256]{1,0:T(8,128)(2,1)S(1)}, u32[]{:S(2)}, u32[]{:S(2)}) collective-permute-start(bf16[256,256]{1,0:T(8,128)(2,1)S(1)} %get-tuple-element.69.refs_3_), channel_id=1, source_target_pairs={{0,1},{1,2},{2,3},{3,4},{4,5},{5,6},{6,7},{7,8},{8,9},{9,10},{10,1... | collective-permute-start | bytes 393224 | tf_op jit(solution)/shard_map/ppermute | solution.py:318
  40.4 6.6 %collective-permute-start.3 = (bf16[256,256]{1,0:T(8,128)(2,1)S(1)}, bf16[256,256]{1,0:T(8,128)(2,1)S(1)}, u32[]{:S(2)}, u32[]{:S(2)}) collective-permute-start(bf16[256,256]{1,0:T(8,128)(2,1)S(1)} %get-tuple-element.67.refs_1_), channel_id=1, source_target_pairs={{1,0},{2,1},{3,2},{4,3},{5,4},{6,5},{7,6},{8,7},{9,8},{10,9},{11,1... | collective-permute-start | bytes 393224 | tf_op jit(solution)/shard_map/ppermute | solution.py:319
  47.0 3.0 %weight.3.zero = bf16[4,4,9,16,256]{4,3,2,1,0:T(8,128)(2,1)S(1)} custom-call(bf16[256,256]{1,0:T(8,128)(2,1)S(1)} %collective-permute-done.refs_0_, bf16[256,256]{1,0:T(8,128)(2,1)S(1)} %collective-permute-done.1.refs_1_, bf16[1,4,256,256]{3,2,1,0:T(8,128)(2,1)} %refs_2_.3, bf16[3,1,4,256,256]{4,3,2,1,0:T(8,128)(2,1)} %refs_5_.5), custom_call_target="tpu_custom_call" | custom-call | flops 1 | bytes 1 | tf_op jit(solution)/shard_map/weight/pallas_call | solution.py:220
  50.0 0.0 collective-permute-done.2.refs_0_
  50.0 0.0 collective-permute-done.3.refs_4_
  50.0 0.0 collective-permute-done.6.refs_7_
  50.1 0.0 collective-permute-done.5.refs_5_
  50.1 3.8 %back.4 = (bf16[3,1,4,256,256]{4,3,2,1,0:T(8,128)(2,1)}, bf16[256,256]{1,0:T(8,128)(2,1)S(1)}, bf16[2,256,256]{2,1,0:T(8,128)(2,1)S(1)}, bf16[256,256]{1,0:T(8,128)(2,1)S(1)}, bf16[9,256,256]{2,1,0:T(8,128)(2,1)S(1)}) custom-call(bf16[256,256]{1,0:T(8,128)(2,1)S(1)} %collective-permute-done.2.refs_0_, ...), custom_call_target="tpu_custom_call", output_to_operand_aliasing={{0}: (10, {})} | custom-call | flops 1 | bytes 1 | tf_op jit(solution)/shard_map/back/pallas_call | solution.py:161
  53.8 2.9 %collective-permute-start.7 = (bf16[256,256]{1,0:T(8,128)(2,1)S(1)}, bf16[256,256]{1,0:T(8,128)(2,1)S(1)}, u32[]{:S(2)}, u32[]{:S(2)}) collective-permute-start(bf16[256,256]{1,0:T(8,128)(2,1)S(1)} %get-tuple-element.74.refs_3_), channel_id=1, source_target_pairs={{0,1},{1,2},{2,3},{3,4},{4,5},{5,6},{6,7},{7,8},{8,9},{9,10},{10,1... | collective-permute-start | bytes 393224 | tf_op jit(solution)/shard_map/ppermute | solution.py:318
  56.8 5.7 %collective-permute-start.8 = (bf16[256,256]{1,0:T(8,128)(2,1)S(1)}, bf16[256,256]{1,0:T(8,128)(2,1)S(1)}, u32[]{:S(2)}, u32[]{:S(2)}) collective-permute-start(bf16[256,256]{1,0:T(8,128)(2,1)S(1)} %get-tuple-element.72.refs_1_), channel_id=1, source_target_pairs={{1,0},{2,1},{3,2},{4,3},{5,4},{6,5},{7,6},{8,7},{9,8},{10,9},{11,1... | collective-permute-start | bytes 393224 | tf_op jit(solution)/shard_map/ppermute | solution.py:319
  62.5 2.9 %weight.4 = bf16[4,4,9,16,256]{4,3,2,1,0:T(8,128)(2,1)S(1)} custom-call(bf16[256,256]{1,0:T(8,128)(2,1)S(1)} %collective-permute-done.2.refs_0_, bf16[256,256]{1,0:T(8,128)(2,1)S(1)} %get-tuple-element.67.refs_1_, bf16[2,256,256]{2,1,0:T(8,128)(2,1)S(1)} %get-tuple-element.68.refs_2_, bf16[256,256]{1,0:T(8,128)(2,1)S(1)} %get-tuple-element.69.refs_3_, ...), custom_call_target="tpu_custom_call" | custom-call | flops 1 | bytes 1 | tf_op jit(solution)/shard_map/weight/pallas_call | solution.py:220
  65.4 0.0 collective-permute-done.7.refs_0_
  65.4 2.2 %collective-permute-done.8.refs_4_ = bf16[256,256]{1,0:T(8,128)(2,1)S(1)} collective-permute-done((bf16[256,256]{1,0:T(8,128)(2,1)S(1)}, bf16[256,256]{1,0:T(8,128)(2,1)S(1)}, u32[]{:S(2)}, u32[]{:S(2)}) %collective-permute-start.8) | collective-permute-done | bytes 131104 | tf_op jit(solution)/shard_map/ppermute | solution.py:319
  67.6 0.1 collective-permute-start.10
  67.7 0.8 collective-permute-start.9
  68.5 2.9 %weight.5.two = bf16[4,4,9,16,256]{4,3,2,1,0:T(8,128)(2,1)S(1)} custom-call(bf16[256,256]{1,0:T(8,128)(2,1)S(1)} %collective-permute-done.7.refs_0_, bf16[256,256]{1,0:T(8,128)(2,1)S(1)} %get-tuple-element.72.refs_1_, bf16[2,256,256]{2,1,0:T(8,128)(2,1)S(1)} %get-tuple-element.73.refs_2_, bf16[256,256]{1,0:T(8,128)(2,1)S(1)} %get-tuple-element.74.refs_3_, ...), custom_call_target="tpu_custom_call" | custom-call | flops 1 | bytes 1 | tf_op jit(solution)/shard_map/weight/pallas_call | solution.py:220
  71.4 0.0 collective-permute-done.10.other
  71.4 0.6 pair_kernel.1
  72.1 1.0 collective-permute-start.11
  73.1 0.3 collective-permute-start.12
  73.3 2.4 %collective-permute-start.13 = (bf16[4,9,16,256]{3,2,1,0:T(8,128)(2,1)S(1)}, bf16[4,9,16,256]{3,2,1,0:T(8,128)(2,1)S(1)}, u32[]{:S(2)}, u32[]{:S(2)}) collective-permute-start(bf16[4,9,16,256]{3,2,1,0:T(8,128)(2,1)S(1)} %get-tuple-element.82), channel_id=1, source_target_pairs={{0,12},{1,13},{2,14},{3,15},{4,0},{5,1},{6,2},{7,3},{8,4},{9,5},{1... | collective-permute-start | bytes 884744 | tf_op jit(solution)/shard_map/ppermute | solution.py:305
  75.7 0.0 collective-permute-start.17
  75.7 9.8 %collective-permute-done.11.one = bf16[4,9,16,256]{3,2,1,0:T(8,128)(2,1)S(1)} collective-permute-done((bf16[4,9,16,256]{3,2,1,0:T(8,128)(2,1)S(1)}, bf16[4,9,16,256]{3,2,1,0:T(8,128)(2,1)S(1)}, u32[]{:S(2)}, u32[]{:S(2)}) %collective-permute-start.11) | collective-permute-done | bytes 294944 | tf_op jit(solution)/shard_map/ppermute | solution.py:305
  85.5 0.0 collective-permute-start.18
  85.5 0.0 collective-permute-done.12.two
  85.5 5.0 %collective-permute-start.19 = (bf16[4,9,16,256]{3,2,1,0:T(8,128)(2,1)S(1)}, bf16[4,9,16,256]{3,2,1,0:T(8,128)(2,1)S(1)}, u32[]{:S(2)}, u32[]{:S(2)}) collective-permute-start(bf16[4,9,16,256]{3,2,1,0:T(8,128)(2,1)S(1)} %get-tuple-element.90), channel_id=1, source_target_pairs={{0,12},{1,13},{2,14},{3,15},{4,0},{5,1},{6,2},{7,3},{8,4},{9,5},{1... | collective-permute-start | bytes 884744 | tf_op jit(solution)/shard_map/ppermute | solution.py:305
  90.6 0.0 collective-permute-done.13.three
  90.6 0.1 regroup_kernel.2
  90.7 0.1 collective-permute-start.14
  90.8 3.9 %collective-permute-done.17.one = bf16[4,9,16,256]{3,2,1,0:T(8,128)(2,1)S(1)} collective-permute-done((bf16[4,9,16,256]{3,2,1,0:T(8,128)(2,1)S(1)}, bf16[4,9,16,256]{3,2,1,0:T(8,128)(2,1)S(1)}, u32[]{:S(2)}, u32[]{:S(2)}) %collective-permute-start.17) | collective-permute-done | bytes 294944 | tf_op jit(solution)/shard_map/ppermute | solution.py:305
  94.7 2.4 %collective-permute-done.18.two = bf16[4,9,16,256]{3,2,1,0:T(8,128)(2,1)S(1)} collective-permute-done((bf16[4,9,16,256]{3,2,1,0:T(8,128)(2,1)S(1)}, bf16[4,9,16,256]{3,2,1,0:T(8,128)(2,1)S(1)}, u32[]{:S(2)}, u32[]{:S(2)}) %collective-permute-start.18) | collective-permute-done | bytes 294944 | tf_op jit(solution)/shard_map/ppermute | solution.py:305
  97.1 4.3 %collective-permute-done.19.three = bf16[4,9,16,256]{3,2,1,0:T(8,128)(2,1)S(1)} collective-permute-done((bf16[4,9,16,256]{3,2,1,0:T(8,128)(2,1)S(1)}, bf16[4,9,16,256]{3,2,1,0:T(8,128)(2,1)S(1)}, u32[]{:S(2)}, u32[]{:S(2)}) %collective-permute-start.19) | collective-permute-done | bytes 294944 | tf_op jit(solution)/shard_map/ppermute | solution.py:305
  101.4 0.1 regroup_kernel.3
  101.6 1.4 %collective-permute-start.20 = (bf16[2,9,16,256]{3,2,1,0:T(8,128)(2,1)S(1)}, bf16[2,9,16,256]{3,2,1,0:T(8,128)(2,1)S(1)}, u32[]{:S(2)}, u32[]{:S(2)}) collective-permute-start(bf16[2,9,16,256]{3,2,1,0:T(8,128)(2,1)S(1)} %get-tuple-element.92), channel_id=1, source_target_pairs={{0,1},{1,0},{2,3},{3,2},{4,5},{5,4},{6,7},{7,6},{8,9},{9,8},{10,11... | collective-permute-start | bytes 442376 | tf_op jit(solution)/shard_map/ppermute | solution.py:305
  102.9 0.0 collective-permute-done.14.came
  103.0 3.6 %collective-permute-start.15 = (bf16[9,16,256]{2,1,0:T(8,128)(2,1)S(1)}, bf16[9,16,256]{2,1,0:T(8,128)(2,1)S(1)}, u32[]{:S(2)}, u32[]{:S(2)}) collective-permute-start(bf16[9,16,256]{2,1,0:T(8,128)(2,1)S(1)} %get-tuple-element.86), channel_id=1, source_target_pairs={{0,2},{1,3},{2,0},{3,1},{4,6},{5,7},{6,4},{7,5},{8,10},{9,11},{10,... | collective-permute-start | bytes 221192 | tf_op jit(solution)/shard_map/ppermute | solution.py:305
  106.6 0.0 collective-permute-done.9.refs_5_
  106.6 0.0 copy-start
  106.6 3.2 %back.5 = bf16[3,1,4,256,256]{4,3,2,1,0:T(8,128)(2,1)} custom-call(bf16[256,256]{1,0:T(8,128)(2,1)S(1)} %collective-permute-done.7.refs_0_, bf16[256,256]{1,0:T(8,128)(2,1)S(1)} %get-tuple-element.72.refs_1_, bf16[2,256,256]{2,1,0:T(8,128)(2,1)S(1)} %get-tuple-element.73.refs_2_, ...), custom_call_target="tpu_custom_call", output_to_operand_aliasing={{}: (7, {})} | custom-call | flops 1 | bytes 1 | tf_op jit(solution)/shard_map/back/pallas_call | solution.py:161
  109.8 0.0 collective-permute-done.20.came
  109.9 1.0 collective-permute-start.21
  110.8 0.0 collective-permute-done.15.came
  110.8 0.0 copy-done
  110.9 0.7 collective-permute-start.16
  111.6 6.1 %collective-permute-done.21.came = bf16[9,16,256]{2,1,0:T(8,128)(2,1)S(1)} collective-permute-done((bf16[9,16,256]{2,1,0:T(8,128)(2,1)S(1)}, bf16[9,16,256]{2,1,0:T(8,128)(2,1)S(1)}, u32[]{:S(2)}, u32[]{:S(2)}) %collective-permute-start.21) | collective-permute-done | bytes 73760 | tf_op jit(solution)/shard_map/ppermute | solution.py:305
  117.7 0.0 collective-permute-done.16.held
  117.7 0.7 finish_kernel.3
  (4 shorter events, 0.1 us)
Async XLA Ops:
  0.6 31.7 %copy-start.1 = (bf16[1,256,9,256]{3,1,2,0:T(8,128)(2,1)S(1)}, bf16[1,256,9,256]{3,1,2,0:T(8,128)(2,1)}, u32[]{:S(2)}) copy-start(bf16[1,256,9,256]{3,1,2,0:T(8,128)(2,1)} %param.5) | copy-start | bytes 3538948
  0.6 12.3 %copy-start.2 = (bf16[1,4,256,256]{3,2,1,0:T(8,128)(2,1)S(1)}, bf16[1,4,256,256]{3,2,1,0:T(8,128)(2,1)}, u32[]{:S(2)}) copy-start(bf16[1,4,256,256]{3,2,1,0:T(8,128)(2,1)} %refs_2_.3) | copy-start | bytes 1572868
  1.9 30.4 %collective-permute-start.4 = (bf16[9,128,256]{2,1,0:T(8,128)(2,1)S(1)}, bf16[9,128,256]{2,1,0:T(8,128)(2,1)S(1)}, u32[]{:S(2)}, u32[]{:S(2)}) collective-permute-start(bf16[9,128,256]{2,1,0:T(8,128)(2,1)S(1)} %half.1), channel_id=1, source_target_pairs={{0,240},{32,16},{64,48},{96,80},{128,112},{160,144},{192,176},{224... | collective-permute-start | bytes 1769480 | tf_op jit(solution)/shard_map/ppermute | solution.py:314
  12.9 17.9 %collective-permute-start.1 = (bf16[256,256]{1,0:T(8,128)(2,1)S(1)}, bf16[256,256]{1,0:T(8,128)(2,1)S(1)}, u32[]{:S(2)}, u32[]{:S(2)}) collective-permute-start(bf16[256,256]{1,0:T(8,128)(2,1)S(1)} %get-tuple-element.96), channel_id=1, source_target_pairs={{1,0},{2,1},{3,2},{4,3},{5,4},{6,5},{7,6},{8,7},{9,8},{10,9},{11,1... | collective-permute-start | bytes 393224 | tf_op jit(solution)/shard_map/ppermute | solution.py:319
  16.8 15.6 %collective-permute-start = (bf16[256,256]{1,0:T(8,128)(2,1)S(1)}, bf16[256,256]{1,0:T(8,128)(2,1)S(1)}, u32[]{:S(2)}, u32[]{:S(2)}) collective-permute-start(bf16[256,256]{1,0:T(8,128)(2,1)S(1)} %get-tuple-element.97), channel_id=1, source_target_pairs={{0,1},{1,2},{2,3},{3,4},{4,5},{5,6},{6,7},{7,8},{8,9},{9,10},{10,1... | collective-permute-start | bytes 393224 | tf_op jit(solution)/shard_map/ppermute | solution.py:318
  32.3 17.7 %collective-permute-start.5 = (bf16[9,256,256]{2,1,0:T(8,128)(2,1)S(1)}, bf16[9,256,256]{2,1,0:T(8,128)(2,1)S(1)}, u32[]{:S(2)}, u32[]{:S(2)}) collective-permute-start(bf16[9,256,256]{2,1,0:T(8,128)(2,1)S(1)} %bitcast.16), channel_id=1, source_target_pairs={{16,0},{48,32},{80,64},{112,96},{144,128},{176,160},{208,192},{240... | collective-permute-start | bytes 3538952 | tf_op jit(solution)/shard_map/ppermute | solution.py:314
  33.6 16.4 %collective-permute-start.6 = (bf16[9,128,256]{2,1,0:T(8,128)(2,1)S(1)}, bf16[9,128,256]{2,1,0:T(8,128)(2,1)S(1)}, u32[]{:S(2)}, u32[]{:S(2)}) collective-permute-start(bf16[9,128,256]{2,1,0:T(8,128)(2,1)S(1)} %collective-permute-done.4.refs_6_), channel_id=1, source_target_pairs={{16,20},{17,21},{18,22},{19,23},{20,16},{21,17},{22,18},{23,19},{2... | collective-permute-start | bytes 1769480 | tf_op jit(solution)/shard_map/ppermute | solution.py:310
  38.4 11.6 %collective-permute-start.2 = (bf16[256,256]{1,0:T(8,128)(2,1)S(1)}, bf16[256,256]{1,0:T(8,128)(2,1)S(1)}, u32[]{:S(2)}, u32[]{:S(2)}) collective-permute-start(bf16[256,256]{1,0:T(8,128)(2,1)S(1)} %get-tuple-element.69.refs_3_), channel_id=1, source_target_pairs={{0,1},{1,2},{2,3},{3,4},{4,5},{5,6},{6,7},{7,8},{8,9},{9,10},{10,1... | collective-permute-start | bytes 393224 | tf_op jit(solution)/shard_map/ppermute | solution.py:318
  40.4 9.7 %collective-permute-start.3 = (bf16[256,256]{1,0:T(8,128)(2,1)S(1)}, bf16[256,256]{1,0:T(8,128)(2,1)S(1)}, u32[]{:S(2)}, u32[]{:S(2)}) collective-permute-start(bf16[256,256]{1,0:T(8,128)(2,1)S(1)} %get-tuple-element.67.refs_1_), channel_id=1, source_target_pairs={{1,0},{2,1},{3,2},{4,3},{5,4},{6,5},{7,6},{8,7},{9,8},{10,9},{11,1... | collective-permute-start | bytes 393224 | tf_op jit(solution)/shard_map/ppermute | solution.py:319
  53.8 11.6 %collective-permute-start.7 = (bf16[256,256]{1,0:T(8,128)(2,1)S(1)}, bf16[256,256]{1,0:T(8,128)(2,1)S(1)}, u32[]{:S(2)}, u32[]{:S(2)}) collective-permute-start(bf16[256,256]{1,0:T(8,128)(2,1)S(1)} %get-tuple-element.74.refs_3_), channel_id=1, source_target_pairs={{0,1},{1,2},{2,3},{3,4},{4,5},{5,6},{6,7},{7,8},{8,9},{9,10},{10,1... | collective-permute-start | bytes 393224 | tf_op jit(solution)/shard_map/ppermute | solution.py:318
  56.8 10.9 %collective-permute-start.8 = (bf16[256,256]{1,0:T(8,128)(2,1)S(1)}, bf16[256,256]{1,0:T(8,128)(2,1)S(1)}, u32[]{:S(2)}, u32[]{:S(2)}) collective-permute-start(bf16[256,256]{1,0:T(8,128)(2,1)S(1)} %get-tuple-element.72.refs_1_), channel_id=1, source_target_pairs={{1,0},{2,1},{3,2},{4,3},{5,4},{6,5},{7,6},{8,7},{9,8},{10,9},{11,1... | collective-permute-start | bytes 393224 | tf_op jit(solution)/shard_map/ppermute | solution.py:319
  67.6 3.8 %collective-permute-start.10 = (bf16[4,4,9,16,256]{4,3,2,1,0:T(8,128)(2,1)S(1)}, bf16[4,4,9,16,256]{4,3,2,1,0:T(8,128)(2,1)S(1)}, u32[]{:S(2)}, u32[]{:S(2)}) collective-permute-start(bf16[4,4,9,16,256]{4,3,2,1,0:T(8,128)(2,1)S(1)} %weight.4), channel_id=1, source_target_pairs={{0,16},{16,0},{32,48},{48,32},{64,80},{80,64},{96,112},{112,96},{1... | collective-permute-start | bytes 3538952 | tf_op jit(solution)/shard_map/ppermute | solution.py:314
  67.7 38.8 %collective-permute-start.9 = (bf16[9,256,256]{2,1,0:T(8,128)(2,1)S(1)}, bf16[9,256,256]{2,1,0:T(8,128)(2,1)S(1)}, u32[]{:S(2)}, u32[]{:S(2)}) collective-permute-start(bf16[9,256,256]{2,1,0:T(8,128)(2,1)S(1)} %get-tuple-element.76), channel_id=1, source_target_pairs={{0,240},{16,0},{32,16},{48,32},{64,48},{80,64},{96,80},{112,96},{1... | collective-permute-start | bytes 3538952 | tf_op jit(solution)/shard_map/ppermute | solution.py:314
  72.1 13.4 %collective-permute-start.11 = (bf16[4,9,16,256]{3,2,1,0:T(8,128)(2,1)S(1)}, bf16[4,9,16,256]{3,2,1,0:T(8,128)(2,1)S(1)}, u32[]{:S(2)}, u32[]{:S(2)}) collective-permute-start(bf16[4,9,16,256]{3,2,1,0:T(8,128)(2,1)S(1)} %get-tuple-element.80), channel_id=1, source_target_pairs={{0,4},{1,5},{2,6},{3,7},{4,8},{5,9},{6,10},{7,11},{8,12},{9,13},{1... | collective-permute-start | bytes 884744 | tf_op jit(solution)/shard_map/ppermute | solution.py:305
  73.1 12.5 %collective-permute-start.12 = (bf16[4,9,16,256]{3,2,1,0:T(8,128)(2,1)S(1)}, bf16[4,9,16,256]{3,2,1,0:T(8,128)(2,1)S(1)}, u32[]{:S(2)}, u32[]{:S(2)}) collective-permute-start(bf16[4,9,16,256]{3,2,1,0:T(8,128)(2,1)S(1)} %get-tuple-element.81), channel_id=1, source_target_pairs={{0,8},{1,9},{2,10},{3,11},{4,12},{5,13},{6,14},{7,15},{8,0},{9,1},... | collective-permute-start | bytes 884744 | tf_op jit(solution)/shard_map/ppermute | solution.py:305
  73.3 17.2 %collective-permute-start.13 = (bf16[4,9,16,256]{3,2,1,0:T(8,128)(2,1)S(1)}, bf16[4,9,16,256]{3,2,1,0:T(8,128)(2,1)S(1)}, u32[]{:S(2)}, u32[]{:S(2)}) collective-permute-start(bf16[4,9,16,256]{3,2,1,0:T(8,128)(2,1)S(1)} %get-tuple-element.82), channel_id=1, source_target_pairs={{0,12},{1,13},{2,14},{3,15},{4,0},{5,1},{6,2},{7,3},{8,4},{9,5},{1... | collective-permute-start | bytes 884744 | tf_op jit(solution)/shard_map/ppermute | solution.py:305
  75.7 19.1 %collective-permute-start.17 = (bf16[4,9,16,256]{3,2,1,0:T(8,128)(2,1)S(1)}, bf16[4,9,16,256]{3,2,1,0:T(8,128)(2,1)S(1)}, u32[]{:S(2)}, u32[]{:S(2)}) collective-permute-start(bf16[4,9,16,256]{3,2,1,0:T(8,128)(2,1)S(1)} %get-tuple-element.88), channel_id=1, source_target_pairs={{0,4},{1,5},{2,6},{3,7},{4,8},{5,9},{6,10},{7,11},{8,12},{9,13},{1... | collective-permute-start | bytes 884744 | tf_op jit(solution)/shard_map/ppermute | solution.py:305
  85.5 11.6 %collective-permute-start.18 = (bf16[4,9,16,256]{3,2,1,0:T(8,128)(2,1)S(1)}, bf16[4,9,16,256]{3,2,1,0:T(8,128)(2,1)S(1)}, u32[]{:S(2)}, u32[]{:S(2)}) collective-permute-start(bf16[4,9,16,256]{3,2,1,0:T(8,128)(2,1)S(1)} %get-tuple-element.89), channel_id=1, source_target_pairs={{0,8},{1,9},{2,10},{3,11},{4,12},{5,13},{6,14},{7,15},{8,0},{9,1},... | collective-permute-start | bytes 884744 | tf_op jit(solution)/shard_map/ppermute | solution.py:305
  85.5 15.9 %collective-permute-start.19 = (bf16[4,9,16,256]{3,2,1,0:T(8,128)(2,1)S(1)}, bf16[4,9,16,256]{3,2,1,0:T(8,128)(2,1)S(1)}, u32[]{:S(2)}, u32[]{:S(2)}) collective-permute-start(bf16[4,9,16,256]{3,2,1,0:T(8,128)(2,1)S(1)} %get-tuple-element.90), channel_id=1, source_target_pairs={{0,12},{1,13},{2,14},{3,15},{4,0},{5,1},{6,2},{7,3},{8,4},{9,5},{1... | collective-permute-start | bytes 884744 | tf_op jit(solution)/shard_map/ppermute | solution.py:305
  90.7 12.2 %collective-permute-start.14 = (bf16[2,9,16,256]{3,2,1,0:T(8,128)(2,1)S(1)}, bf16[2,9,16,256]{3,2,1,0:T(8,128)(2,1)S(1)}, u32[]{:S(2)}, u32[]{:S(2)}) collective-permute-start(bf16[2,9,16,256]{3,2,1,0:T(8,128)(2,1)S(1)} %get-tuple-element.84), channel_id=1, source_target_pairs={{0,1},{1,0},{2,3},{3,2},{4,5},{5,4},{6,7},{7,6},{8,9},{9,8},{10,11... | collective-permute-start | bytes 442376 | tf_op jit(solution)/shard_map/ppermute | solution.py:305
  101.6 8.3 %collective-permute-start.20 = (bf16[2,9,16,256]{3,2,1,0:T(8,128)(2,1)S(1)}, bf16[2,9,16,256]{3,2,1,0:T(8,128)(2,1)S(1)}, u32[]{:S(2)}, u32[]{:S(2)}) collective-permute-start(bf16[2,9,16,256]{3,2,1,0:T(8,128)(2,1)S(1)} %get-tuple-element.92), channel_id=1, source_target_pairs={{0,1},{1,0},{2,3},{3,2},{4,5},{5,4},{6,7},{7,6},{8,9},{9,8},{10,11... | collective-permute-start | bytes 442376 | tf_op jit(solution)/shard_map/ppermute | solution.py:305
  103.0 7.9 %collective-permute-start.15 = (bf16[9,16,256]{2,1,0:T(8,128)(2,1)S(1)}, bf16[9,16,256]{2,1,0:T(8,128)(2,1)S(1)}, u32[]{:S(2)}, u32[]{:S(2)}) collective-permute-start(bf16[9,16,256]{2,1,0:T(8,128)(2,1)S(1)} %get-tuple-element.86), channel_id=1, source_target_pairs={{0,2},{1,3},{2,0},{3,1},{4,6},{5,7},{6,4},{7,5},{8,10},{9,11},{10,... | collective-permute-start | bytes 221192 | tf_op jit(solution)/shard_map/ppermute | solution.py:305
  106.6 4.3 %copy-start = (bf16[1,16,9,256]{3,1,2,0:T(8,128)(2,1)S(1)}, bf16[1,16,9,256]{3,1,2,0:T(8,128)(2,1)}, u32[]{:S(2)}) copy-start(bf16[1,16,9,256]{3,1,2,0:T(8,128)(2,1)} %param.6) | copy-start | bytes 221188
  109.9 7.9 %collective-permute-start.21 = (bf16[9,16,256]{2,1,0:T(8,128)(2,1)S(1)}, bf16[9,16,256]{2,1,0:T(8,128)(2,1)S(1)}, u32[]{:S(2)}, u32[]{:S(2)}) collective-permute-start(bf16[9,16,256]{2,1,0:T(8,128)(2,1)S(1)} %get-tuple-element.95), channel_id=1, source_target_pairs={{0,2},{1,3},{2,0},{3,1},{4,6},{5,7},{6,4},{7,5},{8,10},{9,11},{10,... | collective-permute-start | bytes 221192 | tf_op jit(solution)/shard_map/ppermute | solution.py:305
  110.9 6.9 %collective-permute-start.16 = (bf16[9,16,256]{2,1,0:T(8,128)(2,1)S(1)}, bf16[9,16,256]{2,1,0:T(8,128)(2,1)S(1)}, u32[]{:S(2)}, u32[]{:S(2)}) collective-permute-start(bf16[9,16,256]{2,1,0:T(8,128)(2,1)S(1)} %finish_kernel.2), channel_id=1, source_target_pairs={{0,224},{16,240},{32,0},{48,16},{64,32},{80,48},{96,64},{112,80},{... | collective-permute-start | bytes 221192 | tf_op jit(solution)/shard_map/ppermute | solution.py:314

commit v4 on v3

--- a/solution.py
+++ b/solution.py
@@ -310,6 +310,12 @@
     return lax.ppermute(value, ("blk", "rows"), pairs)
 
 
+def kernels_back(value, pairs):
+    places = [(x * 4 + z, x * 4 + 3 - z, x * 4 + z) for x in range(4) for z in range(4)]
+    moves = [(a * 16 + (far if a // 8 != b // 8 else here), b * 16 + there) for a, b in pairs for here, far, there in places]
+    return lax.ppermute(value, ("blk", "rows"), moves)
+
+
 def around(value, pairs):
     return lax.ppermute(value, "blk", pairs)
 
@@ -334,10 +340,6 @@
     shape = keep.shape[1:]
     keep, send = small(halve_kernel, [near(shape, F32), near(shape)], keep, came)
     return keep, along(send, lambda x, z: x * 4 + (z ^ 2))
-
-
-def summed_over_z(parts, held):
-    return rest_over_z(*part_over_z(parts, held))
 
 
 def shards(section_weights, grad_acc, saved_inputs, cotangent, fresh_grads):
@@ -356,7 +358,7 @@
     def weight(tick, edges):
         return weight_terms(tick, edges, cotangent, saved_inputs, scale)
 
-    half = around(half_of(kernel), [(b, (b - 1) % 16) for b in evens])
+    half = kernels_back(half_of(kernel), [(b, (b - 1) % 16) for b in evens])
     up, _, _, _, down = with_edges(image[0], None, image[height - 1])
     half, kernel_here = after((half, kernel), up, down)
     kernel_one = around(kernel_here, [(b + 1, b) for b in evens])
@@ -370,17 +372,19 @@
     sums_one = weight(1, after(edges_one, parts[0]))
     edges_two, used, sums_one = lax.optimization_barrier((edges_two, used, sums_one))
     other = around(sums_one, [(b, b ^ 1) for b in range(16)])
-    kernel_two = around(used, back_by(1))
+    kernel_two = kernels_back(used, back_by(1))
     sums_two = weight(2, edges_two)
     part = (4, *held.shape)
     spread = ([near(part, F32)] + [near(part)] * 3) * 2
     both = small(pair_kernel, spread, sums_zero, sums_two, other)
     first, last = over_x(both[:4]), over_x(both[4:])
-    early = small(finish_kernel, [near(held.shape)], held, *summed_over_z(first, held))
-    early = around(early[0], back_by(2))
+    keep, came = part_over_z(first, held)
+    (states,) = back(2, after(edges_two, keep), kernel_two, (), states)
+    keep, came = rest_over_z(keep, after(came, states))
+    last = after(last, keep)
+    (early,) = small(finish_kernel, [near(held.shape)], held, keep, came)
+    early = around(early, back_by(2))
     keep, came = part_over_z(last, held)
-    (states,) = back(2, edges_two, kernel_two, (), states)
-    came = after(came, states)
     (held,) = small(finish_kernel, [near(held.shape)], early, *rest_over_z(keep, came))
     return states, jnp.transpose(held, (1, 0, 2))[None]
 

time: 120 us -> 117 us (0.975)
  waiting for transfers between devices: 42.4 us -> 25.7 us
  starting transfers between devices: 52.3 us -> 67.1 us
    ppermute x0 -> x2, starting transfers between devices: none -> 15.7 us  [kernels_back(): return lax.ppermute(value, ('blk', 'rows'), moves)]
    ppermute x10, waiting for transfers between devices: 26.6 us -> 15 us  [along(): lax.ppermute(value, 'rows', [(x * 4 + z, move(x, z)) for x in range(4) fo...]
    ppermute x5 -> x3, starting transfers between devices: 13.9 us -> 6.14 us  [around(): return lax.ppermute(value, 'blk', pairs)]
    ppermute x3, waiting for transfers between devices: 14.3 us -> 6.77 us  [with_edges(): down = lax.ppermute(top, 'rows', [(i + 1, i) for i in range(15)])]
    ppermute x10, starting transfers between devices: 14.7 us -> 21.5 us  [along(): lax.ppermute(value, 'rows', [(x * 4 + z, move(x, z)) for x in range(4) fo...]
    ppermute x0 -> x2, waiting for transfers between devices: none -> 1.52 us  [kernels_back(): return lax.ppermute(value, ('blk', 'rows'), moves)]
  transfers between devices with their start and end apart: 22 -> 22, of which waited for: 8 -> 9; matrix products, arithmetic and copies ran while one was open for 0% -> 0% of each run, Pallas kernels for 15% -> 15%
where the time goes in v4:
time: 117 us
  starting transfers between devices  67.1 us (57%)
  waiting for transfers between devices  25.7 us (22%)
  Pallas kernels  22.8 us (19%)
    ppermute x10, starting transfers between devices, along(): lax.ppermute(value, 'rows', [(x * 4 + z, move(x, z)) for x in range(4) fo...  21.5 us
    ppermute x3, starting transfers between devices, with_edges(): down = lax.ppermute(top, 'rows', [(i + 1, i) for i in range(15)])  17.1 us
    ppermute x2, starting transfers between devices, kernels_back(): return lax.ppermute(value, ('blk', 'rows'), moves)  15.7 us
    ppermute x10, waiting for transfers between devices, along(): lax.ppermute(value, 'rows', [(x * 4 + z, move(x, z)) for x in range(4) fo...  15 us
    pallas_call x3, Pallas kernels, back_project(): pl.pallas_call(functools.partial(back_kernel, tick), out_shape=shapes, in...  11.1 us
    pallas_call x3, Pallas kernels, weight_terms(): pl.pallas_call(functools.partial(weight_kernel, tick, scale), out_shape=n...  8.84 us
    ppermute x3, waiting for transfers between devices, with_edges(): down = lax.ppermute(top, 'rows', [(i + 1, i) for i in range(15)])  6.77 us
    ppermute x3, starting transfers between devices, around(): return lax.ppermute(value, 'blk', pairs)  6.14 us
  transfers between devices with their start and end apart: 22, of which 9 were waited for; matrix products, arithmetic and copies ran while one was open for 0% of the time, Pallas kernels for 15%

profile of v4, /device:TPU:2, one launch (start us, length us, event | category | flops | bytes accessed | tf_op | source)
XLA Modules:
  0.0 116.5 jit_solution(9490005282615328395)
XLA Ops:
  0.6 0.0 copy-start.1
  0.6 0.0 copy-start.2
  0.7 1.2 %half.1 = bf16[9,128,256]{2,1,0:T(8,128)(2,1)S(1)} custom-call(bf16[9,256,256]{2,1,0:T(8,128)(2,1)} %bitcast.14), custom_call_target="tpu_custom_call" | custom-call | tf_op jit(solution)/shard_map/half/pallas_call | solution.py:244
  1.9 9.7 %collective-permute-start.4 = (bf16[9,128,256]{2,1,0:T(8,128)(2,1)S(1)}, bf16[9,128,256]{2,1,0:T(8,128)(2,1)S(1)}, u32[]{:S(2)}, u32[]{:S(2)}) collective-permute-start(bf16[9,128,256]{2,1,0:T(8,128)(2,1)S(1)} %half.1), channel_id=1, source_target_pairs={{3,240},{2,241},{1,242},{0,243},{7,244},{6,245},{5,246},{4,247},{1... | collective-permute-start | bytes 1769480 | tf_op jit(solution)/shard_map/ppermute | solution.py:316
  11.6 0.0 copy-done.2
  11.6 3.8 %collective-permute-start.1 = (bf16[256,256]{1,0:T(8,128)(2,1)S(1)}, bf16[256,256]{1,0:T(8,128)(2,1)S(1)}, u32[]{:S(2)}, u32[]{:S(2)}) collective-permute-start(bf16[256,256]{1,0:T(8,128)(2,1)S(1)} %get-tuple-element.114), channel_id=1, source_target_pairs={{1,0},{2,1},{3,2},{4,3},{5,4},{6,5},{7,6},{8,7},{9,8},{10,9},{11,1... | collective-permute-start | bytes 393224 | tf_op jit(solution)/shard_map/ppermute | solution.py:325
  15.4 2.1 %collective-permute-start = (bf16[256,256]{1,0:T(8,128)(2,1)S(1)}, bf16[256,256]{1,0:T(8,128)(2,1)S(1)}, u32[]{:S(2)}, u32[]{:S(2)}) collective-permute-start(bf16[256,256]{1,0:T(8,128)(2,1)S(1)} %get-tuple-element.115), channel_id=1, source_target_pairs={{0,1},{1,2},{2,3},{3,4},{4,5},{5,6},{6,7},{7,8},{8,9},{9,10},{10,1... | collective-permute-start | bytes 393224 | tf_op jit(solution)/shard_map/ppermute | solution.py:324
  17.5 6.2 %collective-permute-done.1.refs_1_ = bf16[256,256]{1,0:T(8,128)(2,1)S(1)} collective-permute-done((bf16[256,256]{1,0:T(8,128)(2,1)S(1)}, bf16[256,256]{1,0:T(8,128)(2,1)S(1)}, u32[]{:S(2)}, u32[]{:S(2)}) %collective-permute-start.1) | collective-permute-done | bytes 131104 | tf_op jit(solution)/shard_map/ppermute | solution.py:325
  23.7 2.4 %collective-permute-done.refs_0_ = bf16[256,256]{1,0:T(8,128)(2,1)S(1)} collective-permute-done((bf16[256,256]{1,0:T(8,128)(2,1)S(1)}, bf16[256,256]{1,0:T(8,128)(2,1)S(1)}, u32[]{:S(2)}, u32[]{:S(2)}) %collective-permute-start) | collective-permute-done | bytes 131104 | tf_op jit(solution)/shard_map/ppermute | solution.py:324
  26.1 0.0 collective-permute-done.4.refs_6_
  26.1 0.0 copy-done.1
  26.1 1.3 %collective-permute-start.5 = (bf16[9,256,256]{2,1,0:T(8,128)(2,1)S(1)}, bf16[9,256,256]{2,1,0:T(8,128)(2,1)S(1)}, u32[]{:S(2)}, u32[]{:S(2)}) collective-permute-start(bf16[9,256,256]{2,1,0:T(8,128)(2,1)S(1)} %bitcast.16), channel_id=1, source_target_pairs={{16,0},{48,32},{80,64},{112,96},{144,128},{176,160},{208,192},{240... | collective-permute-start | bytes 3538952 | tf_op jit(solution)/shard_map/ppermute | solution.py:320
  27.4 0.7 collective-permute-start.6
  28.1 4.1 %back.3 = (bf16[3,1,4,256,256]{4,3,2,1,0:T(8,128)(2,1)}, bf16[256,256]{1,0:T(8,128)(2,1)S(1)}, bf16[2,256,256]{2,1,0:T(8,128)(2,1)S(1)}, bf16[256,256]{1,0:T(8,128)(2,1)S(1)}) custom-call(bf16[256,256]{1,0:T(8,128)(2,1)S(1)} %collective-permute-done.refs_0_, bf16[256,256]{1,0:T(8,128)(2,1)S(1)} %collective-permute-done.1.refs_1_, ...), custom_call_target="tpu_custom_call" | custom-call | flops 1 | bytes 1 | tf_op jit(solution)/shard_map/back/pallas_call | solution.py:161
  32.2 1.9 %collective-permute-start.2 = (bf16[256,256]{1,0:T(8,128)(2,1)S(1)}, bf16[256,256]{1,0:T(8,128)(2,1)S(1)}, u32[]{:S(2)}, u32[]{:S(2)}) collective-permute-start(bf16[256,256]{1,0:T(8,128)(2,1)S(1)} %get-tuple-element.78.refs_3_), channel_id=1, source_target_pairs={{0,1},{1,2},{2,3},{3,4},{4,5},{5,6},{6,7},{7,8},{8,9},{9,10},{10,1... | collective-permute-start | bytes 393224 | tf_op jit(solution)/shard_map/ppermute | solution.py:324
  34.1 6.6 %collective-permute-start.3 = (bf16[256,256]{1,0:T(8,128)(2,1)S(1)}, bf16[256,256]{1,0:T(8,128)(2,1)S(1)}, u32[]{:S(2)}, u32[]{:S(2)}) collective-permute-start(bf16[256,256]{1,0:T(8,128)(2,1)S(1)} %get-tuple-element.76.refs_1_), channel_id=1, source_target_pairs={{1,0},{2,1},{3,2},{4,3},{5,4},{6,5},{7,6},{8,7},{9,8},{10,9},{11,1... | collective-permute-start | bytes 393224 | tf_op jit(solution)/shard_map/ppermute | solution.py:325
  40.8 3.0 %weight.3.zero = bf16[4,4,9,16,256]{4,3,2,1,0:T(8,128)(2,1)S(1)} custom-call(bf16[256,256]{1,0:T(8,128)(2,1)S(1)} %collective-permute-done.refs_0_, bf16[256,256]{1,0:T(8,128)(2,1)S(1)} %collective-permute-done.1.refs_1_, bf16[1,4,256,256]{3,2,1,0:T(8,128)(2,1)} %refs_2_.3, bf16[3,1,4,256,256]{4,3,2,1,0:T(8,128)(2,1)} %refs_6_.1), custom_call_target="tpu_custom_call" | custom-call | flops 1 | bytes 1 | tf_op jit(solution)/shard_map/weight/pallas_call | solution.py:220
  43.8 0.0 collective-permute-done.2.refs_0_
  43.8 0.0 collective-permute-done.3.refs_4_
  43.8 0.0 collective-permute-done.6.refs_7_
  43.8 0.0 collective-permute-done.5.refs_5_
  43.8 3.8 %back.4 = (bf16[3,1,4,256,256]{4,3,2,1,0:T(8,128)(2,1)}, bf16[256,256]{1,0:T(8,128)(2,1)S(1)}, bf16[2,256,256]{2,1,0:T(8,128)(2,1)S(1)}, bf16[256,256]{1,0:T(8,128)(2,1)S(1)}, bf16[9,256,256]{2,1,0:T(8,128)(2,1)S(1)}) custom-call(bf16[256,256]{1,0:T(8,128)(2,1)S(1)} %collective-permute-done.2.refs_0_, ...), custom_call_target="tpu_custom_call", output_to_operand_aliasing={{0}: (10, {})} | custom-call | flops 1 | bytes 1 | tf_op jit(solution)/shard_map/back/pallas_call | solution.py:161
  47.6 1.9 %collective-permute-start.7 = (bf16[256,256]{1,0:T(8,128)(2,1)S(1)}, bf16[256,256]{1,0:T(8,128)(2,1)S(1)}, u32[]{:S(2)}, u32[]{:S(2)}) collective-permute-start(bf16[256,256]{1,0:T(8,128)(2,1)S(1)} %get-tuple-element.94.refs_3_), channel_id=1, source_target_pairs={{0,1},{1,2},{2,3},{3,4},{4,5},{5,6},{6,7},{7,8},{8,9},{9,10},{10,1... | collective-permute-start | bytes 393224 | tf_op jit(solution)/shard_map/ppermute | solution.py:324
  49.5 6.7 %collective-permute-start.8 = (bf16[256,256]{1,0:T(8,128)(2,1)S(1)}, bf16[256,256]{1,0:T(8,128)(2,1)S(1)}, u32[]{:S(2)}, u32[]{:S(2)}) collective-permute-start(bf16[256,256]{1,0:T(8,128)(2,1)S(1)} %get-tuple-element.92.refs_1_), channel_id=1, source_target_pairs={{1,0},{2,1},{3,2},{4,3},{5,4},{6,5},{7,6},{8,7},{9,8},{10,9},{11,1... | collective-permute-start | bytes 393224 | tf_op jit(solution)/shard_map/ppermute | solution.py:325
  56.2 2.9 %weight.4 = bf16[4,4,9,16,256]{4,3,2,1,0:T(8,128)(2,1)S(1)} custom-call(bf16[256,256]{1,0:T(8,128)(2,1)S(1)} %collective-permute-done.2.refs_0_, bf16[256,256]{1,0:T(8,128)(2,1)S(1)} %get-tuple-element.76.refs_1_, bf16[2,256,256]{2,1,0:T(8,128)(2,1)S(1)} %get-tuple-element.77.refs_2_, bf16[256,256]{1,0:T(8,128)(2,1)S(1)} %get-tuple-element.78.refs_3_, ...), custom_call_target="tpu_custom_call" | custom-call | flops 1 | bytes 1 | tf_op jit(solution)/shard_map/weight/pallas_call | solution.py:220
  59.2 0.0 collective-permute-done.7.refs_0_
  59.2 0.6 collective-permute-done.8.refs_4_
  59.7 0.7 collective-permute-start.9
  60.5 6.0 %collective-permute-start.13 = (bf16[9,256,256]{2,1,0:T(8,128)(2,1)S(1)}, bf16[9,256,256]{2,1,0:T(8,128)(2,1)S(1)}, u32[]{:S(2)}, u32[]{:S(2)}) collective-permute-start(bf16[9,256,256]{2,1,0:T(8,128)(2,1)S(1)} %get-tuple-element.96), channel_id=1, source_target_pairs={{3,240},{2,241},{1,242},{0,243},{7,244},{6,245},{5,246},{4,247},{1... | collective-permute-start | bytes 3538952 | tf_op jit(solution)/shard_map/ppermute | solution.py:316
  66.5 2.9 %weight.5.two = bf16[4,4,9,16,256]{4,3,2,1,0:T(8,128)(2,1)S(1)} custom-call(bf16[256,256]{1,0:T(8,128)(2,1)S(1)} %collective-permute-done.7.refs_0_, bf16[256,256]{1,0:T(8,128)(2,1)S(1)} %get-tuple-element.92.refs_1_, bf16[2,256,256]{2,1,0:T(8,128)(2,1)S(1)} %get-tuple-element.93.refs_2_, bf16[256,256]{1,0:T(8,128)(2,1)S(1)} %get-tuple-element.94.refs_3_, ...), custom_call_target="tpu_custom_call" | custom-call | flops 1 | bytes 1 | tf_op jit(solution)/shard_map/weight/pallas_call | solution.py:220
  69.4 0.0 collective-permute-done.9.other
  69.4 0.6 pair_kernel.1
  70.1 0.9 collective-permute-start.10
  71.0 1.1 collective-permute-start.11
  72.1 1.2 %collective-permute-start.12 = (bf16[4,9,16,256]{3,2,1,0:T(8,128)(2,1)S(1)}, bf16[4,9,16,256]{3,2,1,0:T(8,128)(2,1)S(1)}, u32[]{:S(2)}, u32[]{:S(2)}) collective-permute-start(bf16[4,9,16,256]{3,2,1,0:T(8,128)(2,1)S(1)} %get-tuple-element.89), channel_id=1, source_target_pairs={{0,12},{1,13},{2,14},{3,15},{4,0},{5,1},{6,2},{7,3},{8,4},{9,5},{1... | collective-permute-start | bytes 884744 | tf_op jit(solution)/shard_map/ppermute | solution.py:305
  73.3 0.8 collective-permute-start.17
  74.1 5.8 %collective-permute-done.10.one = bf16[4,9,16,256]{3,2,1,0:T(8,128)(2,1)S(1)} collective-permute-done((bf16[4,9,16,256]{3,2,1,0:T(8,128)(2,1)S(1)}, bf16[4,9,16,256]{3,2,1,0:T(8,128)(2,1)S(1)}, u32[]{:S(2)}, u32[]{:S(2)}) %collective-permute-start.10) | collective-permute-done | bytes 294944 | tf_op jit(solution)/shard_map/ppermute | solution.py:305
  79.9 3.2 %collective-permute-start.18 = (bf16[4,9,16,256]{3,2,1,0:T(8,128)(2,1)S(1)}, bf16[4,9,16,256]{3,2,1,0:T(8,128)(2,1)S(1)}, u32[]{:S(2)}, u32[]{:S(2)}) collective-permute-start(bf16[4,9,16,256]{3,2,1,0:T(8,128)(2,1)S(1)} %get-tuple-element.104), channel_id=1, source_target_pairs={{0,8},{1,9},{2,10},{3,11},{4,12},{5,13},{6,14},{7,15},{8,0},{9,1},... | collective-permute-start | bytes 884744 | tf_op jit(solution)/shard_map/ppermute | solution.py:305
  83.1 0.0 collective-permute-done.11.two
  83.1 6.6 %collective-permute-start.19 = (bf16[4,9,16,256]{3,2,1,0:T(8,128)(2,1)S(1)}, bf16[4,9,16,256]{3,2,1,0:T(8,128)(2,1)S(1)}, u32[]{:S(2)}, u32[]{:S(2)}) collective-permute-start(bf16[4,9,16,256]{3,2,1,0:T(8,128)(2,1)S(1)} %get-tuple-element.105), channel_id=1, source_target_pairs={{0,12},{1,13},{2,14},{3,15},{4,0},{5,1},{6,2},{7,3},{8,4},{9,5},{1... | collective-permute-start | bytes 884744 | tf_op jit(solution)/shard_map/ppermute | solution.py:305
  89.7 0.0 collective-permute-done.12.three
  89.8 0.1 regroup_kernel.2
  89.9 0.1 collective-permute-start.14
  90.0 1.5 %collective-permute-done.13.refs_5_ = bf16[9,256,256]{2,1,0:T(8,128)(2,1)S(1)} collective-permute-done((bf16[9,256,256]{2,1,0:T(8,128)(2,1)S(1)}, bf16[9,256,256]{2,1,0:T(8,128)(2,1)S(1)}, u32[]{:S(2)}, u32[]{:S(2)}) %collective-permute-start.13) | collective-permute-done | bytes 1179680 | tf_op jit(solution)/shard_map/ppermute | solution.py:316
  91.5 3.2 %back.5 = bf16[3,1,4,256,256]{4,3,2,1,0:T(8,128)(2,1)} custom-call(bf16[256,256]{1,0:T(8,128)(2,1)S(1)} %collective-permute-done.7.refs_0_, bf16[256,256]{1,0:T(8,128)(2,1)S(1)} %get-tuple-element.92.refs_1_, bf16[2,256,256]{2,1,0:T(8,128)(2,1)S(1)} %get-tuple-element.93.refs_2_, ...), custom_call_target="tpu_custom_call", output_to_operand_aliasing={{}: (7, {})} | custom-call | flops 1 | bytes 1 | tf_op jit(solution)/shard_map/back/pallas_call | solution.py:161
  94.7 0.0 copy-start
  94.7 0.4 collective-permute-done.14.came
  95.2 0.0 collective-permute-done.17.one
  95.2 0.0 collective-permute-done.18.two
  95.2 0.1 collective-permute-done.19.three
  95.2 0.1 regroup_kernel.3
  95.4 1.1 collective-permute-start.20
  96.5 3.5 %collective-permute-start.15 = (bf16[9,16,256]{2,1,0:T(8,128)(2,1)S(1)}, bf16[9,16,256]{2,1,0:T(8,128)(2,1)S(1)}, u32[]{:S(2)}, u32[]{:S(2)}) collective-permute-start(bf16[9,16,256]{2,1,0:T(8,128)(2,1)S(1)} %get-tuple-element.101), channel_id=1, source_target_pairs={{0,2},{1,3},{2,0},{3,1},{4,6},{5,7},{6,4},{7,5},{8,10},{9,11},{10,... | collective-permute-start | bytes 221192 | tf_op jit(solution)/shard_map/ppermute | solution.py:305
  100.0 3.1 %collective-permute-done.15.came = bf16[9,16,256]{2,1,0:T(8,128)(2,1)S(1)} collective-permute-done((bf16[9,16,256]{2,1,0:T(8,128)(2,1)S(1)}, bf16[9,16,256]{2,1,0:T(8,128)(2,1)S(1)}, u32[]{:S(2)}, u32[]{:S(2)}) %collective-permute-start.15) | collective-permute-done | bytes 73760 | tf_op jit(solution)/shard_map/ppermute | solution.py:305
  103.0 0.0 copy-done
  103.1 4.1 %collective-permute-start.16 = (bf16[9,16,256]{2,1,0:T(8,128)(2,1)S(1)}, bf16[9,16,256]{2,1,0:T(8,128)(2,1)S(1)}, u32[]{:S(2)}, u32[]{:S(2)}) collective-permute-start(bf16[9,16,256]{2,1,0:T(8,128)(2,1)S(1)} %finish_kernel.2), channel_id=1, source_target_pairs={{0,224},{16,240},{32,0},{48,16},{64,32},{80,48},{96,64},{112,80},{... | collective-permute-start | bytes 221192 | tf_op jit(solution)/shard_map/ppermute | solution.py:320
  107.2 0.0 collective-permute-done.20.came
  107.3 3.0 %collective-permute-start.21 = (bf16[9,16,256]{2,1,0:T(8,128)(2,1)S(1)}, bf16[9,16,256]{2,1,0:T(8,128)(2,1)S(1)}, u32[]{:S(2)}, u32[]{:S(2)}) collective-permute-start(bf16[9,16,256]{2,1,0:T(8,128)(2,1)S(1)} %get-tuple-element.113), channel_id=1, source_target_pairs={{0,2},{1,3},{2,0},{3,1},{4,6},{5,7},{6,4},{7,5},{8,10},{9,11},{10,... | collective-permute-start | bytes 221192 | tf_op jit(solution)/shard_map/ppermute | solution.py:305
  110.2 0.0 collective-permute-done.16.held
  110.2 5.7 %collective-permute-done.21.came = bf16[9,16,256]{2,1,0:T(8,128)(2,1)S(1)} collective-permute-done((bf16[9,16,256]{2,1,0:T(8,128)(2,1)S(1)}, bf16[9,16,256]{2,1,0:T(8,128)(2,1)S(1)}, u32[]{:S(2)}, u32[]{:S(2)}) %collective-permute-start.21) | collective-permute-done | bytes 73760 | tf_op jit(solution)/shard_map/ppermute | solution.py:305
  115.9 0.7 finish_kernel.3
  (4 shorter events, 0.1 us)
Async XLA Ops:
  0.6 25.4 %copy-start.1 = (bf16[1,256,9,256]{3,1,2,0:T(8,128)(2,1)S(1)}, bf16[1,256,9,256]{3,1,2,0:T(8,128)(2,1)}, u32[]{:S(2)}) copy-start(bf16[1,256,9,256]{3,1,2,0:T(8,128)(2,1)} %param.5) | copy-start | bytes 3538948
  0.6 10.9 %copy-start.2 = (bf16[1,4,256,256]{3,2,1,0:T(8,128)(2,1)S(1)}, bf16[1,4,256,256]{3,2,1,0:T(8,128)(2,1)}, u32[]{:S(2)}) copy-start(bf16[1,4,256,256]{3,2,1,0:T(8,128)(2,1)} %refs_2_.3) | copy-start | bytes 1572868
  1.9 24.2 %collective-permute-start.4 = (bf16[9,128,256]{2,1,0:T(8,128)(2,1)S(1)}, bf16[9,128,256]{2,1,0:T(8,128)(2,1)S(1)}, u32[]{:S(2)}, u32[]{:S(2)}) collective-permute-start(bf16[9,128,256]{2,1,0:T(8,128)(2,1)S(1)} %half.1), channel_id=1, source_target_pairs={{3,240},{2,241},{1,242},{0,243},{7,244},{6,245},{5,246},{4,247},{1... | collective-permute-start | bytes 1769480 | tf_op jit(solution)/shard_map/ppermute | solution.py:316
  11.6 12.0 %collective-permute-start.1 = (bf16[256,256]{1,0:T(8,128)(2,1)S(1)}, bf16[256,256]{1,0:T(8,128)(2,1)S(1)}, u32[]{:S(2)}, u32[]{:S(2)}) collective-permute-start(bf16[256,256]{1,0:T(8,128)(2,1)S(1)} %get-tuple-element.114), channel_id=1, source_target_pairs={{1,0},{2,1},{3,2},{4,3},{5,4},{6,5},{7,6},{8,7},{9,8},{10,9},{11,1... | collective-permute-start | bytes 393224 | tf_op jit(solution)/shard_map/ppermute | solution.py:325
  15.4 10.7 %collective-permute-start = (bf16[256,256]{1,0:T(8,128)(2,1)S(1)}, bf16[256,256]{1,0:T(8,128)(2,1)S(1)}, u32[]{:S(2)}, u32[]{:S(2)}) collective-permute-start(bf16[256,256]{1,0:T(8,128)(2,1)S(1)} %get-tuple-element.115), channel_id=1, source_target_pairs={{0,1},{1,2},{2,3},{3,4},{4,5},{5,6},{6,7},{7,8},{8,9},{9,10},{10,1... | collective-permute-start | bytes 393224 | tf_op jit(solution)/shard_map/ppermute | solution.py:324
  26.1 17.7 %collective-permute-start.5 = (bf16[9,256,256]{2,1,0:T(8,128)(2,1)S(1)}, bf16[9,256,256]{2,1,0:T(8,128)(2,1)S(1)}, u32[]{:S(2)}, u32[]{:S(2)}) collective-permute-start(bf16[9,256,256]{2,1,0:T(8,128)(2,1)S(1)} %bitcast.16), channel_id=1, source_target_pairs={{16,0},{48,32},{80,64},{112,96},{144,128},{176,160},{208,192},{240... | collective-permute-start | bytes 3538952 | tf_op jit(solution)/shard_map/ppermute | solution.py:320
  27.4 16.4 %collective-permute-start.6 = (bf16[9,128,256]{2,1,0:T(8,128)(2,1)S(1)}, bf16[9,128,256]{2,1,0:T(8,128)(2,1)S(1)}, u32[]{:S(2)}, u32[]{:S(2)}) collective-permute-start(bf16[9,128,256]{2,1,0:T(8,128)(2,1)S(1)} %collective-permute-done.4.refs_6_), channel_id=1, source_target_pairs={{16,20},{17,21},{18,22},{19,23},{20,16},{21,17},{22,18},{23,19},{2... | collective-permute-start | bytes 1769480 | tf_op jit(solution)/shard_map/ppermute | solution.py:310
  32.2 11.6 %collective-permute-start.2 = (bf16[256,256]{1,0:T(8,128)(2,1)S(1)}, bf16[256,256]{1,0:T(8,128)(2,1)S(1)}, u32[]{:S(2)}, u32[]{:S(2)}) collective-permute-start(bf16[256,256]{1,0:T(8,128)(2,1)S(1)} %get-tuple-element.78.refs_3_), channel_id=1, source_target_pairs={{0,1},{1,2},{2,3},{3,4},{4,5},{5,6},{6,7},{7,8},{8,9},{9,10},{10,1... | collective-permute-start | bytes 393224 | tf_op jit(solution)/shard_map/ppermute | solution.py:324
  34.1 9.7 %collective-permute-start.3 = (bf16[256,256]{1,0:T(8,128)(2,1)S(1)}, bf16[256,256]{1,0:T(8,128)(2,1)S(1)}, u32[]{:S(2)}, u32[]{:S(2)}) collective-permute-start(bf16[256,256]{1,0:T(8,128)(2,1)S(1)} %get-tuple-element.76.refs_1_), channel_id=1, source_target_pairs={{1,0},{2,1},{3,2},{4,3},{5,4},{6,5},{7,6},{8,7},{9,8},{10,9},{11,1... | collective-permute-start | bytes 393224 | tf_op jit(solution)/shard_map/ppermute | solution.py:325
  47.6 11.6 %collective-permute-start.7 = (bf16[256,256]{1,0:T(8,128)(2,1)S(1)}, bf16[256,256]{1,0:T(8,128)(2,1)S(1)}, u32[]{:S(2)}, u32[]{:S(2)}) collective-permute-start(bf16[256,256]{1,0:T(8,128)(2,1)S(1)} %get-tuple-element.94.refs_3_), channel_id=1, source_target_pairs={{0,1},{1,2},{2,3},{3,4},{4,5},{5,6},{6,7},{7,8},{8,9},{9,10},{10,1... | collective-permute-start | bytes 393224 | tf_op jit(solution)/shard_map/ppermute | solution.py:324
  49.5 10.2 %collective-permute-start.8 = (bf16[256,256]{1,0:T(8,128)(2,1)S(1)}, bf16[256,256]{1,0:T(8,128)(2,1)S(1)}, u32[]{:S(2)}, u32[]{:S(2)}) collective-permute-start(bf16[256,256]{1,0:T(8,128)(2,1)S(1)} %get-tuple-element.92.refs_1_), channel_id=1, source_target_pairs={{1,0},{2,1},{3,2},{4,3},{5,4},{6,5},{7,6},{8,7},{9,8},{10,9},{11,1... | collective-permute-start | bytes 393224 | tf_op jit(solution)/shard_map/ppermute | solution.py:325
  59.7 9.7 %collective-permute-start.9 = (bf16[4,4,9,16,256]{4,3,2,1,0:T(8,128)(2,1)S(1)}, bf16[4,4,9,16,256]{4,3,2,1,0:T(8,128)(2,1)S(1)}, u32[]{:S(2)}, u32[]{:S(2)}) collective-permute-start(bf16[4,4,9,16,256]{4,3,2,1,0:T(8,128)(2,1)S(1)} %weight.4), channel_id=1, source_target_pairs={{0,16},{16,0},{32,48},{48,32},{64,80},{80,64},{96,112},{112,96},{1... | collective-permute-start | bytes 3538952 | tf_op jit(solution)/shard_map/ppermute | solution.py:320
  60.5 31.0 %collective-permute-start.13 = (bf16[9,256,256]{2,1,0:T(8,128)(2,1)S(1)}, bf16[9,256,256]{2,1,0:T(8,128)(2,1)S(1)}, u32[]{:S(2)}, u32[]{:S(2)}) collective-permute-start(bf16[9,256,256]{2,1,0:T(8,128)(2,1)S(1)} %get-tuple-element.96), channel_id=1, source_target_pairs={{3,240},{2,241},{1,242},{0,243},{7,244},{6,245},{5,246},{4,247},{1... | collective-permute-start | bytes 3538952 | tf_op jit(solution)/shard_map/ppermute | solution.py:316
  70.1 9.8 %collective-permute-start.10 = (bf16[4,9,16,256]{3,2,1,0:T(8,128)(2,1)S(1)}, bf16[4,9,16,256]{3,2,1,0:T(8,128)(2,1)S(1)}, u32[]{:S(2)}, u32[]{:S(2)}) collective-permute-start(bf16[4,9,16,256]{3,2,1,0:T(8,128)(2,1)S(1)} %get-tuple-element.87), channel_id=1, source_target_pairs={{0,4},{1,5},{2,6},{3,7},{4,8},{5,9},{6,10},{7,11},{8,12},{9,13},{1... | collective-permute-start | bytes 884744 | tf_op jit(solution)/shard_map/ppermute | solution.py:305
  71.0 12.2 %collective-permute-start.11 = (bf16[4,9,16,256]{3,2,1,0:T(8,128)(2,1)S(1)}, bf16[4,9,16,256]{3,2,1,0:T(8,128)(2,1)S(1)}, u32[]{:S(2)}, u32[]{:S(2)}) collective-permute-start(bf16[4,9,16,256]{3,2,1,0:T(8,128)(2,1)S(1)} %get-tuple-element.88), channel_id=1, source_target_pairs={{0,8},{1,9},{2,10},{3,11},{4,12},{5,13},{6,14},{7,15},{8,0},{9,1},... | collective-permute-start | bytes 884744 | tf_op jit(solution)/shard_map/ppermute | solution.py:305
  72.1 17.7 %collective-permute-start.12 = (bf16[4,9,16,256]{3,2,1,0:T(8,128)(2,1)S(1)}, bf16[4,9,16,256]{3,2,1,0:T(8,128)(2,1)S(1)}, u32[]{:S(2)}, u32[]{:S(2)}) collective-permute-start(bf16[4,9,16,256]{3,2,1,0:T(8,128)(2,1)S(1)} %get-tuple-element.89), channel_id=1, source_target_pairs={{0,12},{1,13},{2,14},{3,15},{4,0},{5,1},{6,2},{7,3},{8,4},{9,5},{1... | collective-permute-start | bytes 884744 | tf_op jit(solution)/shard_map/ppermute | solution.py:305
  73.3 21.8 %collective-permute-start.17 = (bf16[4,9,16,256]{3,2,1,0:T(8,128)(2,1)S(1)}, bf16[4,9,16,256]{3,2,1,0:T(8,128)(2,1)S(1)}, u32[]{:S(2)}, u32[]{:S(2)}) collective-permute-start(bf16[4,9,16,256]{3,2,1,0:T(8,128)(2,1)S(1)} %get-tuple-element.103), channel_id=1, source_target_pairs={{0,4},{1,5},{2,6},{3,7},{4,8},{5,9},{6,10},{7,11},{8,12},{9,13},{1... | collective-permute-start | bytes 884744 | tf_op jit(solution)/shard_map/ppermute | solution.py:305
  79.9 15.2 %collective-permute-start.18 = (bf16[4,9,16,256]{3,2,1,0:T(8,128)(2,1)S(1)}, bf16[4,9,16,256]{3,2,1,0:T(8,128)(2,1)S(1)}, u32[]{:S(2)}, u32[]{:S(2)}) collective-permute-start(bf16[4,9,16,256]{3,2,1,0:T(8,128)(2,1)S(1)} %get-tuple-element.104), channel_id=1, source_target_pairs={{0,8},{1,9},{2,10},{3,11},{4,12},{5,13},{6,14},{7,15},{8,0},{9,1},... | collective-permute-start | bytes 884744 | tf_op jit(solution)/shard_map/ppermute | solution.py:305
  83.1 12.1 %collective-permute-start.19 = (bf16[4,9,16,256]{3,2,1,0:T(8,128)(2,1)S(1)}, bf16[4,9,16,256]{3,2,1,0:T(8,128)(2,1)S(1)}, u32[]{:S(2)}, u32[]{:S(2)}) collective-permute-start(bf16[4,9,16,256]{3,2,1,0:T(8,128)(2,1)S(1)} %get-tuple-element.105), channel_id=1, source_target_pairs={{0,12},{1,13},{2,14},{3,15},{4,0},{5,1},{6,2},{7,3},{8,4},{9,5},{1... | collective-permute-start | bytes 884744 | tf_op jit(solution)/shard_map/ppermute | solution.py:305
  89.9 5.2 %collective-permute-start.14 = (bf16[2,9,16,256]{3,2,1,0:T(8,128)(2,1)S(1)}, bf16[2,9,16,256]{3,2,1,0:T(8,128)(2,1)S(1)}, u32[]{:S(2)}, u32[]{:S(2)}) collective-permute-start(bf16[2,9,16,256]{3,2,1,0:T(8,128)(2,1)S(1)} %get-tuple-element.98), channel_id=1, source_target_pairs={{0,1},{1,0},{2,3},{3,2},{4,5},{5,4},{6,7},{7,6},{8,9},{9,8},{10,11... | collective-permute-start | bytes 442376 | tf_op jit(solution)/shard_map/ppermute | solution.py:305
  94.7 8.3 %copy-start = (bf16[1,16,9,256]{3,1,2,0:T(8,128)(2,1)S(1)}, bf16[1,16,9,256]{3,1,2,0:T(8,128)(2,1)}, u32[]{:S(2)}) copy-start(bf16[1,16,9,256]{3,1,2,0:T(8,128)(2,1)} %param.6) | copy-start | bytes 221188
  95.4 11.8 %collective-permute-start.20 = (bf16[2,9,16,256]{3,2,1,0:T(8,128)(2,1)S(1)}, bf16[2,9,16,256]{3,2,1,0:T(8,128)(2,1)S(1)}, u32[]{:S(2)}, u32[]{:S(2)}) collective-permute-start(bf16[2,9,16,256]{3,2,1,0:T(8,128)(2,1)S(1)} %get-tuple-element.111), channel_id=1, source_target_pairs={{0,1},{1,0},{2,3},{3,2},{4,5},{5,4},{6,7},{7,6},{8,9},{9,8},{10,11... | collective-permute-start | bytes 442376 | tf_op jit(solution)/shard_map/ppermute | solution.py:305
  96.5 6.6 %collective-permute-start.15 = (bf16[9,16,256]{2,1,0:T(8,128)(2,1)S(1)}, bf16[9,16,256]{2,1,0:T(8,128)(2,1)S(1)}, u32[]{:S(2)}, u32[]{:S(2)}) collective-permute-start(bf16[9,16,256]{2,1,0:T(8,128)(2,1)S(1)} %get-tuple-element.101), channel_id=1, source_target_pairs={{0,2},{1,3},{2,0},{3,1},{4,6},{5,7},{6,4},{7,5},{8,10},{9,11},{10,... | collective-permute-start | bytes 221192 | tf_op jit(solution)/shard_map/ppermute | solution.py:305
  103.1 7.1 %collective-permute-start.16 = (bf16[9,16,256]{2,1,0:T(8,128)(2,1)S(1)}, bf16[9,16,256]{2,1,0:T(8,128)(2,1)S(1)}, u32[]{:S(2)}, u32[]{:S(2)}) collective-permute-start(bf16[9,16,256]{2,1,0:T(8,128)(2,1)S(1)} %finish_kernel.2), channel_id=1, source_target_pairs={{0,224},{16,240},{32,0},{48,16},{64,32},{80,48},{96,64},{112,80},{... | collective-permute-start | bytes 221192 | tf_op jit(solution)/shard_map/ppermute | solution.py:320
  107.3 8.6 %collective-permute-start.21 = (bf16[9,16,256]{2,1,0:T(8,128)(2,1)S(1)}, bf16[9,16,256]{2,1,0:T(8,128)(2,1)S(1)}, u32[]{:S(2)}, u32[]{:S(2)}) collective-permute-start(bf16[9,16,256]{2,1,0:T(8,128)(2,1)S(1)} %get-tuple-element.113), channel_id=1, source_target_pairs={{0,2},{1,3},{2,0},{3,1},{4,6},{5,7},{6,4},{7,5},{8,10},{9,11},{10,... | collective-permute-start | bytes 221192 | tf_op jit(solution)/shard_map/ppermute | solution.py:305

commit v5 on v4

--- a/solution.py
+++ b/solution.py
@@ -20,14 +20,12 @@
 
 def fill_shifted(shift_ref, rows):
     for index, row in enumerate(rows):
-        wide = row.astype(F32)
-        columns = wide.shape[1]
-        place = lax.broadcasted_iota(jnp.int32, wide.shape, 1)
-        ahead = pltpu.roll(wide, columns - 1, 1)
-        behind = pltpu.roll(wide, 1, 1)
-        shift_ref[0, index] = jnp.where(place == columns - 1, 0.0, ahead).astype(BF)
+        columns = row.shape[1]
+        place = lax.broadcasted_iota(jnp.int32, row.shape, 1)
+        nothing = jnp.zeros_like(row)
+        shift_ref[0, index] = jnp.where(place == columns - 1, nothing, pltpu.roll(row, columns - 1, 1))
         shift_ref[1, index] = row
-        shift_ref[2, index] = jnp.where(place == 0, 0.0, behind).astype(BF)
+        shift_ref[2, index] = jnp.where(place == 0, nothing, pltpu.roll(row, 1, 1))
 
 
 def near(shape, kind=BF):
@@ -231,25 +229,28 @@
     )(*[value for value, _ in rest])
 
 
-def half_kernel(kernel, out, sem):
-    part = out.shape[1]
+def opening_kernel(kernel, image, half, top, bot, sems):
+    part = half.shape[1]
     start = pl.multiple_of(lax.rem(lax.axis_index("rows") // 4, 2) * part, part)
-    copy = pltpu.make_async_copy(kernel.at[:, pl.ds(start, part), :], out, sem)
-    copy.start()
-    copy.wait()
-
-
-def half_of(kernel):
+    last = image.shape[1] - 1
+    pairs = [(image.at[0, 0], top), (image.at[0, last], bot), (kernel.at[:, pl.ds(start, part), :], half)]
+    for copy in fetch(pairs, sems):
+        copy.wait()
+
+
+def opening(kernel, image):
     taps, rows, columns = kernel.shape
+    edge = near(image.shape[2:])
     return pl.pallas_call(
-        half_kernel,
-        out_shape=near((taps, rows // 2, columns)),
-        in_specs=[whole(pl.ANY)],
-        out_specs=whole(),
-        scratch_shapes=[pltpu.SemaphoreType.DMA],
+        opening_kernel,
+        out_shape=[near((taps, rows // 2, columns)), edge, edge],
+        in_specs=[whole(pl.ANY)] * 2,
+        out_specs=[whole()] * 3,
+        scratch_shapes=[pltpu.SemaphoreType.DMA((3,))],
         compiler_params=pltpu.CompilerParams(vmem_limit_bytes=SMALL_VMEM_BYTES),
-        name="half",
-    )(kept(kernel))
+        cost_estimate=pl.CostEstimate(flops=1, bytes_accessed=1, transcendentals=0),
+        name="opening",
+    )(kept(kernel), kept(image))
 
 
 def pair_kernel(zero, two, other, *outs):
@@ -348,7 +349,6 @@
     height = cotangent.shape[1]
     columns = cotangent.shape[3]
     scale = float(16 * height * columns) ** (-0.5)
-    image = cotangent[0]
     back_by = lambda by: [(b, (b - by) % 16) for b in range(16)]
     evens = range(0, 16, 2)
 
@@ -358,8 +358,9 @@
     def weight(tick, edges):
         return weight_terms(tick, edges, cotangent, saved_inputs, scale)
 
-    half = kernels_back(half_of(kernel), [(b, (b - 1) % 16) for b in evens])
-    up, _, _, _, down = with_edges(image[0], None, image[height - 1])
+    half, top, bot = opening(kernel, cotangent)
+    half = kernels_back(half, [(b, (b - 1) % 16) for b in evens])
+    up, _, _, _, down = with_edges(top, None, bot)
     half, kernel_here = after((half, kernel), up, down)
     kernel_one = around(kernel_here, [(b + 1, b) for b in evens])
     states, *parts = back(0, (up, down), kernel, (), None)
@@ -381,7 +382,7 @@
     keep, came = part_over_z(first, held)
     (states,) = back(2, after(edges_two, keep), kernel_two, (), states)
     keep, came = rest_over_z(keep, after(came, states))
-    last = after(last, keep)
+    last = after(last, came)
     (early,) = small(finish_kernel, [near(held.shape)], held, keep, came)
     early = around(early, back_by(2))
     keep, came = part_over_z(last, held)

time: 117 us -> 115 us (0.983)
  starting transfers between devices: 67.1 us -> 56.2 us
  waiting for transfers between devices: 25.7 us -> 34.2 us
    ppermute x10, starting transfers between devices: 21.5 us -> 12.4 us  [along(): lax.ppermute(value, 'rows', [(x * 4 + z, move(x, z)) for x in range(4) fo...]
    ppermute x10, waiting for transfers between devices: 15 us -> 23.5 us  [along(): lax.ppermute(value, 'rows', [(x * 4 + z, move(x, z)) for x in range(4) fo...]
    ppermute x3, waiting for transfers between devices: 6.77 us -> 2.38 us  [with_edges(): down = lax.ppermute(top, 'rows', [(i + 1, i) for i in range(15)])]
    ppermute x3, starting transfers between devices: 6.14 us -> 1.97 us  [around(): return lax.ppermute(value, 'blk', pairs)]
    ppermute x3, starting transfers between devices: 5.91 us -> 9.45 us  [with_edges(): up = lax.ppermute(bot, 'rows', [(i, i + 1) for i in range(15)])]
    ppermute x3, waiting for transfers between devices: 2.42 us -> 4.71 us  [with_edges(): up = lax.ppermute(bot, 'rows', [(i, i + 1) for i in range(15)])]
    ppermute x2, waiting for transfers between devices: 1.52 us -> 3.62 us  [kernels_back(): return lax.ppermute(value, ('blk', 'rows'), moves)]
  transfers between devices with their start and end apart: 22 -> 22, of which waited for: 9 -> 11; matrix products, arithmetic and copies ran while one was open for 0% -> 0% of each run, Pallas kernels for 15% -> 15%
where the time goes in v5:
time: 115 us; the launch traced here: 114 us
  starting transfers between devices  56.2 us (49%)
  waiting for transfers between devices  34.2 us (30%)
  Pallas kernels  22.9 us (20%)
    ppermute x10, waiting for transfers between devices, along(): lax.ppermute(value, 'rows', [(x * 4 + z, move(x, z)) for x in range(4) fo...  23.5 us
    ppermute x3, starting transfers between devices, with_edges(): down = lax.ppermute(top, 'rows', [(i + 1, i) for i in range(15)])  16.2 us
    ppermute x2, starting transfers between devices, kernels_back(): return lax.ppermute(value, ('blk', 'rows'), moves)  15.5 us
    ppermute x10, starting transfers between devices, along(): lax.ppermute(value, 'rows', [(x * 4 + z, move(x, z)) for x in range(4) fo...  12.4 us
    pallas_call x3, Pallas kernels, back_project(): pl.pallas_call(functools.partial(back_kernel, tick), out_shape=shapes, in...  11.2 us
    ppermute x3, starting transfers between devices, with_edges(): up = lax.ppermute(bot, 'rows', [(i, i + 1) for i in range(15)])  9.45 us
    pallas_call x3, Pallas kernels, weight_terms(): pl.pallas_call(functools.partial(weight_kernel, tick, scale), out_shape=n...  8.66 us
    ppermute x3, waiting for transfers between devices, with_edges(): up = lax.ppermute(bot, 'rows', [(i, i + 1) for i in range(15)])  4.71 us
  transfers between devices with their start and end apart: 22, of which 11 were waited for; matrix products, arithmetic and copies ran while one was open for 0% of the time, Pallas kernels for 15%

profile of v5, /device:TPU:2, one launch (start us, length us, event | category | flops | bytes accessed | tf_op | source)
XLA Modules:
  0.0 114.2 jit_solution(5106685349173193450)
XLA Ops:
  0.6 0.0 copy-start.1
  0.6 1.3 %opening.1 = (bf16[9,128,256]{2,1,0:T(8,128)(2,1)S(1)}, bf16[256,256]{1,0:T(8,128)(2,1)S(1)}, bf16[256,256]{1,0:T(8,128)(2,1)S(1)}) custom-call(bf16[9,256,256]{2,1,0:T(8,128)(2,1)} %bitcast.10, bf16[1,4,256,256]{3,2,1,0:T(8,128)(2,1)} %refs_2_.3), custom_call_target="tpu_custom_call" | custom-call | flops 1 | bytes 1 | tf_op jit(solution)/shard_map/opening/pallas_call | solution.py:244
  2.0 9.7 %collective-permute-start.4 = (bf16[9,128,256]{2,1,0:T(8,128)(2,1)S(1)}, bf16[9,128,256]{2,1,0:T(8,128)(2,1)S(1)}, u32[]{:S(2)}, u32[]{:S(2)}) collective-permute-start(bf16[9,128,256]{2,1,0:T(8,128)(2,1)S(1)} %get-tuple-element.73), channel_id=1, source_target_pairs={{3,240},{2,241},{1,242},{0,243},{7,244},{6,245},{5,246},{4,247},{1... | collective-permute-start | bytes 1769480 | tf_op jit(solution)/shard_map/ppermute | solution.py:317
  11.7 3.8 %collective-permute-start = (bf16[256,256]{1,0:T(8,128)(2,1)S(1)}, bf16[256,256]{1,0:T(8,128)(2,1)S(1)}, u32[]{:S(2)}, u32[]{:S(2)}) collective-permute-start(bf16[256,256]{1,0:T(8,128)(2,1)S(1)} %get-tuple-element.61), channel_id=1, source_target_pairs={{0,1},{1,2},{2,3},{3,4},{4,5},{5,6},{6,7},{7,8},{8,9},{9,10},{10,1... | collective-permute-start | bytes 393224 | tf_op jit(solution)/shard_map/ppermute | solution.py:325
  15.5 4.7 %collective-permute-start.1 = (bf16[256,256]{1,0:T(8,128)(2,1)S(1)}, bf16[256,256]{1,0:T(8,128)(2,1)S(1)}, u32[]{:S(2)}, u32[]{:S(2)}) collective-permute-start(bf16[256,256]{1,0:T(8,128)(2,1)S(1)} %get-tuple-element.62), channel_id=1, source_target_pairs={{1,0},{2,1},{3,2},{4,3},{5,4},{6,5},{7,6},{8,7},{9,8},{10,9},{11,1... | collective-permute-start | bytes 393224 | tf_op jit(solution)/shard_map/ppermute | solution.py:326
  20.2 4.7 %collective-permute-done.refs_0_ = bf16[256,256]{1,0:T(8,128)(2,1)S(1)} collective-permute-done((bf16[256,256]{1,0:T(8,128)(2,1)S(1)}, bf16[256,256]{1,0:T(8,128)(2,1)S(1)}, u32[]{:S(2)}, u32[]{:S(2)}) %collective-permute-start) | collective-permute-done | bytes 131104 | tf_op jit(solution)/shard_map/ppermute | solution.py:325
  24.9 0.0 collective-permute-done.1.refs_1_
  24.9 0.4 collective-permute-done.4.refs_6_
  25.3 0.0 copy-done.1
  25.3 1.3 %collective-permute-start.5 = (bf16[9,256,256]{2,1,0:T(8,128)(2,1)S(1)}, bf16[9,256,256]{2,1,0:T(8,128)(2,1)S(1)}, u32[]{:S(2)}, u32[]{:S(2)}) collective-permute-start(bf16[9,256,256]{2,1,0:T(8,128)(2,1)S(1)} %bitcast.12), channel_id=1, source_target_pairs={{16,0},{48,32},{80,64},{112,96},{144,128},{176,160},{208,192},{240... | collective-permute-start | bytes 3538952 | tf_op jit(solution)/shard_map/ppermute | solution.py:321
  26.6 0.7 collective-permute-start.6
  27.3 4.1 %back.3 = (bf16[3,1,4,256,256]{4,3,2,1,0:T(8,128)(2,1)}, bf16[256,256]{1,0:T(8,128)(2,1)S(1)}, bf16[2,256,256]{2,1,0:T(8,128)(2,1)S(1)}, bf16[256,256]{1,0:T(8,128)(2,1)S(1)}) custom-call(bf16[256,256]{1,0:T(8,128)(2,1)S(1)} %collective-permute-done.refs_0_, bf16[256,256]{1,0:T(8,128)(2,1)S(1)} %collective-permute-done.1.refs_1_, ...), custom_call_target="tpu_custom_call" | custom-call | flops 1 | bytes 1 | tf_op jit(solution)/shard_map/back/pallas_call | solution.py:159
  31.4 1.9 %collective-permute-start.2 = (bf16[256,256]{1,0:T(8,128)(2,1)S(1)}, bf16[256,256]{1,0:T(8,128)(2,1)S(1)}, u32[]{:S(2)}, u32[]{:S(2)}) collective-permute-start(bf16[256,256]{1,0:T(8,128)(2,1)S(1)} %get-tuple-element.84.refs_3_), channel_id=1, source_target_pairs={{0,1},{1,2},{2,3},{3,4},{4,5},{5,6},{6,7},{7,8},{8,9},{9,10},{10,1... | collective-permute-start | bytes 393224 | tf_op jit(solution)/shard_map/ppermute | solution.py:325
  33.3 6.6 %collective-permute-start.3 = (bf16[256,256]{1,0:T(8,128)(2,1)S(1)}, bf16[256,256]{1,0:T(8,128)(2,1)S(1)}, u32[]{:S(2)}, u32[]{:S(2)}) collective-permute-start(bf16[256,256]{1,0:T(8,128)(2,1)S(1)} %get-tuple-element.82.refs_1_), channel_id=1, source_target_pairs={{1,0},{2,1},{3,2},{4,3},{5,4},{6,5},{7,6},{8,7},{9,8},{10,9},{11,1... | collective-permute-start | bytes 393224 | tf_op jit(solution)/shard_map/ppermute | solution.py:326
  39.9 3.0 %weight.3.zero = bf16[4,4,9,16,256]{4,3,2,1,0:T(8,128)(2,1)S(1)} custom-call(bf16[256,256]{1,0:T(8,128)(2,1)S(1)} %collective-permute-done.refs_0_, bf16[256,256]{1,0:T(8,128)(2,1)S(1)} %collective-permute-done.1.refs_1_, bf16[1,4,256,256]{3,2,1,0:T(8,128)(2,1)} %refs_2_.3, bf16[3,1,4,256,256]{4,3,2,1,0:T(8,128)(2,1)} %refs_6_.1), custom_call_target="tpu_custom_call" | custom-call | flops 1 | bytes 1 | tf_op jit(solution)/shard_map/weight/pallas_call | solution.py:218
  42.9 0.0 collective-permute-done.2.refs_0_
  42.9 0.0 collective-permute-done.3.refs_4_
  42.9 0.0 collective-permute-done.6.refs_7_
  42.9 0.0 collective-permute-done.5.refs_5_
  43.0 4.0 %back.4 = (bf16[3,1,4,256,256]{4,3,2,1,0:T(8,128)(2,1)}, bf16[256,256]{1,0:T(8,128)(2,1)S(1)}, bf16[2,256,256]{2,1,0:T(8,128)(2,1)S(1)}, bf16[256,256]{1,0:T(8,128)(2,1)S(1)}, bf16[9,256,256]{2,1,0:T(8,128)(2,1)S(1)}) custom-call(bf16[256,256]{1,0:T(8,128)(2,1)S(1)} %collective-permute-done.2.refs_0_, ...), custom_call_target="tpu_custom_call", output_to_operand_aliasing={{0}: (10, {})} | custom-call | flops 1 | bytes 1 | tf_op jit(solution)/shard_map/back/pallas_call | solution.py:159
  46.9 3.7 %collective-permute-start.7 = (bf16[256,256]{1,0:T(8,128)(2,1)S(1)}, bf16[256,256]{1,0:T(8,128)(2,1)S(1)}, u32[]{:S(2)}, u32[]{:S(2)}) collective-permute-start(bf16[256,256]{1,0:T(8,128)(2,1)S(1)} %get-tuple-element.100.refs_3_), channel_id=1, source_target_pairs={{0,1},{1,2},{2,3},{3,4},{4,5},{5,6},{6,7},{7,8},{8,9},{9,10},{10,1... | collective-permute-start | bytes 393224 | tf_op jit(solution)/shard_map/ppermute | solution.py:325
  50.7 4.8 %collective-permute-start.8 = (bf16[256,256]{1,0:T(8,128)(2,1)S(1)}, bf16[256,256]{1,0:T(8,128)(2,1)S(1)}, u32[]{:S(2)}, u32[]{:S(2)}) collective-permute-start(bf16[256,256]{1,0:T(8,128)(2,1)S(1)} %get-tuple-element.98.refs_1_), channel_id=1, source_target_pairs={{1,0},{2,1},{3,2},{4,3},{5,4},{6,5},{7,6},{8,7},{9,8},{10,9},{11,1... | collective-permute-start | bytes 393224 | tf_op jit(solution)/shard_map/ppermute | solution.py:326
  55.5 2.9 %weight.4 = bf16[4,4,9,16,256]{4,3,2,1,0:T(8,128)(2,1)S(1)} custom-call(bf16[256,256]{1,0:T(8,128)(2,1)S(1)} %collective-permute-done.2.refs_0_, bf16[256,256]{1,0:T(8,128)(2,1)S(1)} %get-tuple-element.82.refs_1_, bf16[2,256,256]{2,1,0:T(8,128)(2,1)S(1)} %get-tuple-element.83.refs_2_, bf16[256,256]{1,0:T(8,128)(2,1)S(1)} %get-tuple-element.84.refs_3_, ...), custom_call_target="tpu_custom_call" | custom-call | flops 1 | bytes 1 | tf_op jit(solution)/shard_map/weight/pallas_call | solution.py:218
  58.4 0.0 collective-permute-done.7.refs_0_
  58.4 2.4 %collective-permute-done.8.refs_4_ = bf16[256,256]{1,0:T(8,128)(2,1)S(1)} collective-permute-done((bf16[256,256]{1,0:T(8,128)(2,1)S(1)}, bf16[256,256]{1,0:T(8,128)(2,1)S(1)}, u32[]{:S(2)}, u32[]{:S(2)}) %collective-permute-start.8) | collective-permute-done | bytes 131104 | tf_op jit(solution)/shard_map/ppermute | solution.py:326
  60.7 0.1 collective-permute-start.9
  60.8 5.9 %collective-permute-start.13 = (bf16[9,256,256]{2,1,0:T(8,128)(2,1)S(1)}, bf16[9,256,256]{2,1,0:T(8,128)(2,1)S(1)}, u32[]{:S(2)}, u32[]{:S(2)}) collective-permute-start(bf16[9,256,256]{2,1,0:T(8,128)(2,1)S(1)} %get-tuple-element.102), channel_id=1, source_target_pairs={{3,240},{2,241},{1,242},{0,243},{7,244},{6,245},{5,246},{4,247},{1... | collective-permute-start | bytes 3538952 | tf_op jit(solution)/shard_map/ppermute | solution.py:317
  66.7 2.9 %weight.5.two = bf16[4,4,9,16,256]{4,3,2,1,0:T(8,128)(2,1)S(1)} custom-call(bf16[256,256]{1,0:T(8,128)(2,1)S(1)} %collective-permute-done.7.refs_0_, bf16[256,256]{1,0:T(8,128)(2,1)S(1)} %get-tuple-element.98.refs_1_, bf16[2,256,256]{2,1,0:T(8,128)(2,1)S(1)} %get-tuple-element.99.refs_2_, bf16[256,256]{1,0:T(8,128)(2,1)S(1)} %get-tuple-element.100.refs_3_, ...), custom_call_target="tpu_custom_call" | custom-call | flops 1 | bytes 1 | tf_op jit(solution)/shard_map/weight/pallas_call | solution.py:218
  69.5 0.0 collective-permute-done.9.other
  69.6 0.6 pair_kernel.1
  70.2 0.9 collective-permute-start.10
  71.1 1.1 collective-permute-start.11
  72.2 1.1 collective-permute-start.12
  73.3 1.0 collective-permute-start.17
  74.3 6.0 %collective-permute-done.10.one = bf16[4,9,16,256]{3,2,1,0:T(8,128)(2,1)S(1)} collective-permute-done((bf16[4,9,16,256]{3,2,1,0:T(8,128)(2,1)S(1)}, bf16[4,9,16,256]{3,2,1,0:T(8,128)(2,1)S(1)}, u32[]{:S(2)}, u32[]{:S(2)}) %collective-permute-start.10) | collective-permute-done | bytes 294944 | tf_op jit(solution)/shard_map/ppermute | solution.py:306
  80.2 1.7 %collective-permute-start.18 = (bf16[4,9,16,256]{3,2,1,0:T(8,128)(2,1)S(1)}, bf16[4,9,16,256]{3,2,1,0:T(8,128)(2,1)S(1)}, u32[]{:S(2)}, u32[]{:S(2)}) collective-permute-start(bf16[4,9,16,256]{3,2,1,0:T(8,128)(2,1)S(1)} %get-tuple-element.110), channel_id=1, source_target_pairs={{0,8},{1,9},{2,10},{3,11},{4,12},{5,13},{6,14},{7,15},{8,0},{9,1},... | collective-permute-start | bytes 884744 | tf_op jit(solution)/shard_map/ppermute | solution.py:306
  81.9 0.8 collective-permute-done.11.two
  82.7 4.9 %collective-permute-start.19 = (bf16[4,9,16,256]{3,2,1,0:T(8,128)(2,1)S(1)}, bf16[4,9,16,256]{3,2,1,0:T(8,128)(2,1)S(1)}, u32[]{:S(2)}, u32[]{:S(2)}) collective-permute-start(bf16[4,9,16,256]{3,2,1,0:T(8,128)(2,1)S(1)} %get-tuple-element.111), channel_id=1, source_target_pairs={{0,12},{1,13},{2,14},{3,15},{4,0},{5,1},{6,2},{7,3},{8,4},{9,5},{1... | collective-permute-start | bytes 884744 | tf_op jit(solution)/shard_map/ppermute | solution.py:306
  87.5 0.8 collective-permute-done.12.three
  88.3 0.1 regroup_kernel.2
  88.4 0.1 collective-permute-start.14
  88.5 3.2 %collective-permute-done.13.refs_5_ = bf16[9,256,256]{2,1,0:T(8,128)(2,1)S(1)} collective-permute-done((bf16[9,256,256]{2,1,0:T(8,128)(2,1)S(1)}, bf16[9,256,256]{2,1,0:T(8,128)(2,1)S(1)}, u32[]{:S(2)}, u32[]{:S(2)}) %collective-permute-start.13) | collective-permute-done | bytes 1179680 | tf_op jit(solution)/shard_map/ppermute | solution.py:317
  91.8 3.2 %back.5 = bf16[3,1,4,256,256]{4,3,2,1,0:T(8,128)(2,1)} custom-call(bf16[256,256]{1,0:T(8,128)(2,1)S(1)} %collective-permute-done.7.refs_0_, bf16[256,256]{1,0:T(8,128)(2,1)S(1)} %get-tuple-element.98.refs_1_, bf16[2,256,256]{2,1,0:T(8,128)(2,1)S(1)} %get-tuple-element.99.refs_2_, ...), custom_call_target="tpu_custom_call", output_to_operand_aliasing={{}: (7, {})} | custom-call | flops 1 | bytes 1 | tf_op jit(solution)/shard_map/back/pallas_call | solution.py:159
  95.0 0.0 copy-start
  95.0 0.0 collective-permute-done.14.came
  95.0 0.1 collective-permute-start.15
  95.1 0.0 collective-permute-done.17.one
  95.1 0.0 collective-permute-done.18.two
  95.1 0.3 collective-permute-done.19.three
  95.5 4.9 %collective-permute-done.15.came = bf16[9,16,256]{2,1,0:T(8,128)(2,1)S(1)} collective-permute-done((bf16[9,16,256]{2,1,0:T(8,128)(2,1)S(1)}, bf16[9,16,256]{2,1,0:T(8,128)(2,1)S(1)}, u32[]{:S(2)}, u32[]{:S(2)}) %collective-permute-start.15) | collective-permute-done | bytes 73760 | tf_op jit(solution)/shard_map/ppermute | solution.py:306
  100.4 0.1 regroup_kernel.3
  100.5 0.1 collective-permute-start.20
  100.6 0.0 copy-done
  100.6 0.6 collective-permute-start.16
  101.3 4.5 %collective-permute-done.20.came = bf16[2,9,16,256]{3,2,1,0:T(8,128)(2,1)S(1)} collective-permute-done((bf16[2,9,16,256]{3,2,1,0:T(8,128)(2,1)S(1)}, bf16[2,9,16,256]{3,2,1,0:T(8,128)(2,1)S(1)}, u32[]{:S(2)}, u32[]{:S(2)}) %collective-permute-start.20) | collective-permute-done | bytes 147488 | tf_op jit(solution)/shard_map/ppermute | solution.py:306
  105.8 1.5 %collective-permute-start.21 = (bf16[9,16,256]{2,1,0:T(8,128)(2,1)S(1)}, bf16[9,16,256]{2,1,0:T(8,128)(2,1)S(1)}, u32[]{:S(2)}, u32[]{:S(2)}) collective-permute-start(bf16[9,16,256]{2,1,0:T(8,128)(2,1)S(1)} %get-tuple-element.119), channel_id=1, source_target_pairs={{0,2},{1,3},{2,0},{3,1},{4,6},{5,7},{6,4},{7,5},{8,10},{9,11},{10,... | collective-permute-start | bytes 221192 | tf_op jit(solution)/shard_map/ppermute | solution.py:306
  107.3 0.0 collective-permute-done.16.held
  107.3 6.3 %collective-permute-done.21.came = bf16[9,16,256]{2,1,0:T(8,128)(2,1)S(1)} collective-permute-done((bf16[9,16,256]{2,1,0:T(8,128)(2,1)S(1)}, bf16[9,16,256]{2,1,0:T(8,128)(2,1)S(1)}, u32[]{:S(2)}, u32[]{:S(2)}) %collective-permute-start.21) | collective-permute-done | bytes 73760 | tf_op jit(solution)/shard_map/ppermute | solution.py:306
  113.5 0.7 finish_kernel.3
  (3 shorter events, 0.1 us)
Async XLA Ops:
  0.6 24.7 %copy-start.1 = (bf16[1,256,9,256]{3,1,2,0:T(8,128)(2,1)S(1)}, bf16[1,256,9,256]{3,1,2,0:T(8,128)(2,1)}, u32[]{:S(2)}) copy-start(bf16[1,256,9,256]{3,1,2,0:T(8,128)(2,1)} %param.5) | copy-start | bytes 3538948
  2.0 23.4 %collective-permute-start.4 = (bf16[9,128,256]{2,1,0:T(8,128)(2,1)S(1)}, bf16[9,128,256]{2,1,0:T(8,128)(2,1)S(1)}, u32[]{:S(2)}, u32[]{:S(2)}) collective-permute-start(bf16[9,128,256]{2,1,0:T(8,128)(2,1)S(1)} %get-tuple-element.73), channel_id=1, source_target_pairs={{3,240},{2,241},{1,242},{0,243},{7,244},{6,245},{5,246},{4,247},{1... | collective-permute-start | bytes 1769480 | tf_op jit(solution)/shard_map/ppermute | solution.py:317
  11.7 13.3 %collective-permute-start = (bf16[256,256]{1,0:T(8,128)(2,1)S(1)}, bf16[256,256]{1,0:T(8,128)(2,1)S(1)}, u32[]{:S(2)}, u32[]{:S(2)}) collective-permute-start(bf16[256,256]{1,0:T(8,128)(2,1)S(1)} %get-tuple-element.61), channel_id=1, source_target_pairs={{0,1},{1,2},{2,3},{3,4},{4,5},{5,6},{6,7},{7,8},{8,9},{9,10},{10,1... | collective-permute-start | bytes 393224 | tf_op jit(solution)/shard_map/ppermute | solution.py:325
  15.5 9.4 %collective-permute-start.1 = (bf16[256,256]{1,0:T(8,128)(2,1)S(1)}, bf16[256,256]{1,0:T(8,128)(2,1)S(1)}, u32[]{:S(2)}, u32[]{:S(2)}) collective-permute-start(bf16[256,256]{1,0:T(8,128)(2,1)S(1)} %get-tuple-element.62), channel_id=1, source_target_pairs={{1,0},{2,1},{3,2},{4,3},{5,4},{6,5},{7,6},{8,7},{9,8},{10,9},{11,1... | collective-permute-start | bytes 393224 | tf_op jit(solution)/shard_map/ppermute | solution.py:326
  25.3 17.6 %collective-permute-start.5 = (bf16[9,256,256]{2,1,0:T(8,128)(2,1)S(1)}, bf16[9,256,256]{2,1,0:T(8,128)(2,1)S(1)}, u32[]{:S(2)}, u32[]{:S(2)}) collective-permute-start(bf16[9,256,256]{2,1,0:T(8,128)(2,1)S(1)} %bitcast.12), channel_id=1, source_target_pairs={{16,0},{48,32},{80,64},{112,96},{144,128},{176,160},{208,192},{240... | collective-permute-start | bytes 3538952 | tf_op jit(solution)/shard_map/ppermute | solution.py:321
  26.6 16.3 %collective-permute-start.6 = (bf16[9,128,256]{2,1,0:T(8,128)(2,1)S(1)}, bf16[9,128,256]{2,1,0:T(8,128)(2,1)S(1)}, u32[]{:S(2)}, u32[]{:S(2)}) collective-permute-start(bf16[9,128,256]{2,1,0:T(8,128)(2,1)S(1)} %collective-permute-done.4.refs_6_), channel_id=1, source_target_pairs={{16,20},{17,21},{18,22},{19,23},{20,16},{21,17},{22,18},{23,19},{2... | collective-permute-start | bytes 1769480 | tf_op jit(solution)/shard_map/ppermute | solution.py:311
  31.4 11.5 %collective-permute-start.2 = (bf16[256,256]{1,0:T(8,128)(2,1)S(1)}, bf16[256,256]{1,0:T(8,128)(2,1)S(1)}, u32[]{:S(2)}, u32[]{:S(2)}) collective-permute-start(bf16[256,256]{1,0:T(8,128)(2,1)S(1)} %get-tuple-element.84.refs_3_), channel_id=1, source_target_pairs={{0,1},{1,2},{2,3},{3,4},{4,5},{5,6},{6,7},{7,8},{8,9},{9,10},{10,1... | collective-permute-start | bytes 393224 | tf_op jit(solution)/shard_map/ppermute | solution.py:325
  33.3 9.6 %collective-permute-start.3 = (bf16[256,256]{1,0:T(8,128)(2,1)S(1)}, bf16[256,256]{1,0:T(8,128)(2,1)S(1)}, u32[]{:S(2)}, u32[]{:S(2)}) collective-permute-start(bf16[256,256]{1,0:T(8,128)(2,1)S(1)} %get-tuple-element.82.refs_1_), channel_id=1, source_target_pairs={{1,0},{2,1},{3,2},{4,3},{5,4},{6,5},{7,6},{8,7},{9,8},{10,9},{11,1... | collective-permute-start | bytes 393224 | tf_op jit(solution)/shard_map/ppermute | solution.py:326
  46.9 11.4 %collective-permute-start.7 = (bf16[256,256]{1,0:T(8,128)(2,1)S(1)}, bf16[256,256]{1,0:T(8,128)(2,1)S(1)}, u32[]{:S(2)}, u32[]{:S(2)}) collective-permute-start(bf16[256,256]{1,0:T(8,128)(2,1)S(1)} %get-tuple-element.100.refs_3_), channel_id=1, source_target_pairs={{0,1},{1,2},{2,3},{3,4},{4,5},{5,6},{6,7},{7,8},{8,9},{9,10},{10,1... | collective-permute-start | bytes 393224 | tf_op jit(solution)/shard_map/ppermute | solution.py:325
  50.7 10.1 %collective-permute-start.8 = (bf16[256,256]{1,0:T(8,128)(2,1)S(1)}, bf16[256,256]{1,0:T(8,128)(2,1)S(1)}, u32[]{:S(2)}, u32[]{:S(2)}) collective-permute-start(bf16[256,256]{1,0:T(8,128)(2,1)S(1)} %get-tuple-element.98.refs_1_), channel_id=1, source_target_pairs={{1,0},{2,1},{3,2},{4,3},{5,4},{6,5},{7,6},{8,7},{9,8},{10,9},{11,1... | collective-permute-start | bytes 393224 | tf_op jit(solution)/shard_map/ppermute | solution.py:326
  60.7 8.8 %collective-permute-start.9 = (bf16[4,4,9,16,256]{4,3,2,1,0:T(8,128)(2,1)S(1)}, bf16[4,4,9,16,256]{4,3,2,1,0:T(8,128)(2,1)S(1)}, u32[]{:S(2)}, u32[]{:S(2)}) collective-permute-start(bf16[4,4,9,16,256]{4,3,2,1,0:T(8,128)(2,1)S(1)} %weight.4), channel_id=1, source_target_pairs={{0,16},{16,0},{32,48},{48,32},{64,80},{80,64},{96,112},{112,96},{1... | collective-permute-start | bytes 3538952 | tf_op jit(solution)/shard_map/ppermute | solution.py:321
  60.8 30.9 %collective-permute-start.13 = (bf16[9,256,256]{2,1,0:T(8,128)(2,1)S(1)}, bf16[9,256,256]{2,1,0:T(8,128)(2,1)S(1)}, u32[]{:S(2)}, u32[]{:S(2)}) collective-permute-start(bf16[9,256,256]{2,1,0:T(8,128)(2,1)S(1)} %get-tuple-element.102), channel_id=1, source_target_pairs={{3,240},{2,241},{1,242},{0,243},{7,244},{6,245},{5,246},{4,247},{1... | collective-permute-start | bytes 3538952 | tf_op jit(solution)/shard_map/ppermute | solution.py:317
  70.2 10.0 %collective-permute-start.10 = (bf16[4,9,16,256]{3,2,1,0:T(8,128)(2,1)S(1)}, bf16[4,9,16,256]{3,2,1,0:T(8,128)(2,1)S(1)}, u32[]{:S(2)}, u32[]{:S(2)}) collective-permute-start(bf16[4,9,16,256]{3,2,1,0:T(8,128)(2,1)S(1)} %get-tuple-element.93), channel_id=1, source_target_pairs={{0,4},{1,5},{2,6},{3,7},{4,8},{5,9},{6,10},{7,11},{8,12},{9,13},{1... | collective-permute-start | bytes 884744 | tf_op jit(solution)/shard_map/ppermute | solution.py:306
  71.1 11.6 %collective-permute-start.11 = (bf16[4,9,16,256]{3,2,1,0:T(8,128)(2,1)S(1)}, bf16[4,9,16,256]{3,2,1,0:T(8,128)(2,1)S(1)}, u32[]{:S(2)}, u32[]{:S(2)}) collective-permute-start(bf16[4,9,16,256]{3,2,1,0:T(8,128)(2,1)S(1)} %get-tuple-element.94), channel_id=1, source_target_pairs={{0,8},{1,9},{2,10},{3,11},{4,12},{5,13},{6,14},{7,15},{8,0},{9,1},... | collective-permute-start | bytes 884744 | tf_op jit(solution)/shard_map/ppermute | solution.py:306
  72.2 16.1 %collective-permute-start.12 = (bf16[4,9,16,256]{3,2,1,0:T(8,128)(2,1)S(1)}, bf16[4,9,16,256]{3,2,1,0:T(8,128)(2,1)S(1)}, u32[]{:S(2)}, u32[]{:S(2)}) collective-permute-start(bf16[4,9,16,256]{3,2,1,0:T(8,128)(2,1)S(1)} %get-tuple-element.95), channel_id=1, source_target_pairs={{0,12},{1,13},{2,14},{3,15},{4,0},{5,1},{6,2},{7,3},{8,4},{9,5},{1... | collective-permute-start | bytes 884744 | tf_op jit(solution)/shard_map/ppermute | solution.py:306
  73.3 21.9 %collective-permute-start.17 = (bf16[4,9,16,256]{3,2,1,0:T(8,128)(2,1)S(1)}, bf16[4,9,16,256]{3,2,1,0:T(8,128)(2,1)S(1)}, u32[]{:S(2)}, u32[]{:S(2)}) collective-permute-start(bf16[4,9,16,256]{3,2,1,0:T(8,128)(2,1)S(1)} %get-tuple-element.109), channel_id=1, source_target_pairs={{0,4},{1,5},{2,6},{3,7},{4,8},{5,9},{6,10},{7,11},{8,12},{9,13},{1... | collective-permute-start | bytes 884744 | tf_op jit(solution)/shard_map/ppermute | solution.py:306
  80.2 14.9 %collective-permute-start.18 = (bf16[4,9,16,256]{3,2,1,0:T(8,128)(2,1)S(1)}, bf16[4,9,16,256]{3,2,1,0:T(8,128)(2,1)S(1)}, u32[]{:S(2)}, u32[]{:S(2)}) collective-permute-start(bf16[4,9,16,256]{3,2,1,0:T(8,128)(2,1)S(1)} %get-tuple-element.110), channel_id=1, source_target_pairs={{0,8},{1,9},{2,10},{3,11},{4,12},{5,13},{6,14},{7,15},{8,0},{9,1},... | collective-permute-start | bytes 884744 | tf_op jit(solution)/shard_map/ppermute | solution.py:306
  82.7 12.8 %collective-permute-start.19 = (bf16[4,9,16,256]{3,2,1,0:T(8,128)(2,1)S(1)}, bf16[4,9,16,256]{3,2,1,0:T(8,128)(2,1)S(1)}, u32[]{:S(2)}, u32[]{:S(2)}) collective-permute-start(bf16[4,9,16,256]{3,2,1,0:T(8,128)(2,1)S(1)} %get-tuple-element.111), channel_id=1, source_target_pairs={{0,12},{1,13},{2,14},{3,15},{4,0},{5,1},{6,2},{7,3},{8,4},{9,5},{1... | collective-permute-start | bytes 884744 | tf_op jit(solution)/shard_map/ppermute | solution.py:306
  88.4 6.5 %collective-permute-start.14 = (bf16[2,9,16,256]{3,2,1,0:T(8,128)(2,1)S(1)}, bf16[2,9,16,256]{3,2,1,0:T(8,128)(2,1)S(1)}, u32[]{:S(2)}, u32[]{:S(2)}) collective-permute-start(bf16[2,9,16,256]{3,2,1,0:T(8,128)(2,1)S(1)} %get-tuple-element.104), channel_id=1, source_target_pairs={{0,1},{1,0},{2,3},{3,2},{4,5},{5,4},{6,7},{7,6},{8,9},{9,8},{10,11... | collective-permute-start | bytes 442376 | tf_op jit(solution)/shard_map/ppermute | solution.py:306
  95.0 5.6 %copy-start = (bf16[1,16,9,256]{3,1,2,0:T(8,128)(2,1)S(1)}, bf16[1,16,9,256]{3,1,2,0:T(8,128)(2,1)}, u32[]{:S(2)}) copy-start(bf16[1,16,9,256]{3,1,2,0:T(8,128)(2,1)} %param.6) | copy-start | bytes 221188
  95.0 5.3 %collective-permute-start.15 = (bf16[9,16,256]{2,1,0:T(8,128)(2,1)S(1)}, bf16[9,16,256]{2,1,0:T(8,128)(2,1)S(1)}, u32[]{:S(2)}, u32[]{:S(2)}) collective-permute-start(bf16[9,16,256]{2,1,0:T(8,128)(2,1)S(1)} %get-tuple-element.107), channel_id=1, source_target_pairs={{0,2},{1,3},{2,0},{3,1},{4,6},{5,7},{6,4},{7,5},{8,10},{9,11},{10,... | collective-permute-start | bytes 221192 | tf_op jit(solution)/shard_map/ppermute | solution.py:306
  100.5 5.2 %collective-permute-start.20 = (bf16[2,9,16,256]{3,2,1,0:T(8,128)(2,1)S(1)}, bf16[2,9,16,256]{3,2,1,0:T(8,128)(2,1)S(1)}, u32[]{:S(2)}, u32[]{:S(2)}) collective-permute-start(bf16[2,9,16,256]{3,2,1,0:T(8,128)(2,1)S(1)} %get-tuple-element.117), channel_id=1, source_target_pairs={{0,1},{1,0},{2,3},{3,2},{4,5},{5,4},{6,7},{7,6},{8,9},{9,8},{10,11... | collective-permute-start | bytes 442376 | tf_op jit(solution)/shard_map/ppermute | solution.py:306
  100.6 6.6 %collective-permute-start.16 = (bf16[9,16,256]{2,1,0:T(8,128)(2,1)S(1)}, bf16[9,16,256]{2,1,0:T(8,128)(2,1)S(1)}, u32[]{:S(2)}, u32[]{:S(2)}) collective-permute-start(bf16[9,16,256]{2,1,0:T(8,128)(2,1)S(1)} %finish_kernel.2), channel_id=1, source_target_pairs={{0,224},{16,240},{32,0},{48,16},{64,32},{80,48},{96,64},{112,80},{... | collective-permute-start | bytes 221192 | tf_op jit(solution)/shard_map/ppermute | solution.py:321
  105.8 7.8 %collective-permute-start.21 = (bf16[9,16,256]{2,1,0:T(8,128)(2,1)S(1)}, bf16[9,16,256]{2,1,0:T(8,128)(2,1)S(1)}, u32[]{:S(2)}, u32[]{:S(2)}) collective-permute-start(bf16[9,16,256]{2,1,0:T(8,128)(2,1)S(1)} %get-tuple-element.119), channel_id=1, source_target_pairs={{0,2},{1,3},{2,0},{3,1},{4,6},{5,7},{6,4},{7,5},{8,10},{9,11},{10,... | collective-permute-start | bytes 221192 | tf_op jit(solution)/shard_map/ppermute | solution.py:306

commit v6 on v5

--- a/solution.py
+++ b/solution.py
@@ -371,22 +371,22 @@
     states, *parts, used = back(1, edges_one, kernel_one, halves, states)
     edges_two = with_edges(*parts)
     sums_one = weight(1, after(edges_one, parts[0]))
-    edges_two, used, sums_one = lax.optimization_barrier((edges_two, used, sums_one))
+    edges_two, sums_one = lax.optimization_barrier((edges_two, sums_one))
     other = around(sums_one, [(b, b ^ 1) for b in range(16)])
-    kernel_two = kernels_back(used, back_by(1))
     sums_two = weight(2, edges_two)
     part = (4, *held.shape)
     spread = ([near(part, F32)] + [near(part)] * 3) * 2
     both = small(pair_kernel, spread, sums_zero, sums_two, other)
     first, last = over_x(both[:4]), over_x(both[4:])
-    keep, came = part_over_z(first, held)
-    (states,) = back(2, after(edges_two, keep), kernel_two, (), states)
-    keep, came = rest_over_z(keep, after(came, states))
+    kernel_two = kernels_back(after(used, both[0]), back_by(1))
+    keep, came = rest_over_z(*part_over_z(first, held))
     last = after(last, came)
     (early,) = small(finish_kernel, [near(held.shape)], held, keep, came)
     early = around(early, back_by(2))
-    keep, came = part_over_z(last, held)
-    (held,) = small(finish_kernel, [near(held.shape)], early, *rest_over_z(keep, came))
+    keep, came = rest_over_z(*part_over_z(last, held))
+    (states,) = back(2, after(edges_two, keep), kernel_two, (), states)
+    early = after(early, states)
+    (held,) = small(finish_kernel, [near(held.shape)], early, keep, came)
     return states, jnp.transpose(held, (1, 0, 2))[None]
 
 

time: 115 us -> 114 us (level)
  waiting for transfers between devices: 34.2 us -> 32.2 us
    ppermute x2, waiting for transfers between devices: 3.62 us -> 0.4 us  [kernels_back(): return lax.ppermute(value, ('blk', 'rows'), moves)]
    ppermute x10, waiting for transfers between devices: 23.5 us -> 24.7 us  [along(): lax.ppermute(value, 'rows', [(x * 4 + z, move(x, z)) for x in range(4) fo...]
  transfers between devices with their start and end apart: 22 -> 22, of which waited for: 11 -> 11; matrix products, arithmetic and copies ran while one was open for 0% -> 0% of each run, Pallas kernels for 15% -> 14%
where the time goes in v6:
time: 114 us; the launch traced here: 113 us
  starting transfers between devices  56.9 us (50%)
  waiting for transfers between devices  32.2 us (28%)
  Pallas kernels  22.9 us (20%)
    ppermute x10, waiting for transfers between devices, along(): lax.ppermute(value, 'rows', [(x * 4 + z, move(x, z)) for x in range(4) fo...  24.7 us
    ppermute x3, starting transfers between devices, with_edges(): down = lax.ppermute(top, 'rows', [(i + 1, i) for i in range(15)])  16.2 us
    ppermute x2, starting transfers between devices, kernels_back(): return lax.ppermute(value, ('blk', 'rows'), moves)  15.6 us
    ppermute x10, starting transfers between devices, along(): lax.ppermute(value, 'rows', [(x * 4 + z, move(x, z)) for x in range(4) fo...  12.5 us
    pallas_call x3, Pallas kernels, back_project(): pl.pallas_call(functools.partial(back_kernel, tick), out_shape=shapes, in...  11.2 us
    ppermute x3, starting transfers between devices, with_edges(): up = lax.ppermute(bot, 'rows', [(i, i + 1) for i in range(15)])  9.45 us
    pallas_call x3, Pallas kernels, weight_terms(): pl.pallas_call(functools.partial(weight_kernel, tick, scale), out_shape=n...  8.66 us
    ppermute x3, waiting for transfers between devices, with_edges(): up = lax.ppermute(bot, 'rows', [(i, i + 1) for i in range(15)])  4.71 us
  transfers between devices with their start and end apart: 22, of which 11 were waited for; matrix products, arithmetic and copies ran while one was open for 0% of the time, Pallas kernels for 14%

profile of v6, /device:TPU:2, one launch (start us, length us, event | category | flops | bytes accessed | tf_op | source)
XLA Modules:
  0.0 113.0 jit_solution(11159514643965607458)
XLA Ops:
  0.6 0.0 copy-start.1
  0.6 1.3 %opening.1 = (bf16[9,128,256]{2,1,0:T(8,128)(2,1)S(1)}, bf16[256,256]{1,0:T(8,128)(2,1)S(1)}, bf16[256,256]{1,0:T(8,128)(2,1)S(1)}) custom-call(bf16[9,256,256]{2,1,0:T(8,128)(2,1)} %bitcast.10, bf16[1,4,256,256]{3,2,1,0:T(8,128)(2,1)} %refs_2_.3), custom_call_target="tpu_custom_call" | custom-call | flops 1 | bytes 1 | tf_op jit(solution)/shard_map/opening/pallas_call | solution.py:244
  2.0 9.7 %collective-permute-start.4 = (bf16[9,128,256]{2,1,0:T(8,128)(2,1)S(1)}, bf16[9,128,256]{2,1,0:T(8,128)(2,1)S(1)}, u32[]{:S(2)}, u32[]{:S(2)}) collective-permute-start(bf16[9,128,256]{2,1,0:T(8,128)(2,1)S(1)} %get-tuple-element.73), channel_id=1, source_target_pairs={{3,240},{2,241},{1,242},{0,243},{7,244},{6,245},{5,246},{4,247},{1... | collective-permute-start | bytes 1769480 | tf_op jit(solution)/shard_map/ppermute | solution.py:317
  11.7 3.8 %collective-permute-start = (bf16[256,256]{1,0:T(8,128)(2,1)S(1)}, bf16[256,256]{1,0:T(8,128)(2,1)S(1)}, u32[]{:S(2)}, u32[]{:S(2)}) collective-permute-start(bf16[256,256]{1,0:T(8,128)(2,1)S(1)} %get-tuple-element.61), channel_id=1, source_target_pairs={{0,1},{1,2},{2,3},{3,4},{4,5},{5,6},{6,7},{7,8},{8,9},{9,10},{10,1... | collective-permute-start | bytes 393224 | tf_op jit(solution)/shard_map/ppermute | solution.py:325
  15.5 4.7 %collective-permute-start.1 = (bf16[256,256]{1,0:T(8,128)(2,1)S(1)}, bf16[256,256]{1,0:T(8,128)(2,1)S(1)}, u32[]{:S(2)}, u32[]{:S(2)}) collective-permute-start(bf16[256,256]{1,0:T(8,128)(2,1)S(1)} %get-tuple-element.62), channel_id=1, source_target_pairs={{1,0},{2,1},{3,2},{4,3},{5,4},{6,5},{7,6},{8,7},{9,8},{10,9},{11,1... | collective-permute-start | bytes 393224 | tf_op jit(solution)/shard_map/ppermute | solution.py:326
  20.2 4.7 %collective-permute-done.refs_0_ = bf16[256,256]{1,0:T(8,128)(2,1)S(1)} collective-permute-done((bf16[256,256]{1,0:T(8,128)(2,1)S(1)}, bf16[256,256]{1,0:T(8,128)(2,1)S(1)}, u32[]{:S(2)}, u32[]{:S(2)}) %collective-permute-start) | collective-permute-done | bytes 131104 | tf_op jit(solution)/shard_map/ppermute | solution.py:325
  24.9 0.0 collective-permute-done.1.refs_1_
  24.9 0.4 collective-permute-done.4.refs_6_
  25.3 0.0 copy-done.1
  25.3 1.3 %collective-permute-start.5 = (bf16[9,256,256]{2,1,0:T(8,128)(2,1)S(1)}, bf16[9,256,256]{2,1,0:T(8,128)(2,1)S(1)}, u32[]{:S(2)}, u32[]{:S(2)}) collective-permute-start(bf16[9,256,256]{2,1,0:T(8,128)(2,1)S(1)} %bitcast.12), channel_id=1, source_target_pairs={{16,0},{48,32},{80,64},{112,96},{144,128},{176,160},{208,192},{240... | collective-permute-start | bytes 3538952 | tf_op jit(solution)/shard_map/ppermute | solution.py:321
  26.6 0.7 collective-permute-start.6
  27.3 4.1 %back.3 = (bf16[3,1,4,256,256]{4,3,2,1,0:T(8,128)(2,1)}, bf16[256,256]{1,0:T(8,128)(2,1)S(1)}, bf16[2,256,256]{2,1,0:T(8,128)(2,1)S(1)}, bf16[256,256]{1,0:T(8,128)(2,1)S(1)}) custom-call(bf16[256,256]{1,0:T(8,128)(2,1)S(1)} %collective-permute-done.refs_0_, bf16[256,256]{1,0:T(8,128)(2,1)S(1)} %collective-permute-done.1.refs_1_, ...), custom_call_target="tpu_custom_call" | custom-call | flops 1 | bytes 1 | tf_op jit(solution)/shard_map/back/pallas_call | solution.py:159
  31.4 1.9 %collective-permute-start.2 = (bf16[256,256]{1,0:T(8,128)(2,1)S(1)}, bf16[256,256]{1,0:T(8,128)(2,1)S(1)}, u32[]{:S(2)}, u32[]{:S(2)}) collective-permute-start(bf16[256,256]{1,0:T(8,128)(2,1)S(1)} %get-tuple-element.83.refs_3_), channel_id=1, source_target_pairs={{0,1},{1,2},{2,3},{3,4},{4,5},{5,6},{6,7},{7,8},{8,9},{9,10},{10,1... | collective-permute-start | bytes 393224 | tf_op jit(solution)/shard_map/ppermute | solution.py:325
  33.3 6.6 %collective-permute-start.3 = (bf16[256,256]{1,0:T(8,128)(2,1)S(1)}, bf16[256,256]{1,0:T(8,128)(2,1)S(1)}, u32[]{:S(2)}, u32[]{:S(2)}) collective-permute-start(bf16[256,256]{1,0:T(8,128)(2,1)S(1)} %get-tuple-element.81.refs_1_), channel_id=1, source_target_pairs={{1,0},{2,1},{3,2},{4,3},{5,4},{6,5},{7,6},{8,7},{9,8},{10,9},{11,1... | collective-permute-start | bytes 393224 | tf_op jit(solution)/shard_map/ppermute | solution.py:326
  39.9 3.0 %weight.3.zero = bf16[4,4,9,16,256]{4,3,2,1,0:T(8,128)(2,1)S(1)} custom-call(bf16[256,256]{1,0:T(8,128)(2,1)S(1)} %collective-permute-done.refs_0_, bf16[256,256]{1,0:T(8,128)(2,1)S(1)} %collective-permute-done.1.refs_1_, bf16[1,4,256,256]{3,2,1,0:T(8,128)(2,1)} %refs_2_.3, bf16[3,1,4,256,256]{4,3,2,1,0:T(8,128)(2,1)} %refs_6_.1), custom_call_target="tpu_custom_call" | custom-call | flops 1 | bytes 1 | tf_op jit(solution)/shard_map/weight/pallas_call | solution.py:218
  42.9 0.0 collective-permute-done.2.refs_0_
  42.9 0.0 collective-permute-done.3.refs_4_
  42.9 0.0 collective-permute-done.6.refs_7_
  42.9 0.0 collective-permute-done.5.refs_5_
  43.0 4.0 %back.4 = (bf16[3,1,4,256,256]{4,3,2,1,0:T(8,128)(2,1)}, bf16[256,256]{1,0:T(8,128)(2,1)S(1)}, bf16[2,256,256]{2,1,0:T(8,128)(2,1)S(1)}, bf16[256,256]{1,0:T(8,128)(2,1)S(1)}, bf16[9,256,256]{2,1,0:T(8,128)(2,1)S(1)}) custom-call(bf16[256,256]{1,0:T(8,128)(2,1)S(1)} %collective-permute-done.2.refs_0_, ...), custom_call_target="tpu_custom_call", output_to_operand_aliasing={{0}: (10, {})} | custom-call | flops 1 | bytes 1 | tf_op jit(solution)/shard_map/back/pallas_call | solution.py:159
  46.9 3.7 %collective-permute-start.7 = (bf16[256,256]{1,0:T(8,128)(2,1)S(1)}, bf16[256,256]{1,0:T(8,128)(2,1)S(1)}, u32[]{:S(2)}, u32[]{:S(2)}) collective-permute-start(bf16[256,256]{1,0:T(8,128)(2,1)S(1)} %get-tuple-element.112.refs_3_), channel_id=1, source_target_pairs={{0,1},{1,2},{2,3},{3,4},{4,5},{5,6},{6,7},{7,8},{8,9},{9,10},{10,1... | collective-permute-start | bytes 393224 | tf_op jit(solution)/shard_map/ppermute | solution.py:325
  50.7 4.8 %collective-permute-start.8 = (bf16[256,256]{1,0:T(8,128)(2,1)S(1)}, bf16[256,256]{1,0:T(8,128)(2,1)S(1)}, u32[]{:S(2)}, u32[]{:S(2)}) collective-permute-start(bf16[256,256]{1,0:T(8,128)(2,1)S(1)} %get-tuple-element.110.refs_1_), channel_id=1, source_target_pairs={{1,0},{2,1},{3,2},{4,3},{5,4},{6,5},{7,6},{8,7},{9,8},{10,9},{11,1... | collective-permute-start | bytes 393224 | tf_op jit(solution)/shard_map/ppermute | solution.py:326
  55.5 2.9 %weight.4 = bf16[4,4,9,16,256]{4,3,2,1,0:T(8,128)(2,1)S(1)} custom-call(bf16[256,256]{1,0:T(8,128)(2,1)S(1)} %collective-permute-done.2.refs_0_, bf16[256,256]{1,0:T(8,128)(2,1)S(1)} %get-tuple-element.81.refs_1_, bf16[2,256,256]{2,1,0:T(8,128)(2,1)S(1)} %get-tuple-element.82.refs_2_, bf16[256,256]{1,0:T(8,128)(2,1)S(1)} %get-tuple-element.83.refs_3_, ...), custom_call_target="tpu_custom_call" | custom-call | flops 1 | bytes 1 | tf_op jit(solution)/shard_map/weight/pallas_call | solution.py:218
  58.4 0.0 collective-permute-done.7.refs_0_
  58.4 2.4 %collective-permute-done.8.refs_4_ = bf16[256,256]{1,0:T(8,128)(2,1)S(1)} collective-permute-done((bf16[256,256]{1,0:T(8,128)(2,1)S(1)}, bf16[256,256]{1,0:T(8,128)(2,1)S(1)}, u32[]{:S(2)}, u32[]{:S(2)}) %collective-permute-start.8) | collective-permute-done | bytes 131104 | tf_op jit(solution)/shard_map/ppermute | solution.py:326
  60.7 0.1 collective-permute-start.9
  60.8 2.9 %weight.5.two = bf16[4,4,9,16,256]{4,3,2,1,0:T(8,128)(2,1)S(1)} custom-call(bf16[256,256]{1,0:T(8,128)(2,1)S(1)} %collective-permute-done.7.refs_0_, bf16[256,256]{1,0:T(8,128)(2,1)S(1)} %get-tuple-element.110.refs_1_, bf16[2,256,256]{2,1,0:T(8,128)(2,1)S(1)} %get-tuple-element.111.refs_2_, bf16[256,256]{1,0:T(8,128)(2,1)S(1)} %get-tuple-element.112.refs_3_, ...), custom_call_target="tpu_custom_call" | custom-call | flops 1 | bytes 1 | tf_op jit(solution)/shard_map/weight/pallas_call | solution.py:218
  63.7 0.0 collective-permute-done.9.other
  63.7 0.6 pair_kernel.1
  64.3 5.9 %collective-permute-start.19 = (bf16[9,256,256]{2,1,0:T(8,128)(2,1)S(1)}, bf16[9,256,256]{2,1,0:T(8,128)(2,1)S(1)}, u32[]{:S(2)}, u32[]{:S(2)}) collective-permute-start(bf16[9,256,256]{2,1,0:T(8,128)(2,1)S(1)} %get-tuple-element.115), channel_id=1, source_target_pairs={{3,240},{2,241},{1,242},{0,243},{7,244},{6,245},{5,246},{4,247},{1... | collective-permute-start | bytes 3538952 | tf_op jit(solution)/shard_map/ppermute | solution.py:317
  70.3 0.8 collective-permute-start.13
  71.1 1.1 collective-permute-start.14
  72.2 1.0 collective-permute-start.15
  73.2 1.1 collective-permute-start.10
  74.2 6.0 %collective-permute-done.13.one = bf16[4,9,16,256]{3,2,1,0:T(8,128)(2,1)S(1)} collective-permute-done((bf16[4,9,16,256]{3,2,1,0:T(8,128)(2,1)S(1)}, bf16[4,9,16,256]{3,2,1,0:T(8,128)(2,1)S(1)}, u32[]{:S(2)}, u32[]{:S(2)}) %collective-permute-start.13) | collective-permute-done | bytes 294944 | tf_op jit(solution)/shard_map/ppermute | solution.py:306
  80.2 1.7 %collective-permute-start.11 = (bf16[4,9,16,256]{3,2,1,0:T(8,128)(2,1)S(1)}, bf16[4,9,16,256]{3,2,1,0:T(8,128)(2,1)S(1)}, u32[]{:S(2)}, u32[]{:S(2)}) collective-permute-start(bf16[4,9,16,256]{3,2,1,0:T(8,128)(2,1)S(1)} %get-tuple-element.93), channel_id=1, source_target_pairs={{0,8},{1,9},{2,10},{3,11},{4,12},{5,13},{6,14},{7,15},{8,0},{9,1},... | collective-permute-start | bytes 884744 | tf_op jit(solution)/shard_map/ppermute | solution.py:306
  81.9 0.7 collective-permute-done.14.two
  82.7 4.9 %collective-permute-start.12 = (bf16[4,9,16,256]{3,2,1,0:T(8,128)(2,1)S(1)}, bf16[4,9,16,256]{3,2,1,0:T(8,128)(2,1)S(1)}, u32[]{:S(2)}, u32[]{:S(2)}) collective-permute-start(bf16[4,9,16,256]{3,2,1,0:T(8,128)(2,1)S(1)} %get-tuple-element.94), channel_id=1, source_target_pairs={{0,12},{1,13},{2,14},{3,15},{4,0},{5,1},{6,2},{7,3},{8,4},{9,5},{1... | collective-permute-start | bytes 884744 | tf_op jit(solution)/shard_map/ppermute | solution.py:306
  87.5 0.8 collective-permute-done.15.three
  88.3 0.1 regroup_kernel.2
  88.5 0.0 copy-start
  88.5 0.1 collective-permute-start.16
  88.6 5.9 %collective-permute-done.16.came = bf16[2,9,16,256]{3,2,1,0:T(8,128)(2,1)S(1)} collective-permute-done((bf16[2,9,16,256]{3,2,1,0:T(8,128)(2,1)S(1)}, bf16[2,9,16,256]{3,2,1,0:T(8,128)(2,1)S(1)}, u32[]{:S(2)}, u32[]{:S(2)}) %collective-permute-start.16) | collective-permute-done | bytes 147488 | tf_op jit(solution)/shard_map/ppermute | solution.py:306
  94.5 0.1 collective-permute-start.17
  94.6 0.0 collective-permute-done.10.one
  94.6 0.0 collective-permute-done.11.two
  94.6 0.8 collective-permute-done.12.three
  95.5 4.4 %collective-permute-done.17.came = bf16[9,16,256]{2,1,0:T(8,128)(2,1)S(1)} collective-permute-done((bf16[9,16,256]{2,1,0:T(8,128)(2,1)S(1)}, bf16[9,16,256]{2,1,0:T(8,128)(2,1)S(1)}, u32[]{:S(2)}, u32[]{:S(2)}) %collective-permute-start.17) | collective-permute-done | bytes 73760 | tf_op jit(solution)/shard_map/ppermute | solution.py:306
  99.8 0.1 regroup_kernel.3
  100.0 0.1 collective-permute-start.18
  100.1 0.0 copy-done
  100.1 1.1 collective-permute-start.20
  101.2 4.9 %collective-permute-done.18.came = bf16[2,9,16,256]{3,2,1,0:T(8,128)(2,1)S(1)} collective-permute-done((bf16[2,9,16,256]{3,2,1,0:T(8,128)(2,1)S(1)}, bf16[2,9,16,256]{3,2,1,0:T(8,128)(2,1)S(1)}, u32[]{:S(2)}, u32[]{:S(2)}) %collective-permute-start.18) | collective-permute-done | bytes 147488 | tf_op jit(solution)/shard_map/ppermute | solution.py:306
  106.2 1.7 %collective-permute-start.21 = (bf16[9,16,256]{2,1,0:T(8,128)(2,1)S(1)}, bf16[9,16,256]{2,1,0:T(8,128)(2,1)S(1)}, u32[]{:S(2)}, u32[]{:S(2)}) collective-permute-start(bf16[9,16,256]{2,1,0:T(8,128)(2,1)S(1)} %get-tuple-element.119), channel_id=1, source_target_pairs={{0,2},{1,3},{2,0},{3,1},{4,6},{5,7},{6,4},{7,5},{8,10},{9,11},{10,... | collective-permute-start | bytes 221192 | tf_op jit(solution)/shard_map/ppermute | solution.py:306
  107.9 0.0 collective-permute-done.19.refs_5_
  107.9 3.2 %back.5 = bf16[3,1,4,256,256]{4,3,2,1,0:T(8,128)(2,1)} custom-call(bf16[256,256]{1,0:T(8,128)(2,1)S(1)} %collective-permute-done.7.refs_0_, bf16[256,256]{1,0:T(8,128)(2,1)S(1)} %get-tuple-element.110.refs_1_, bf16[2,256,256]{2,1,0:T(8,128)(2,1)S(1)} %get-tuple-element.111.refs_2_, ...), custom_call_target="tpu_custom_call", output_to_operand_aliasing={{}: (7, {})} | custom-call | flops 1 | bytes 1 | tf_op jit(solution)/shard_map/back/pallas_call | solution.py:159
  111.1 0.0 collective-permute-done.20.held
  111.1 1.2 %collective-permute-done.21.came = bf16[9,16,256]{2,1,0:T(8,128)(2,1)S(1)} collective-permute-done((bf16[9,16,256]{2,1,0:T(8,128)(2,1)S(1)}, bf16[9,16,256]{2,1,0:T(8,128)(2,1)S(1)}, u32[]{:S(2)}, u32[]{:S(2)}) %collective-permute-start.21) | collective-permute-done | bytes 73760 | tf_op jit(solution)/shard_map/ppermute | solution.py:306
  112.3 0.7 finish_kernel.3
  (3 shorter events, 0.1 us)
Async XLA Ops:
  0.6 24.7 %copy-start.1 = (bf16[1,256,9,256]{3,1,2,0:T(8,128)(2,1)S(1)}, bf16[1,256,9,256]{3,1,2,0:T(8,128)(2,1)}, u32[]{:S(2)}) copy-start(bf16[1,256,9,256]{3,1,2,0:T(8,128)(2,1)} %param.5) | copy-start | bytes 3538948
  2.0 23.4 %collective-permute-start.4 = (bf16[9,128,256]{2,1,0:T(8,128)(2,1)S(1)}, bf16[9,128,256]{2,1,0:T(8,128)(2,1)S(1)}, u32[]{:S(2)}, u32[]{:S(2)}) collective-permute-start(bf16[9,128,256]{2,1,0:T(8,128)(2,1)S(1)} %get-tuple-element.73), channel_id=1, source_target_pairs={{3,240},{2,241},{1,242},{0,243},{7,244},{6,245},{5,246},{4,247},{1... | collective-permute-start | bytes 1769480 | tf_op jit(solution)/shard_map/ppermute | solution.py:317
  11.7 13.3 %collective-permute-start = (bf16[256,256]{1,0:T(8,128)(2,1)S(1)}, bf16[256,256]{1,0:T(8,128)(2,1)S(1)}, u32[]{:S(2)}, u32[]{:S(2)}) collective-permute-start(bf16[256,256]{1,0:T(8,128)(2,1)S(1)} %get-tuple-element.61), channel_id=1, source_target_pairs={{0,1},{1,2},{2,3},{3,4},{4,5},{5,6},{6,7},{7,8},{8,9},{9,10},{10,1... | collective-permute-start | bytes 393224 | tf_op jit(solution)/shard_map/ppermute | solution.py:325
  15.5 9.4 %collective-permute-start.1 = (bf16[256,256]{1,0:T(8,128)(2,1)S(1)}, bf16[256,256]{1,0:T(8,128)(2,1)S(1)}, u32[]{:S(2)}, u32[]{:S(2)}) collective-permute-start(bf16[256,256]{1,0:T(8,128)(2,1)S(1)} %get-tuple-element.62), channel_id=1, source_target_pairs={{1,0},{2,1},{3,2},{4,3},{5,4},{6,5},{7,6},{8,7},{9,8},{10,9},{11,1... | collective-permute-start | bytes 393224 | tf_op jit(solution)/shard_map/ppermute | solution.py:326
  25.3 17.6 %collective-permute-start.5 = (bf16[9,256,256]{2,1,0:T(8,128)(2,1)S(1)}, bf16[9,256,256]{2,1,0:T(8,128)(2,1)S(1)}, u32[]{:S(2)}, u32[]{:S(2)}) collective-permute-start(bf16[9,256,256]{2,1,0:T(8,128)(2,1)S(1)} %bitcast.12), channel_id=1, source_target_pairs={{16,0},{48,32},{80,64},{112,96},{144,128},{176,160},{208,192},{240... | collective-permute-start | bytes 3538952 | tf_op jit(solution)/shard_map/ppermute | solution.py:321
  26.6 16.3 %collective-permute-start.6 = (bf16[9,128,256]{2,1,0:T(8,128)(2,1)S(1)}, bf16[9,128,256]{2,1,0:T(8,128)(2,1)S(1)}, u32[]{:S(2)}, u32[]{:S(2)}) collective-permute-start(bf16[9,128,256]{2,1,0:T(8,128)(2,1)S(1)} %collective-permute-done.4.refs_6_), channel_id=1, source_target_pairs={{16,20},{17,21},{18,22},{19,23},{20,16},{21,17},{22,18},{23,19},{2... | collective-permute-start | bytes 1769480 | tf_op jit(solution)/shard_map/ppermute | solution.py:311
  31.4 11.5 %collective-permute-start.2 = (bf16[256,256]{1,0:T(8,128)(2,1)S(1)}, bf16[256,256]{1,0:T(8,128)(2,1)S(1)}, u32[]{:S(2)}, u32[]{:S(2)}) collective-permute-start(bf16[256,256]{1,0:T(8,128)(2,1)S(1)} %get-tuple-element.83.refs_3_), channel_id=1, source_target_pairs={{0,1},{1,2},{2,3},{3,4},{4,5},{5,6},{6,7},{7,8},{8,9},{9,10},{10,1... | collective-permute-start | bytes 393224 | tf_op jit(solution)/shard_map/ppermute | solution.py:325
  33.3 9.6 %collective-permute-start.3 = (bf16[256,256]{1,0:T(8,128)(2,1)S(1)}, bf16[256,256]{1,0:T(8,128)(2,1)S(1)}, u32[]{:S(2)}, u32[]{:S(2)}) collective-permute-start(bf16[256,256]{1,0:T(8,128)(2,1)S(1)} %get-tuple-element.81.refs_1_), channel_id=1, source_target_pairs={{1,0},{2,1},{3,2},{4,3},{5,4},{6,5},{7,6},{8,7},{9,8},{10,9},{11,1... | collective-permute-start | bytes 393224 | tf_op jit(solution)/shard_map/ppermute | solution.py:326
  46.9 11.4 %collective-permute-start.7 = (bf16[256,256]{1,0:T(8,128)(2,1)S(1)}, bf16[256,256]{1,0:T(8,128)(2,1)S(1)}, u32[]{:S(2)}, u32[]{:S(2)}) collective-permute-start(bf16[256,256]{1,0:T(8,128)(2,1)S(1)} %get-tuple-element.112.refs_3_), channel_id=1, source_target_pairs={{0,1},{1,2},{2,3},{3,4},{4,5},{5,6},{6,7},{7,8},{8,9},{9,10},{10,1... | collective-permute-start | bytes 393224 | tf_op jit(solution)/shard_map/ppermute | solution.py:325
  50.7 10.1 %collective-permute-start.8 = (bf16[256,256]{1,0:T(8,128)(2,1)S(1)}, bf16[256,256]{1,0:T(8,128)(2,1)S(1)}, u32[]{:S(2)}, u32[]{:S(2)}) collective-permute-start(bf16[256,256]{1,0:T(8,128)(2,1)S(1)} %get-tuple-element.110.refs_1_), channel_id=1, source_target_pairs={{1,0},{2,1},{3,2},{4,3},{5,4},{6,5},{7,6},{8,7},{9,8},{10,9},{11,1... | collective-permute-start | bytes 393224 | tf_op jit(solution)/shard_map/ppermute | solution.py:326
  60.7 2.9 %collective-permute-start.9 = (bf16[4,4,9,16,256]{4,3,2,1,0:T(8,128)(2,1)S(1)}, bf16[4,4,9,16,256]{4,3,2,1,0:T(8,128)(2,1)S(1)}, u32[]{:S(2)}, u32[]{:S(2)}) collective-permute-start(bf16[4,4,9,16,256]{4,3,2,1,0:T(8,128)(2,1)S(1)} %weight.4), channel_id=1, source_target_pairs={{0,16},{16,0},{32,48},{48,32},{64,80},{80,64},{96,112},{112,96},{1... | collective-permute-start | bytes 3538952 | tf_op jit(solution)/shard_map/ppermute | solution.py:321
  64.3 43.6 %collective-permute-start.19 = (bf16[9,256,256]{2,1,0:T(8,128)(2,1)S(1)}, bf16[9,256,256]{2,1,0:T(8,128)(2,1)S(1)}, u32[]{:S(2)}, u32[]{:S(2)}) collective-permute-start(bf16[9,256,256]{2,1,0:T(8,128)(2,1)S(1)} %get-tuple-element.115), channel_id=1, source_target_pairs={{3,240},{2,241},{1,242},{0,243},{7,244},{6,245},{5,246},{4,247},{1... | collective-permute-start | bytes 3538952 | tf_op jit(solution)/shard_map/ppermute | solution.py:317
  70.3 9.9 %collective-permute-start.13 = (bf16[4,9,16,256]{3,2,1,0:T(8,128)(2,1)S(1)}, bf16[4,9,16,256]{3,2,1,0:T(8,128)(2,1)S(1)}, u32[]{:S(2)}, u32[]{:S(2)}) collective-permute-start(bf16[4,9,16,256]{3,2,1,0:T(8,128)(2,1)S(1)} %get-tuple-element.96), channel_id=1, source_target_pairs={{0,4},{1,5},{2,6},{3,7},{4,8},{5,9},{6,10},{7,11},{8,12},{9,13},{1... | collective-permute-start | bytes 884744 | tf_op jit(solution)/shard_map/ppermute | solution.py:306
  71.1 11.6 %collective-permute-start.14 = (bf16[4,9,16,256]{3,2,1,0:T(8,128)(2,1)S(1)}, bf16[4,9,16,256]{3,2,1,0:T(8,128)(2,1)S(1)}, u32[]{:S(2)}, u32[]{:S(2)}) collective-permute-start(bf16[4,9,16,256]{3,2,1,0:T(8,128)(2,1)S(1)} %get-tuple-element.97), channel_id=1, source_target_pairs={{0,8},{1,9},{2,10},{3,11},{4,12},{5,13},{6,14},{7,15},{8,0},{9,1},... | collective-permute-start | bytes 884744 | tf_op jit(solution)/shard_map/ppermute | solution.py:306
  72.2 16.1 %collective-permute-start.15 = (bf16[4,9,16,256]{3,2,1,0:T(8,128)(2,1)S(1)}, bf16[4,9,16,256]{3,2,1,0:T(8,128)(2,1)S(1)}, u32[]{:S(2)}, u32[]{:S(2)}) collective-permute-start(bf16[4,9,16,256]{3,2,1,0:T(8,128)(2,1)S(1)} %get-tuple-element.98), channel_id=1, source_target_pairs={{0,12},{1,13},{2,14},{3,15},{4,0},{5,1},{6,2},{7,3},{8,4},{9,5},{1... | collective-permute-start | bytes 884744 | tf_op jit(solution)/shard_map/ppermute | solution.py:306
  73.2 21.4 %collective-permute-start.10 = (bf16[4,9,16,256]{3,2,1,0:T(8,128)(2,1)S(1)}, bf16[4,9,16,256]{3,2,1,0:T(8,128)(2,1)S(1)}, u32[]{:S(2)}, u32[]{:S(2)}) collective-permute-start(bf16[4,9,16,256]{3,2,1,0:T(8,128)(2,1)S(1)} %get-tuple-element.92), channel_id=1, source_target_pairs={{0,4},{1,5},{2,6},{3,7},{4,8},{5,9},{6,10},{7,11},{8,12},{9,13},{1... | collective-permute-start | bytes 884744 | tf_op jit(solution)/shard_map/ppermute | solution.py:306
  80.2 14.4 %collective-permute-start.11 = (bf16[4,9,16,256]{3,2,1,0:T(8,128)(2,1)S(1)}, bf16[4,9,16,256]{3,2,1,0:T(8,128)(2,1)S(1)}, u32[]{:S(2)}, u32[]{:S(2)}) collective-permute-start(bf16[4,9,16,256]{3,2,1,0:T(8,128)(2,1)S(1)} %get-tuple-element.93), channel_id=1, source_target_pairs={{0,8},{1,9},{2,10},{3,11},{4,12},{5,13},{6,14},{7,15},{8,0},{9,1},... | collective-permute-start | bytes 884744 | tf_op jit(solution)/shard_map/ppermute | solution.py:306
  82.7 12.8 %collective-permute-start.12 = (bf16[4,9,16,256]{3,2,1,0:T(8,128)(2,1)S(1)}, bf16[4,9,16,256]{3,2,1,0:T(8,128)(2,1)S(1)}, u32[]{:S(2)}, u32[]{:S(2)}) collective-permute-start(bf16[4,9,16,256]{3,2,1,0:T(8,128)(2,1)S(1)} %get-tuple-element.94), channel_id=1, source_target_pairs={{0,12},{1,13},{2,14},{3,15},{4,0},{5,1},{6,2},{7,3},{8,4},{9,5},{1... | collective-permute-start | bytes 884744 | tf_op jit(solution)/shard_map/ppermute | solution.py:306
  88.5 11.6 %copy-start = (bf16[1,16,9,256]{3,1,2,0:T(8,128)(2,1)S(1)}, bf16[1,16,9,256]{3,1,2,0:T(8,128)(2,1)}, u32[]{:S(2)}) copy-start(bf16[1,16,9,256]{3,1,2,0:T(8,128)(2,1)} %param.6) | copy-start | bytes 221188
  88.5 6.0 %collective-permute-start.16 = (bf16[2,9,16,256]{3,2,1,0:T(8,128)(2,1)S(1)}, bf16[2,9,16,256]{3,2,1,0:T(8,128)(2,1)S(1)}, u32[]{:S(2)}, u32[]{:S(2)}) collective-permute-start(bf16[2,9,16,256]{3,2,1,0:T(8,128)(2,1)S(1)} %get-tuple-element.100), channel_id=1, source_target_pairs={{0,1},{1,0},{2,3},{3,2},{4,5},{5,4},{6,7},{7,6},{8,9},{9,8},{10,11... | collective-permute-start | bytes 442376 | tf_op jit(solution)/shard_map/ppermute | solution.py:306
  94.5 5.3 %collective-permute-start.17 = (bf16[9,16,256]{2,1,0:T(8,128)(2,1)S(1)}, bf16[9,16,256]{2,1,0:T(8,128)(2,1)S(1)}, u32[]{:S(2)}, u32[]{:S(2)}) collective-permute-start(bf16[9,16,256]{2,1,0:T(8,128)(2,1)S(1)} %get-tuple-element.101), channel_id=1, source_target_pairs={{0,2},{1,3},{2,0},{3,1},{4,6},{5,7},{6,4},{7,5},{8,10},{9,11},{10,... | collective-permute-start | bytes 221192 | tf_op jit(solution)/shard_map/ppermute | solution.py:306
  100.0 6.2 %collective-permute-start.18 = (bf16[2,9,16,256]{3,2,1,0:T(8,128)(2,1)S(1)}, bf16[2,9,16,256]{3,2,1,0:T(8,128)(2,1)S(1)}, u32[]{:S(2)}, u32[]{:S(2)}) collective-permute-start(bf16[2,9,16,256]{3,2,1,0:T(8,128)(2,1)S(1)} %get-tuple-element.107), channel_id=1, source_target_pairs={{0,1},{1,0},{2,3},{3,2},{4,5},{5,4},{6,7},{7,6},{8,9},{9,8},{10,11... | collective-permute-start | bytes 442376 | tf_op jit(solution)/shard_map/ppermute | solution.py:306
  100.1 11.0 %collective-permute-start.20 = (bf16[9,16,256]{2,1,0:T(8,128)(2,1)S(1)}, bf16[9,16,256]{2,1,0:T(8,128)(2,1)S(1)}, u32[]{:S(2)}, u32[]{:S(2)}) collective-permute-start(bf16[9,16,256]{2,1,0:T(8,128)(2,1)S(1)} %finish_kernel.2), channel_id=1, source_target_pairs={{0,224},{16,240},{32,0},{48,16},{64,32},{80,48},{96,64},{112,80},{... | collective-permute-start | bytes 221192 | tf_op jit(solution)/shard_map/ppermute | solution.py:321
  106.2 6.1 %collective-permute-start.21 = (bf16[9,16,256]{2,1,0:T(8,128)(2,1)S(1)}, bf16[9,16,256]{2,1,0:T(8,128)(2,1)S(1)}, u32[]{:S(2)}, u32[]{:S(2)}) collective-permute-start(bf16[9,16,256]{2,1,0:T(8,128)(2,1)S(1)} %get-tuple-element.119), channel_id=1, source_target_pairs={{0,2},{1,3},{2,0},{3,1},{4,6},{5,7},{6,4},{7,5},{8,10},{9,11},{10,... | collective-permute-start | bytes 221192 | tf_op jit(solution)/shard_map/ppermute | solution.py:306
